TPU v7x, 32 devices: a whole 2x2x4 slice. The times are simulated.
32 devices in a mesh: ang: 4 (over x, core), tile: 8 (over z, y).
Axes of the slice: x: 2, y: 2, z: 4, core: 2. Of those that a mesh axis runs over, the one named last changes fastest.
Arguments:
- volume: float32 [256, 128, 256], P('ang', 'tile'), may hold values from -6 to 6
- phase: float32 [4, 128, 256], P('ang', 'tile'), may hold values from -6 to 6
- dual: float32 [4, 128, 256], P('ang', 'tile'), may hold values from -3 to 3
- probe_real: float32 [128, 128], replicated, may hold values from -4 to 4
- probe_imag: float32 [128, 128], replicated, may hold values from -4 to 4
- intensity: float32 [4, 32, 128, 128], P('ang', 'tile'), may hold values from 0.05 to 4
- offsets: int32 [4, 32], P('ang', 'tile'), may hold values from 0 to 128
- angle_index: int32 [4], P('ang'), may hold values from 0 to 180
Outputs:
- phase_new: float32 [4, 128, 256], P('ang', 'tile')
- volume_new: float32 [256, 128, 256], P('ang', 'tile')
- dual_new: float32 [4, 128, 256], P('ang', 'tile')
Inputs may be any that keep to these rules, and one draw needn't show every extreme that they name: `offsets`: the probe's 128 columns starting at the offset lie inside the 256 columns of a projection.
All inputs are finite; a program needn't handle non-finite values.
Results may differ from a plain program's by a relative error of at most 0.015.
Values may be sent and summed in bfloat16 or wider, within the bound.
No kernel may reach another device: no remote copies, remote signals or barrier semaphores. Data moves between devices by JAX's collectives and lax.ppermute only.
A program may use at most 64 MiB of HBM per device.

v0:
```python
import functools
import math

import jax
import jax.numpy as jnp
import numpy as np
from jax import lax
from jax.experimental import pallas as pl
from jax.experimental.pallas import tpu as pltpu
from jax.sharding import PartitionSpec as P

angle_center = 90.0
rho_weight = 1.0
eta_step = 0.01
tau_step = 1.0
smooth_weight = 0.25

F32 = jnp.float32
BF16 = jnp.bfloat16
VMEM_SPEC = pl.BlockSpec(memory_space=pltpu.VMEM)
SMEM_SPEC = pl.BlockSpec(memory_space=pltpu.SMEM)
VMEM_LIMIT = 56 * 1024 * 1024


def table_pair(length):
    index = np.arange(length)
    phases = (index[:, None] * index[None, :] % length) * (2.0 * np.pi / length)
    return np.cos(phases).astype(np.float32), np.sin(phases).astype(np.float32)


def packed_tables(length):
    half = length // 2
    cos_t, sin_t = table_pair(length)
    bf = np.asarray(jnp.bfloat16).dtype if False else jnp.bfloat16
    out = []
    for kind in (np.float32, bf):
        c = cos_t.astype(kind).astype(np.float32)
        s = sin_t.astype(kind).astype(np.float32)
        forward = np.concatenate([c[:, : half + 1], -s[:, 1:half]], axis=1)
        weight = np.full((length, 1), 2.0 / length, np.float32)
        weight[0] = weight[half] = 1.0 / length
        inverse = forward.T * weight
        out.append((forward.astype(kind), inverse.astype(kind)))
    return out


def split_const(array):
    high = array.astype(jnp.bfloat16)
    low = (array - high.astype(np.float32)).astype(jnp.bfloat16)
    return np.stack([high, low])


def patch_tables(width):
    cos_t, sin_t = table_pair(width)
    c = cos_t / np.float32(math.sqrt(width))
    s = sin_t / np.float32(math.sqrt(width))
    right = np.block([[c, -s], [s, c]])
    left = np.block([[c, s], [-s, c]])
    right_conj = np.block([[c, s], [-s, c]])
    left_conj = np.block([[c, -s], [s, c]])
    return tuple(split_const(m.astype(np.float32)) for m in (right, left, left_conj, right_conj))


def dot(left, right):
    return jnp.dot(left, right, preferred_element_type=F32)


def dot_high(left, right):
    return jnp.dot(left, right, precision=lax.Precision.HIGHEST, preferred_element_type=F32)


def dot_split(left, right):
    def parts(value):
        if value.dtype == BF16:
            return value[0], value[1]
        high = value.astype(BF16)
        return high, (value - high.astype(F32)).astype(BF16)

    left_high, left_low = parts(left)
    right_high, right_low = parts(right)
    return dot(left_high, right_high) + dot(left_low, right_high) + dot(left_high, right_low)


def turn(re, im, c1, s, c2, sign):
    if sign > 0:
        return re * c1 + im * s, im * c2 - re * s
    return re * c1 - im * s, im * c2 + re * s


def fill_turn_tables(angle, slot, length, row_ref, col_ref, nyq_ref):
    half = length // 2
    unit = 2.0 * math.pi / length
    theta = (jnp.full((8, half), angle, jnp.int32).astype(F32) - angle_center) * (math.pi / 360.0)
    coef_a = -(jnp.sin(0.5 * theta) / jnp.cos(0.5 * theta))
    coef_b = jnp.sin(theta)

    lane = lax.broadcasted_iota(jnp.int32, (8, half), 1)
    sub = lax.broadcasted_iota(jnp.int32, (8, half), 0)
    freq = jnp.where(lane == 0, half, lane).astype(F32)
    phase = unit * coef_a * freq
    base = phase * sub.astype(F32)
    base_c, base_s = jnp.cos(base), jnp.sin(base)
    for block in range(length // 64):
        first = 8 * block * 8 - half
        step = phase * (first + 8 * sub).astype(F32)
        step_c, step_s = jnp.cos(step), jnp.sin(step)
        for q in range(8):
            sc, ss = step_c[q : q + 1], step_s[q : q + 1]
            c2 = base_c * sc - base_s * ss
            s = base_s * sc + base_c * ss
            rows = pl.ds((block * 8 + q) * 8, 8)
            row_ref[slot, 0, rows, :] = jnp.where(lane == 0, 1.0, c2)
            row_ref[slot, 1, rows, :] = jnp.where(lane == 0, 0.0, s)
            row_ref[slot, 2, rows, :] = c2

    for side in range(2):
        place = (lane + (side * half - half)).astype(F32)
        phase = unit * coef_b * place
        lanes = slice(side * half, side * half + half)
        base = phase * sub.astype(F32)
        base_c, base_s = jnp.cos(base), jnp.sin(base)
        for block in range(half // 64):
            step = phase * (block * 64 + 8 * sub).astype(F32)
            step_c, step_s = jnp.cos(step), jnp.sin(step)
            for q in range(8):
                sc, ss = step_c[q : q + 1], step_s[q : q + 1]
                rows = pl.ds((block * 8 + q) * 8, 8)
                col_ref[slot, 0, rows, lanes] = base_c * sc - base_s * ss
                col_ref[slot, 1, rows, lanes] = base_s * sc + base_c * ss
        top = jnp.where(sub == 0, jnp.cos(phase * float(half)), base_c)
        nyq_ref[slot, :, lanes] = top


def fill_pair_rows(slot, share, row_ref, pair_ref):
    here = lax.axis_index("ang")
    other = here + 1 - 2 * lax.rem(here, 2)
    for part in range(3):
        for place, which in enumerate((here, other)):
            rows = pl.ds(pl.multiple_of(which * share, 8), share)
            pair_ref[slot, part, place * share : (place + 1) * share, :] = row_ref[slot, part, rows, :]


def turn_cols(spectrum, slot, col_ref, nyq_ref, sign):
    half = spectrum.shape[0] // 2
    c1 = col_ref[slot, 0]
    c2 = jnp.concatenate([nyq_ref[slot], col_ref[slot, 0, 8:half, :]], axis=0)
    re, im = turn(spectrum[:half], spectrum[half:], c1, col_ref[slot, 1], c2, sign)
    return jnp.concatenate([re, im], axis=0).astype(BF16)


def turn_rows(spectrum, table_ref, slot, sign):
    half = spectrum.shape[1] // 2
    return turn(
        spectrum[:, :half],
        spectrum[:, half:],
        table_ref[slot, 0],
        table_ref[slot, 1],
        table_ref[slot, 2],
        sign,
    )


def project_slice(slab, z, groups, refs, lines_ref):
    forward_ref, inverse_ref, down_ref, up_ref, row_ref, pair_ref, col_ref, nyq_ref = refs
    here = lax.axis_index("ang")
    spectrum = dot(slab, forward_ref[...])
    for g in range(groups):
        turned = jnp.concatenate(turn_rows(spectrum, pair_ref, g, 1), axis=1).astype(BF16)
        first = dot(turned, inverse_ref[...]).astype(BF16)
        columns = turn_cols(dot(down_ref[here], first), g, col_ref, nyq_ref, 1)
        second = dot(up_ref[...], columns).astype(BF16)
        re, im = turn_rows(dot(second, forward_ref[...]), row_ref, g, 1)
        line = jnp.concatenate(
            [jnp.sum(re, axis=0, keepdims=True), jnp.sum(im, axis=0, keepdims=True)], axis=1
        )
        lines_ref[g, pl.ds(z, 1), :] = line


def slice_rows(side_refs, z, share, slices):
    return jnp.concatenate([ref[pl.ds(z, share, stride=slices), :] for ref in side_refs], axis=1)


def prepare_kernel(left_ref, right_ref, out_ref):
    slices, share, _ = out_ref.shape
    for z in range(slices):
        out_ref[z] = slice_rows((left_ref, right_ref), z, share, slices).astype(BF16)


def base_kernel(left_ref, right_ref, before_ref, after_ref, base_ref, sent_ref):
    slices, share, _ = base_ref.shape

    def rows(z):
        return slice_rows((left_ref, right_ref), z, share, slices)

    for z in range(slices):
        now = rows(z)
        low = before_ref[...].astype(F32) if z == 0 else rows(z - 1)
        high = after_ref[...].astype(F32) if z == slices - 1 else rows(z + 1)
        base = now - tau_step * smooth_weight * (2.0 * now - low - high)
        base_ref[z] = base
        sent_ref[z] = base.astype(BF16)


def setup_tables(angles_ref, share, length, row_ref, pair_ref, col_ref, nyq_ref):
    for g in range(row_ref.shape[0]):
        fill_turn_tables(angles_ref[g], g, length, row_ref, col_ref, nyq_ref)
        fill_pair_rows(g, share, row_ref, pair_ref)


def project_kernel(
    unroll, angles_ref, own_ref, other_ref, forward_ref, inverse_ref, down_ref, up_ref,
    lines_ref, row_ref, pair_ref, col_ref, nyq_ref,
):
    groups, slices, length = lines_ref.shape
    share = own_ref.shape[1]
    setup_tables(angles_ref, share, length, row_ref, pair_ref, col_ref, nyq_ref)
    refs = (forward_ref, inverse_ref, down_ref, up_ref, row_ref, pair_ref, col_ref, nyq_ref)

    def body(step, carry):
        for u in range(unroll):
            z = step * unroll + u
            slab = jnp.concatenate([own_ref[z], other_ref[z]], axis=0)
            project_slice(slab, z, groups, refs, lines_ref)
        return carry

    lax.fori_loop(0, slices // unroll, body, 0)


def back_kernel(
    unroll, angles_ref, spectra_ref, forward_ref, inverse_ref, down_ref, up_ref,
    out_ref, row_ref, pair_ref, col_ref, nyq_ref,
):
    groups, slices, length = spectra_ref.shape
    half = length // 2
    share = out_ref.shape[1] // 2
    setup_tables(angles_ref, share, length, row_ref, pair_ref, col_ref, nyq_ref)
    here = lax.axis_index("ang")

    def body(step, carry):
        for u in range(unroll):
            z = step * unroll + u
            total_re = total_im = None
            for g in range(groups):
                line = spectra_ref[g, pl.ds(z, 1), :]
                re, im = turn(
                    line[:, :half], line[:, half:],
                    row_ref[g, 0], row_ref[g, 1], row_ref[g, 2], -1,
                )
                turned = jnp.concatenate([re, im], axis=1).astype(BF16)
                spread = dot(turned, inverse_ref[...]).astype(BF16)
                columns = turn_cols(dot(down_ref[...], spread), g, col_ref, nyq_ref, -1)
                second = dot(up_ref[here], columns).astype(BF16)
                re, im = turn_rows(dot(second, forward_ref[...]), pair_ref, g, -1)
                total_re = re if total_re is None else total_re + re
                total_im = im if total_im is None else total_im + im
            total = jnp.concatenate([total_re, total_im], axis=1).astype(BF16)
            out_ref[z] = dot(total, inverse_ref[...]).astype(BF16)
        return carry

    lax.fori_loop(0, slices // unroll, body, 0)


def update_kernel(
    unroll, angles_ref, base_ref, base_other_ref, mine_ref, theirs_ref,
    forward_ref, inverse_ref, down_ref, up_ref,
    volume_ref, lines_ref, row_ref, pair_ref, col_ref, nyq_ref, side_refs,
):
    groups, slices, length = lines_ref.shape
    share = base_ref.shape[1]
    setup_tables(angles_ref, share, length, row_ref, pair_ref, col_ref, nyq_ref)
    refs = (forward_ref, inverse_ref, down_ref, up_ref, row_ref, pair_ref, col_ref, nyq_ref)

    def body(step, carry):
        for u in range(unroll):
            z = step * unroll + u
            own = base_ref[z] - tau_step * (
                mine_ref[z, :share, :].astype(F32) + theirs_ref[z, share:, :].astype(F32)
            )
            for side in range(2):
                lanes = slice(side * length // 2, (side + 1) * length // 2)
                side_refs[side][pl.ds(z, share, stride=slices), :] = own[:, lanes]
            other = base_other_ref[z].astype(F32) - tau_step * (
                mine_ref[z, share:, :].astype(F32) + theirs_ref[z, :share, :].astype(F32)
            )
            slab = jnp.concatenate([own.astype(BF16), other.astype(BF16)], axis=0)
            project_slice(slab, z, groups, refs, lines_ref)
        return carry

    lax.fori_loop(0, slices // unroll, body, 0)
    volume_ref[...] = jnp.concatenate([ref[...] for ref in side_refs], axis=1)


def gradient_kernel(
    offsets_ref, image_ref, measured_ref, probe_r_ref, probe_i_ref,
    right_ref, left_ref, left_conj_ref, right_conj_ref, out_ref,
):
    positions, height, width = measured_ref.shape
    length = image_ref.shape[1]
    image = image_ref[...]
    cos_image, sin_image = jnp.cos(image), jnp.sin(image)
    probe_r, probe_i = probe_r_ref[...], probe_i_ref[...]
    waves = []
    for p in range(positions):
        back = length - offsets_ref[0, p]
        cos_p = pltpu.roll(cos_image, back, 1)[:, :width]
        sin_p = pltpu.roll(sin_image, back, 1)[:, :width]
        waves.append((probe_r * cos_p - probe_i * sin_p, probe_r * sin_p + probe_i * cos_p))
    total = jnp.zeros((height, length), F32)
    for p0 in range(0, positions, 2):
        some = range(p0, min(p0 + 2, positions))
        half = [
            dot_split(jnp.concatenate(waves[p], axis=1), right_ref[...]) for p in some
        ]
        stacked = jnp.concatenate(
            [jnp.concatenate([h[:, :width], h[:, width:]], axis=0) for h in half], axis=1
        )
        far = dot_split(left_ref[...], stacked)
        far_r, far_i = far[:height], far[height:]
        measured = jnp.concatenate([measured_ref[p] for p in some], axis=1)
        misfit = far_r * far_r + far_i * far_i - measured
        weighted = jnp.concatenate([misfit * far_r, misfit * far_i], axis=0)
        returned = dot_split(left_conj_ref[...], weighted)
        for i, p in enumerate(some):
            lanes = slice(i * width, (i + 1) * width)
            rows = jnp.concatenate([returned[:height, lanes], returned[height:, lanes]], axis=1)
            chi = dot_split(rows, right_conj_ref[...])
            wave_r, wave_i = waves[p]
            term = 2.0 * (chi[:, width:] * wave_r - chi[:, :width] * wave_i)
            padded = jnp.concatenate([term, jnp.zeros((height, length - width), F32)], axis=1)
            total = total + pltpu.roll(padded, offsets_ref[0, p], 1)
    out_ref[...] = total.astype(out_ref.dtype)


def phase_kernel(
    peers, grad_ref, phase_ref, dual_ref, forward_ref, inverse_ref, *rest
):
    lines = rest[:peers]
    phase_new_ref, spectrum_ref = rest[peers:]
    tiles, slices, length = grad_ref.shape
    grad = grad_ref[0].astype(F32)
    for t in range(1, tiles):
        grad = grad + grad_ref[t].astype(F32)
    line = lines[0][...]
    for other in lines[1:]:
        line = line + other[...]
    scale = 1.0 / math.sqrt(length)
    proj_old = dot_high(line, inverse_ref[...]) * scale
    phase, dual = phase_ref[...], dual_ref[...]
    phase_new = phase - eta_step * (grad + dual + rho_weight * (phase - proj_old))
    resid = rho_weight * (proj_old - phase_new) - dual
    phase_new_ref[...] = phase_new
    spectrum_ref[...] = dot_high(resid, forward_ref[...]) * scale


def dual_kernel(peers, phase_ref, dual_ref, inverse_ref, *rest):
    lines = rest[:peers]
    dual_new_ref = rest[peers]
    line = lines[0][...]
    for other in lines[1:]:
        line = line + other[...]
    proj_new = dot_high(line, inverse_ref[...]) * (1.0 / math.sqrt(line.shape[1]))
    dual_new_ref[...] = dual_ref[...] + rho_weight * (phase_ref[...] - proj_new)


def call(kernel, outs, specs, *args, scratch=(), cost=None, name=None, grid=()):
    return pl.pallas_call(
        kernel,
        grid=grid,
        out_shape=outs,
        in_specs=specs,
        out_specs=jax.tree.map(lambda _: VMEM_SPEC, outs),
        scratch_shapes=list(scratch),
        cost_estimate=cost,
        name=name,
        compiler_params=pltpu.CompilerParams(vmem_limit_bytes=VMEM_LIMIT),
    )(*args)


def shards(volume, phase, dual, probe_real, probe_imag, intensity, offsets, angle_index):
    share, slices, length = volume.shape
    width = probe_real.shape[1]
    half = length // 2
    ang = lax.axis_size("ang")
    tiles = lax.axis_size("tile")
    groups = ang // 2
    pair = 2 * share
    shape = jax.ShapeDtypeStruct

    (forward_full, inverse_full), (forward, inverse) = packed_tables(length)
    down, up = forward.T, inverse.T
    owners = [
        np.r_[i * share : (i + 1) * share, (i ^ 1) * share : ((i ^ 1) + 1) * share] for i in range(ang)
    ]
    down_part = np.stack([down[:, rows] for rows in owners])
    up_part = np.stack([up[rows] for rows in owners])
    right, left, left_conj, right_conj = patch_tables(width)

    scratch = (
        pltpu.VMEM((groups, 3, length, half), F32),
        pltpu.VMEM((groups, 3, pair, half), F32),
        pltpu.VMEM((groups, 2, half, length), F32),
        pltpu.VMEM((groups, 8, length), F32),
    )
    unroll = 2 if groups <= 2 else 1

    def swap(value):
        return lax.ppermute(value, "ang", [(i, i ^ 1) for i in range(ang)])

    def from_peer(value, j):
        return lax.ppermute(value, "ang", [((i + 2 * j) % ang, i) for i in range(ang)])

    def to_peer(value, j):
        return lax.ppermute(value, "ang", [(i, (i + 2 * j) % ang) for i in range(ang)])

    image = lax.all_to_all(
        jnp.broadcast_to(phase, (tiles, slices, length)), "tile", split_axis=0, concat_axis=0, tiled=True
    ).reshape(tiles * slices, length)
    angles = jnp.concatenate([angle_index] + [from_peer(angle_index, j) for j in range(1, groups)])

    flat = volume.reshape(share * slices, length)
    sides = [
        pl.BlockSpec((share * slices, half), functools.partial(lambda side, _: (0, side), side))
        for side in range(2)
    ]
    own = call(
        prepare_kernel,
        shape((slices, share, length), BF16),
        sides,
        flat, flat,
        grid=(1,),
        name="to_slices",
    )
    other = swap(own)

    edge_count = tiles - 1
    before = lax.ppermute(own[-1], "tile", [(i, i + 1) for i in range(edge_count)])
    after = lax.ppermute(own[0], "tile", [(i + 1, i) for i in range(edge_count)])
    base, base_sent = call(
        base_kernel,
        (shape((slices, share, length), F32), shape((slices, share, length), BF16)),
        sides + [VMEM_SPEC] * 2,
        flat, flat, before, after,
        grid=(1,),
        name="smooth",
    )
    base_other = swap(base_sent)

    grad = call(
        gradient_kernel,
        shape((tiles * slices, length), BF16),
        [SMEM_SPEC] + [VMEM_SPEC] * 8,
        offsets, image, intensity[0], probe_real, probe_imag, right, left, left_conj, right_conj,
        name="gradient",
    ).reshape(tiles, slices, length)
    grad = lax.all_to_all(grad, "tile", split_axis=0, concat_axis=0, tiled=True)

    lines = call(
        functools.partial(project_kernel, unroll),
        shape((groups, slices, length), F32),
        [SMEM_SPEC] + [VMEM_SPEC] * 6,
        angles, own, other, forward, inverse, down_part, up,
        scratch=scratch,
        name="project_old",
    )
    old = [lines[0]] + [to_peer(lines[j], j) for j in range(1, groups)]

    phase_new, spectrum = call(
        functools.partial(phase_kernel, groups),
        (shape((slices, length), F32), shape((slices, length), F32)),
        [VMEM_SPEC] * (5 + groups),
        grad, phase[0], dual[0], forward_full, inverse_full, *old,
        name="phase_step",
    )
    spectra = jnp.stack([spectrum] + [from_peer(spectrum, j) for j in range(1, groups)])

    mine = call(
        functools.partial(back_kernel, unroll),
        shape((slices, pair, length), BF16),
        [SMEM_SPEC] + [VMEM_SPEC] * 5,
        angles, spectra, forward, inverse, down, up_part,
        scratch=scratch,
        name="backproject",
    )
    theirs = swap(mine)
    volume_new, lines = call(
        functools.partial(update_kernel, unroll),
        (shape((share * slices, length), F32), shape((groups, slices, length), F32)),
        [SMEM_SPEC] + [VMEM_SPEC] * 8,
        angles, base, base_other, mine, theirs, forward, inverse, down_part, up,
        scratch=scratch + ([pltpu.VMEM((share * slices, half), F32)] * 2,),
        name="project_new",
    )
    new = [lines[0]] + [to_peer(lines[j], j) for j in range(1, groups)]
    dual_new = call(
        functools.partial(dual_kernel, groups),
        shape((slices, length), F32),
        [VMEM_SPEC] * (3 + groups),
        phase_new, dual[0], inverse_full, *new,
        name="dual_step",
    )
    return phase_new[None], volume_new.reshape(share, slices, length), dual_new[None]


def solution(mesh):
    placed = (
        P("ang", "tile", None),
        P("ang", "tile", None),
        P("ang", "tile", None),
        P(),
        P(),
        P("ang", "tile", None, None),
        P("ang", "tile"),
        P("ang"),
    )
    return jax.shard_map(
        shards,
        mesh=mesh,
        in_specs=placed,
        out_specs=(P("ang", "tile", None), P("ang", "tile", None), P("ang", "tile", None)),
        check_vma=False,
    )
```

profile of v0, /device:TPU:0, one launch (start us, length us, event | category | flops | bytes accessed | tf_op | source)
XLA Modules:
  0.0 126.5 jit_solution(18001135816351480826)
XLA Ops:
  0.6 0.0 copy-start.5
  0.6 2.3 %to_slices.1.own_ref = bf16[16,64,256]{2,1,0:T(8,128)(2,1)} custom-call(f32[1024,256]{1,0:T(8,128)} %bitcast.23, f32[1024,256]{1,0:T(8,128)} %bitcast.24), custom_call_target="tpu_custom_call" | custom-call | tf_op jit(solution)/shard_map/to_slices/pallas_call | solution.py:366
  3.0 0.5 collective-permute-start.1
  3.4 0.0 copy-done.5
  3.4 0.7 broadcast_in_dim.14
  4.1 6.8 %all-to-all-start = ((f32[8,16,256]{2,1,0:T(8,128)}), f32[8,16,256]{2,1,0:T(8,128)S(1)}, u32[]{:S(2)}, u32[]{:S(2)}) async-start(f32[8,16,256]{2,1,0:T(8,128)} %broadcast_in_dim.14), calls=%async_computation | async-start | bytes 262144 | tf_op jit(solution)/shard_map/all_to_all | solution.py:415
  10.9 1.5 %collective-permute-start = (s32[1]{0:T(128)}, s32[1]{0:T(128)}, u32[]{:S(2)}, u32[]{:S(2)}) collective-permute-start(s32[1]{0:T(128)} %param.27), channel_id=1, source_target_pairs={{16,0},{24,8},{0,16},{8,24},{17,1},{25,9},{1,17},{9,25},{18,2},{26... | collective-permute-start | bytes 20 | tf_op jit(solution)/shard_map/ppermute | solution.py:410
  13.1 1.5 %collective-permute-done = s32[1]{0:T(128)} collective-permute-done((s32[1]{0:T(128)}, s32[1]{0:T(128)}, u32[]{:S(2)}, u32[]{:S(2)}) %collective-permute-start) | collective-permute-done | bytes 36 | tf_op jit(solution)/shard_map/ppermute | solution.py:410
  14.6 1.3 pad_add_fusion.angles_ref
  15.8 2.8 %all-to-all-done = f32[8,16,256]{2,1,0:T(8,128)S(1)} async-done(((f32[8,16,256]{2,1,0:T(8,128)}), f32[8,16,256]{2,1,0:T(8,128)S(1)}, u32[]{:S(2)}, u32[]{:S(2)}) %all-to-all-start) | async-done | bytes 131104 | tf_op jit(solution)/shard_map/all_to_all | solution.py:415
  18.6 0.7 copy-done.2
  19.2 4.8 %gradient.1 = bf16[128,256]{1,0:T(8,128)(2,1)} custom-call(s32[1,4]{1,0:T(1,128)} %offsets_ref.1, f32[128,256]{1,0:T(8,128)} %bitcast.27, f32[4,128,128]{2,1,0:T(8,128)} %bitcast.29, f32[128,128]{1,0:T(8,128)} %probe_r_ref.1, f32[128,128]{1,0:T(8,128)} %probe_i_ref.1, bf16[2,256,256]{2,1,0:T(8,128)(2,1)} %constant.20.clone.right_ref.left_conj_ref, ...), custom_call_target="tpu_custom_call" | custom-call | tf_op jit(solution)/shard_map/gradient/pallas_call | solution.py:366
  24.0 3.3 %all-to-all-start.1 = ((bf16[8,16,256]{2,1,0:T(8,128)(2,1)}), bf16[8,16,256]{2,1,0:T(8,128)(2,1)S(1)}, u32[]{:S(2)}, u32[]{:S(2)}) async-start(bf16[8,16,256]{2,1,0:T(8,128)(2,1)} %bitcast.28), calls=%async_computation.1 | async-start | bytes 131072 | tf_op jit(solution)/shard_map/all_to_all | solution.py:455
  27.4 0.0 collective-permute-done.1.other_ref
  27.4 0.0 copy-start.3
  27.4 0.8 copy-done.3
  28.2 20.3 %project_old.1 = f32[2,16,256]{2,1,0:T(8,128)} custom-call(s32[2]{0:T(128)} %pad_add_fusion.angles_ref, bf16[16,64,256]{2,1,0:T(8,128)(2,1)} %to_slices.1.own_ref, bf16[16,64,256]{2,1,0:T(8,128)(2,1)} %copy-done.3, bf16[256,256]{1,0:T(8,128)(2,1)} %constant.22.clone.forward_ref, bf16[256,256]{1,0:T(8,128)(2,1)} %constant.23.clone.inverse_ref, ...), custom_call_target="tpu_custom_call" | custom-call | tf_op jit(solution)/shard_map/project_old/pallas_call | solution.py:366
  48.5 1.3 %slice_bitcast_fusion.2 = (f32[16,256]{1,0:T(8,128)S(1)}, f32[16,256]{1,0:T(8,128)}) fusion(f32[2,16,256]{2,1,0:T(8,128)} %project_old.1), kind=kLoop, calls=%fused_computation.3 | loop fusion | bytes 65536 | tf_op jit(solution)/shard_map/squeeze | solution.py:465
  49.8 1.5 %collective-permute-start.2 = (f32[16,256]{1,0:T(8,128)S(1)}, f32[16,256]{1,0:T(8,128)S(1)}, u32[]{:S(2)}, u32[]{:S(2)}) collective-permute-start(f32[16,256]{1,0:T(8,128)S(1)} %get-tuple-element.19), channel_id=1, source_target_pairs={{0,16},{8,24},{16,0},{24,8},{1,17},{9,25},{17,1},{25,9},{2,18},{10... | collective-permute-start | bytes 49160 | tf_op jit(solution)/shard_map/ppermute | solution.py:413
  51.3 0.0 all-to-all-done.1.grad_ref
  51.3 2.2 %collective-permute-done.2.rest_1_ = f32[16,256]{1,0:T(8,128)S(1)} collective-permute-done((f32[16,256]{1,0:T(8,128)S(1)}, f32[16,256]{1,0:T(8,128)S(1)}, u32[]{:S(2)}, u32[]{:S(2)}) %collective-permute-start.2) | collective-permute-done | bytes 16416 | tf_op jit(solution)/shard_map/ppermute | solution.py:413
  53.6 0.0 copy-done.4
  53.6 0.6 copy-done.8
  54.2 2.3 %phase_step.1 = (f32[16,256]{1,0:T(8,128)}, f32[16,256]{1,0:T(8,128)}) custom-call(bf16[8,16,256]{2,1,0:T(8,128)(2,1)} %copy-done.4, f32[16,256]{1,0:T(8,128)} %bitcast.30, f32[16,256]{1,0:T(8,128)} %bitcast.32, f32[256,256]{1,0:T(8,128)} %constant.26.clone.forward_ref, f32[256,256]{1,0:T(8,128)} %constant.27.clone.inverse_ref, ...), custom_call_target="tpu_custom_call" | custom-call | tf_op jit(solution)/shard_map/phase_step/pallas_call | solution.py:366
  56.5 1.5 %collective-permute-start.6 = (f32[16,256]{1,0:T(8,128)}, f32[16,256]{1,0:T(8,128)S(1)}, u32[]{:S(2)}, u32[]{:S(2)}) collective-permute-start(f32[16,256]{1,0:T(8,128)} %get-tuple-element.12), channel_id=1, source_target_pairs={{16,0},{24,8},{0,16},{8,24},{17,1},{25,9},{1,17},{9,25},{18,2},{26... | collective-permute-start | bytes 49160 | tf_op jit(solution)/shard_map/ppermute | solution.py:410
  58.0 2.5 %collective-permute-done.6 = f32[16,256]{1,0:T(8,128)S(1)} collective-permute-done((f32[16,256]{1,0:T(8,128)}, f32[16,256]{1,0:T(8,128)S(1)}, u32[]{:S(2)}, u32[]{:S(2)}) %collective-permute-start.6) | collective-permute-done | bytes 16416 | tf_op jit(solution)/shard_map/ppermute | solution.py:410
  60.5 1.3 %pad_maximum_fusion.spectra_ref = f32[2,16,256]{2,1,0:T(8,128)} fusion(f32[1,16,256]{2,1,0:T(8,128)S(1)} %bitcast.35, f32[1,16,256]{2,1,0:T(8,128)} %bitcast.34), kind=kLoop, calls=%fused_computation.2 | loop fusion | flops 8192 | bytes 65536 | tf_op jit(solution)/shard_map/stack | solution.py:474
  61.8 20.4 %backproject.1.mine_ref = bf16[16,128,256]{2,1,0:T(8,128)(2,1)} custom-call(s32[2]{0:T(128)} %pad_add_fusion.angles_ref, f32[2,16,256]{2,1,0:T(8,128)} %pad_maximum_fusion.spectra_ref, bf16[256,256]{1,0:T(8,128)(2,1)} %constant.22.clone.forward_ref, bf16[256,256]{1,0:T(8,128)(2,1)} %constant.23.clone.inverse_ref, bf16[256,256]{1,0:T(8,128)(2,1)} %constant.28.clone.down_ref, ...), custom_call_target="tpu_custom_call" | custom-call | tf_op jit(solution)/shard_map/backproject/pallas_call | solution.py:366
  82.2 0.0 collective-permute-start.7
  82.2 0.8 slice_bitcast_fusion
  83.0 1.3 %collective-permute-start.4 = (bf16[64,256]{1,0:T(8,128)(2,1)S(1)}, bf16[64,256]{1,0:T(8,128)(2,1)S(1)}, u32[]{:S(2)}, u32[]{:S(2)}) collective-permute-start(bf16[64,256]{1,0:T(8,128)(2,1)S(1)} %get-tuple-element.15), channel_id=1, source_target_pairs={{1,0},{2,1},{3,2},{4,3},{5,4},{6,5},{7,6},{9,8},{10,9},{11,10},{12... | collective-permute-start | bytes 98312 | tf_op jit(solution)/shard_map/ppermute | solution.py:437
  84.3 4.5 %collective-permute-start.3 = (bf16[64,256]{1,0:T(8,128)(2,1)S(1)}, bf16[64,256]{1,0:T(8,128)(2,1)S(1)}, u32[]{:S(2)}, u32[]{:S(2)}) collective-permute-start(bf16[64,256]{1,0:T(8,128)(2,1)S(1)} %get-tuple-element.16), channel_id=1, source_target_pairs={{0,1},{1,2},{2,3},{3,4},{4,5},{5,6},{6,7},{8,9},{9,10},{10,11},{11... | collective-permute-start | bytes 98312 | tf_op jit(solution)/shard_map/ppermute | solution.py:436
  88.8 0.0 collective-permute-done.4.after_ref
  88.9 1.6 %collective-permute-done.3.before_ref = bf16[64,256]{1,0:T(8,128)(2,1)S(1)} collective-permute-done((bf16[64,256]{1,0:T(8,128)(2,1)S(1)}, bf16[64,256]{1,0:T(8,128)(2,1)S(1)}, u32[]{:S(2)}, u32[]{:S(2)}) %collective-permute-start.3) | collective-permute-done | bytes 32800 | tf_op jit(solution)/shard_map/ppermute | solution.py:436
  90.4 0.0 copy-done.6
  90.4 0.6 copy-done.7
  91.0 3.0 %smooth.1 = (f32[16,64,256]{2,1,0:T(8,128)}, bf16[16,64,256]{2,1,0:T(8,128)(2,1)}) custom-call(f32[1024,256]{1,0:T(8,128)} %bitcast.25, f32[1024,256]{1,0:T(8,128)} %bitcast.26, bf16[64,256]{1,0:T(8,128)(2,1)} %copy-done.7, bf16[64,256]{1,0:T(8,128)(2,1)} %copy-done.6), custom_call_target="tpu_custom_call" | custom-call | tf_op jit(solution)/shard_map/smooth/pallas_call | solution.py:366
  94.0 0.0 collective-permute-start.5
  94.0 2.1 %collective-permute-done.5.base_other_ref = bf16[16,64,256]{2,1,0:T(8,128)(2,1)S(1)} collective-permute-done((bf16[16,64,256]{2,1,0:T(8,128)(2,1)}, bf16[16,64,256]{2,1,0:T(8,128)(2,1)S(1)}, u32[]{:S(2)}, u32[]{:S(2)}) %collective-permute-start.5) | collective-permute-done | bytes 524320 | tf_op jit(solution)/shard_map/ppermute | solution.py:407
  96.2 0.0 collective-permute-done.7.theirs_ref
  96.2 0.8 copy-done.1
  97.0 0.3 copy-done
  97.3 21.7 %project_new.1 = (f32[1024,256]{1,0:T(8,128)}, f32[2,16,256]{2,1,0:T(8,128)}) custom-call(s32[2]{0:T(128)} %pad_add_fusion.angles_ref, f32[16,64,256]{2,1,0:T(8,128)} %get-tuple-element.10.base_ref, bf16[16,64,256]{2,1,0:T(8,128)(2,1)} %copy-done.1, bf16[16,128,256]{2,1,0:T(8,128)(2,1)} %backproject.1.mine_ref, bf16[16,128,256]{2,1,0:T(8,128)(2,1)} %copy-done, ...), custom_call_target="tpu_custom_call" | custom-call | tf_op jit(solution)/shard_map/project_new/pallas_call | solution.py:366
  119.0 1.3 %slice_bitcast_fusion.4 = (f32[16,256]{1,0:T(8,128)S(1)}, f32[16,256]{1,0:T(8,128)}) fusion(f32[2,16,256]{2,1,0:T(8,128)} %get-tuple-element.14), kind=kLoop, calls=%fused_computation.5 | loop fusion | bytes 65536 | tf_op jit(solution)/shard_map/squeeze | solution.py:493
  120.4 1.5 %collective-permute-start.8 = (f32[16,256]{1,0:T(8,128)S(1)}, f32[16,256]{1,0:T(8,128)S(1)}, u32[]{:S(2)}, u32[]{:S(2)}) collective-permute-start(f32[16,256]{1,0:T(8,128)S(1)} %get-tuple-element.17), channel_id=1, source_target_pairs={{0,16},{8,24},{16,0},{24,8},{1,17},{9,25},{17,1},{25,9},{2,18},{10... | collective-permute-start | bytes 49160 | tf_op jit(solution)/shard_map/ppermute | solution.py:413
  121.8 2.2 %collective-permute-done.8.rest_1_ = f32[16,256]{1,0:T(8,128)S(1)} collective-permute-done((f32[16,256]{1,0:T(8,128)S(1)}, f32[16,256]{1,0:T(8,128)S(1)}, u32[]{:S(2)}, u32[]{:S(2)}) %collective-permute-start.8) | collective-permute-done | bytes 16416 | tf_op jit(solution)/shard_map/ppermute | solution.py:413
  124.1 0.6 copy-done.9
  124.7 1.8 %dual_step.1 = f32[16,256]{1,0:T(8,128)} custom-call(f32[16,256]{1,0:T(8,128)} %get-tuple-element.9.phase_ref, f32[16,256]{1,0:T(8,128)} %bitcast.33, f32[256,256]{1,0:T(8,128)} %constant.27.clone.inverse_ref, f32[16,256]{1,0:T(8,128)} %get-tuple-element.18.rest_0_, f32[16,256]{1,0:T(8,128)} %copy-done.9), custom_call_target="tpu_custom_call" | custom-call | tf_op jit(solution)/shard_map/dual_step/pallas_call | solution.py:366
  (8 shorter events, 0.0 us)
Async XLA Ops:
  0.6 2.8 %copy-start.5 = (f32[1,16,256]{2,1,0:T(8,128)S(1)}, f32[1,16,256]{2,1,0:T(8,128)}, u32[]{:S(2)}) copy-start(f32[1,16,256]{2,1,0:T(8,128)} %param.21) | copy-start | bytes 49156
  3.0 24.4 %collective-permute-start.1 = (bf16[16,64,256]{2,1,0:T(8,128)(2,1)}, bf16[16,64,256]{2,1,0:T(8,128)(2,1)S(1)}, u32[]{:S(2)}, u32[]{:S(2)}) collective-permute-start(bf16[16,64,256]{2,1,0:T(8,128)(2,1)} %to_slices.1.own_ref), channel_id=1, source_target_pairs={{0,8},{8,0},{16,24},{24,16},{1,9},{9,1},{17,25},{25,17},{2,10},{10... | collective-permute-start | bytes 1572872 | tf_op jit(solution)/shard_map/ppermute | solution.py:407
  4.1 14.5 %all-to-all-start = ((f32[8,16,256]{2,1,0:T(8,128)}), f32[8,16,256]{2,1,0:T(8,128)S(1)}, u32[]{:S(2)}, u32[]{:S(2)}) async-start(f32[8,16,256]{2,1,0:T(8,128)} %broadcast_in_dim.14), calls=%async_computation | async-start | bytes 262144 | tf_op jit(solution)/shard_map/all_to_all | solution.py:415
  10.9 3.6 %collective-permute-start = (s32[1]{0:T(128)}, s32[1]{0:T(128)}, u32[]{:S(2)}, u32[]{:S(2)}) collective-permute-start(s32[1]{0:T(128)} %param.27), channel_id=1, source_target_pairs={{16,0},{24,8},{0,16},{8,24},{17,1},{25,9},{1,17},{9,25},{18,2},{26... | collective-permute-start | bytes 20 | tf_op jit(solution)/shard_map/ppermute | solution.py:410
  18.6 0.7 copy-start.2
  24.0 27.3 %all-to-all-start.1 = ((bf16[8,16,256]{2,1,0:T(8,128)(2,1)}), bf16[8,16,256]{2,1,0:T(8,128)(2,1)S(1)}, u32[]{:S(2)}, u32[]{:S(2)}) async-start(bf16[8,16,256]{2,1,0:T(8,128)(2,1)} %bitcast.28), calls=%async_computation.1 | async-start | bytes 131072 | tf_op jit(solution)/shard_map/all_to_all | solution.py:455
  27.4 0.8 copy-start.3
  49.8 3.7 %collective-permute-start.2 = (f32[16,256]{1,0:T(8,128)S(1)}, f32[16,256]{1,0:T(8,128)S(1)}, u32[]{:S(2)}, u32[]{:S(2)}) collective-permute-start(f32[16,256]{1,0:T(8,128)S(1)} %get-tuple-element.19), channel_id=1, source_target_pairs={{0,16},{8,24},{16,0},{24,8},{1,17},{9,25},{17,1},{25,9},{2,18},{10... | collective-permute-start | bytes 49160 | tf_op jit(solution)/shard_map/ppermute | solution.py:413
  51.3 2.3 %copy-start.4 = (bf16[8,16,256]{2,1,0:T(8,128)(2,1)}, bf16[8,16,256]{2,1,0:T(8,128)(2,1)S(1)}, u32[]{:S(2)}) copy-start(bf16[8,16,256]{2,1,0:T(8,128)(2,1)S(1)} %all-to-all-done.1.grad_ref) | copy-start | bytes 196612
  53.6 0.6 copy-start.8
  56.5 3.9 %collective-permute-start.6 = (f32[16,256]{1,0:T(8,128)}, f32[16,256]{1,0:T(8,128)S(1)}, u32[]{:S(2)}, u32[]{:S(2)}) collective-permute-start(f32[16,256]{1,0:T(8,128)} %get-tuple-element.12), channel_id=1, source_target_pairs={{16,0},{24,8},{0,16},{8,24},{17,1},{25,9},{1,17},{9,25},{18,2},{26... | collective-permute-start | bytes 49160 | tf_op jit(solution)/shard_map/ppermute | solution.py:410
  82.2 14.0 %collective-permute-start.7 = (bf16[16,128,256]{2,1,0:T(8,128)(2,1)}, bf16[16,128,256]{2,1,0:T(8,128)(2,1)S(1)}, u32[]{:S(2)}, u32[]{:S(2)}) collective-permute-start(bf16[16,128,256]{2,1,0:T(8,128)(2,1)} %backproject.1.mine_ref), channel_id=1, source_target_pairs={{0,8},{8,0},{16,24},{24,16},{1,9},{9,1},{17,25},{25,17},{2,10},{10... | collective-permute-start | bytes 3145736 | tf_op jit(solution)/shard_map/ppermute | solution.py:407
  83.0 5.9 %collective-permute-start.4 = (bf16[64,256]{1,0:T(8,128)(2,1)S(1)}, bf16[64,256]{1,0:T(8,128)(2,1)S(1)}, u32[]{:S(2)}, u32[]{:S(2)}) collective-permute-start(bf16[64,256]{1,0:T(8,128)(2,1)S(1)} %get-tuple-element.15), channel_id=1, source_target_pairs={{1,0},{2,1},{3,2},{4,3},{5,4},{6,5},{7,6},{9,8},{10,9},{11,10},{12... | collective-permute-start | bytes 98312 | tf_op jit(solution)/shard_map/ppermute | solution.py:437
  84.3 6.1 %collective-permute-start.3 = (bf16[64,256]{1,0:T(8,128)(2,1)S(1)}, bf16[64,256]{1,0:T(8,128)(2,1)S(1)}, u32[]{:S(2)}, u32[]{:S(2)}) collective-permute-start(bf16[64,256]{1,0:T(8,128)(2,1)S(1)} %get-tuple-element.16), channel_id=1, source_target_pairs={{0,1},{1,2},{2,3},{3,4},{4,5},{5,6},{6,7},{8,9},{9,10},{10,11},{11... | collective-permute-start | bytes 98312 | tf_op jit(solution)/shard_map/ppermute | solution.py:436
  88.9 1.6 %copy-start.6 = (bf16[64,256]{1,0:T(8,128)(2,1)}, bf16[64,256]{1,0:T(8,128)(2,1)S(1)}, u32[]{:S(2)}) copy-start(bf16[64,256]{1,0:T(8,128)(2,1)S(1)} %collective-permute-done.4.after_ref) | copy-start | bytes 98308
  90.4 0.6 copy-start.7
  94.0 2.1 %collective-permute-start.5 = (bf16[16,64,256]{2,1,0:T(8,128)(2,1)}, bf16[16,64,256]{2,1,0:T(8,128)(2,1)S(1)}, u32[]{:S(2)}, u32[]{:S(2)}) collective-permute-start(bf16[16,64,256]{2,1,0:T(8,128)(2,1)} %get-tuple-element.11), channel_id=1, source_target_pairs={{0,8},{8,0},{16,24},{24,16},{1,9},{9,1},{17,25},{25,17},{2,10},{10... | collective-permute-start | bytes 1572872 | tf_op jit(solution)/shard_map/ppermute | solution.py:407
  96.2 0.8 copy-start.1
  96.2 1.1 copy-start
  120.4 3.7 %collective-permute-start.8 = (f32[16,256]{1,0:T(8,128)S(1)}, f32[16,256]{1,0:T(8,128)S(1)}, u32[]{:S(2)}, u32[]{:S(2)}) collective-permute-start(f32[16,256]{1,0:T(8,128)S(1)} %get-tuple-element.17), channel_id=1, source_target_pairs={{0,16},{8,24},{16,0},{24,8},{1,17},{9,25},{17,1},{25,9},{2,18},{10... | collective-permute-start | bytes 49160 | tf_op jit(solution)/shard_map/ppermute | solution.py:413
  124.1 0.6 copy-start.9
where the time goes:
time: 129 us; the launch traced here: 127 us
  Pallas kernels  76.7 us (59%)
  starting transfers between devices  22.4 us (17%)
  waiting for transfers between devices  14.9 us (12%)
  local copies, waits for them, and re-layouts  8.56 us (7%)
  other arithmetic  2.59 us (2%)
  between operations  1.39 us (1%)
    pallas_call x8, Pallas kernels, call(): pl.pallas_call(kernel, grid=grid, out_shape=outs, in_specs=specs, out_spe...  76.7 us
    all_to_all x1, starting transfers between devices, shards(): lax.all_to_all(jnp.broadcast_to(phase, (tiles, slices, length)), 'tile',...  6.83 us
    ppermute x1, starting transfers between devices, shards(): lax.ppermute(own[-1], 'tile', [(i, i + 1) for i in range(edge_count)])  4.55 us
    ppermute x2, waiting for transfers between devices, to_peer(): lax.ppermute(value, 'ang', [(i, (i + 2 * j) % ang) for i in range(ang)])  4.49 us
    unnamed x20, local copies, waits for them, and re-layouts  4.43 us
    ppermute x2, waiting for transfers between devices, from_peer(): lax.ppermute(value, 'ang', [((i + 2 * j) % ang, i) for i in range(ang)])  3.91 us
    all_to_all x1, starting transfers between devices, shards(): grad = lax.all_to_all(grad, 'tile', split_axis=0, concat_axis=0, tiled=True)  3.35 us
    ppermute x2, starting transfers between devices, from_peer(): lax.ppermute(value, 'ang', [((i + 2 * j) % ang, i) for i in range(ang)])  2.98 us
  transfers between devices with their start and end apart: 11, of which 7 were waited for; matrix products, arithmetic and copies ran while one was open for 3% of the time, Pallas kernels for 22%

commit v1 on v0

v1 whole, which is shorter than its diff:
```python
import functools
import math

import jax
import jax.numpy as jnp
import numpy as np
from jax import lax
from jax.experimental import pallas as pl
from jax.experimental.pallas import tpu as pltpu
from jax.sharding import PartitionSpec as P

angle_center = 90.0
rho_weight = 1.0
eta_step = 0.01
tau_step = 1.0
smooth_weight = 0.25

F32 = jnp.float32
BF16 = jnp.bfloat16
VMEM_SPEC = pl.BlockSpec(memory_space=pltpu.VMEM)
SMEM_SPEC = pl.BlockSpec(memory_space=pltpu.SMEM)
VMEM_LIMIT = 40 * 1024 * 1024


def table_pair(length):
    index = np.arange(length)
    phases = (index[:, None] * index[None, :] % length) * (2.0 * np.pi / length)
    return np.cos(phases).astype(np.float32), np.sin(phases).astype(np.float32)


def packed_tables(length):
    half = length // 2
    cos_t, sin_t = table_pair(length)
    bf = np.asarray(jnp.bfloat16).dtype if False else jnp.bfloat16
    out = []
    for kind in (np.float32, bf):
        c = cos_t.astype(kind).astype(np.float32)
        s = sin_t.astype(kind).astype(np.float32)
        forward = np.concatenate([c[:, : half + 1], -s[:, 1:half]], axis=1)
        weight = np.full((length, 1), 2.0 / length, np.float32)
        weight[0] = weight[half] = 1.0 / length
        inverse = forward.T * weight
        out.append((forward.astype(kind), inverse.astype(kind)))
    return out


def split_pair(array):
    high = array.astype(jnp.bfloat16)
    low = (array - high.astype(np.float32)).astype(jnp.bfloat16)
    return np.stack([high, low])


def patch_tables(width):
    cos_t, sin_t = table_pair(width)
    c = cos_t / np.float32(math.sqrt(width))
    s = sin_t / np.float32(math.sqrt(width))
    right = np.block([[c, -s], [s, c]])
    left = np.block([[c, s], [-s, c]])
    right_conj = np.block([[c, s], [-s, c]])
    left_conj = np.block([[c, -s], [s, c]])
    return tuple(split_pair(m.astype(np.float32)) for m in (right, left, left_conj, right_conj))


def dot(left, right):
    return jnp.dot(left, right, preferred_element_type=F32)


def dot_high(left, right):
    return jnp.dot(left, right, precision=lax.Precision.HIGHEST, preferred_element_type=F32)


def dot_split(left, right):
    def parts(value):
        if value.dtype == BF16:
            return value[0], value[1]
        high = value.astype(BF16)
        return high, (value - high.astype(F32)).astype(BF16)

    left_high, left_low = parts(left)
    right_high, right_low = parts(right)
    return dot(left_high, right_high) + dot(left_low, right_high) + dot(left_high, right_low)


def turn(re, im, c1, s, c2, sign):
    if sign > 0:
        return re * c1 + im * s, im * c2 - re * s
    return re * c1 - im * s, im * c2 + re * s


def fill_turn_tables(angle, length, row_ref, col_ref, nyq_ref):
    half = length // 2
    unit = 2.0 * math.pi / length
    theta = (jnp.full((8, half), angle, jnp.int32).astype(F32) - angle_center) * (math.pi / 360.0)
    coef_a = -(jnp.sin(0.5 * theta) / jnp.cos(0.5 * theta))
    coef_b = jnp.sin(theta)

    lane = lax.broadcasted_iota(jnp.int32, (8, half), 1)
    sub = lax.broadcasted_iota(jnp.int32, (8, half), 0)
    freq = jnp.where(lane == 0, half, lane).astype(F32)
    phase = unit * coef_a * freq
    base = phase * sub.astype(F32)
    base_c, base_s = jnp.cos(base), jnp.sin(base)
    for block in range(length // 64):
        first = 8 * block * 8 - half
        step = phase * (first + 8 * sub).astype(F32)
        step_c, step_s = jnp.cos(step), jnp.sin(step)
        for q in range(8):
            sc, ss = step_c[q : q + 1], step_s[q : q + 1]
            c2 = base_c * sc - base_s * ss
            s = base_s * sc + base_c * ss
            rows = pl.ds((block * 8 + q) * 8, 8)
            row_ref[0, rows, :] = jnp.where(lane == 0, 1.0, c2)
            row_ref[1, rows, :] = jnp.where(lane == 0, 0.0, s)
            row_ref[2, rows, :] = c2

    for side in range(2):
        place = (lane + (side * half - half)).astype(F32)
        phase = unit * coef_b * place
        lanes = slice(side * half, side * half + half)
        base = phase * sub.astype(F32)
        base_c, base_s = jnp.cos(base), jnp.sin(base)
        for block in range(half // 64):
            step = phase * (block * 64 + 8 * sub).astype(F32)
            step_c, step_s = jnp.cos(step), jnp.sin(step)
            for q in range(8):
                sc, ss = step_c[q : q + 1], step_s[q : q + 1]
                rows = pl.ds((block * 8 + q) * 8, 8)
                col_ref[0, rows, lanes] = base_c * sc - base_s * ss
                col_ref[1, rows, lanes] = base_s * sc + base_c * ss
        top = jnp.where(sub == 0, jnp.cos(phase * float(half)), base_c)
        nyq_ref[:, lanes] = top


class Tables:
    def __init__(self, row, col, nyq):
        self.row, self.col, self.nyq = row, col, nyq

    def rows(self):
        return self.row[0], self.row[1], self.row[2]

    def chip_rows(self, share):
        here = lax.axis_index("ang")
        other = here + 1 - 2 * lax.rem(here, 2)
        places = [pl.ds(pl.multiple_of(which * share, 8), share) for which in (here, other)]
        return tuple(jnp.concatenate([self.row[part, rows, :] for rows in places], axis=0) for part in range(3))

    def columns(self):
        c1 = self.col[0]
        return c1, self.col[1], jnp.concatenate([self.nyq[...], c1[8:]], axis=0)


def turn_rows(spectrum, tables, sign):
    half = spectrum.shape[1] // 2
    return turn(spectrum[:, :half], spectrum[:, half:], *tables, sign)


def turn_columns(spectrum, tables, sign):
    half = spectrum.shape[0] // 2
    pair = turn(spectrum[:half], spectrum[half:], *tables, sign)
    return jnp.concatenate(pair, axis=0).astype(BF16)


def side_by_side(value, count):
    rows = value.shape[0] // count
    return jnp.concatenate([value[i * rows : (i + 1) * rows] for i in range(count)], axis=1)


def stacked(value, count):
    columns = value.shape[1] // count
    return jnp.concatenate([value[:, i * columns : (i + 1) * columns] for i in range(count)], axis=0)


def block_of(value, i, count, axis):
    size = value.shape[axis] // count
    return lax.slice_in_dim(value, i * size, (i + 1) * size, axis=axis)


def project_slices(slab, count, share, tables, consts, lines_refs):
    forward_ref, inverse_ref, down_ref, up_ref = consts
    here = lax.axis_index("ang")
    spectrum = dot(slab, forward_ref[...])
    for table, lines_ref in zip(tables, lines_refs):
        chip_rows = table.chip_rows(share)
        turned = [
            jnp.concatenate(turn_rows(block_of(spectrum, i, count, 0), chip_rows, 1), axis=1).astype(BF16)
            for i in range(count)
        ]
        first = dot(jnp.concatenate(turned, axis=0), inverse_ref[...]).astype(BF16)
        columns = dot(down_ref[here], side_by_side(first, count))
        turned = [turn_columns(block_of(columns, i, count, 1), table.columns(), 1) for i in range(count)]
        second = dot(up_ref[...], jnp.concatenate(turned, axis=1)).astype(BF16)
        last = dot(stacked(second, count), forward_ref[...])
        for i in range(count):
            re, im = turn_rows(block_of(last, i, count, 0), table.rows(), 1)
            sums = [jnp.sum(part, axis=0, keepdims=True) for part in (re, im)]
            lines_ref[pl.ds(i, 1), :] = jnp.concatenate(sums, axis=1)


def take(refs, *counts):
    refs, out = list(refs), []
    for count in counts:
        out.append(refs[:count])
        refs = refs[count:]
    return out


def as_tables(refs):
    return [Tables(*refs[i : i + 3]) for i in range(0, len(refs), 3)]


def project_kernel(groups, slices, *refs):
    angle_refs, sides, consts, lines_refs, bases, edges, table_refs = take(
        refs, groups, 4, 4, groups, 2, 2, 3 * groups
    )
    share = sides[0].shape[0] // slices
    length = consts[0].shape[0]
    for g in range(groups):
        fill_turn_tables(angle_refs[g][0], length, *table_refs[3 * g : 3 * g + 3])

    def rows(z):
        parts = [ref[pl.ds(z, share, stride=slices), :] for ref in sides]
        return [jnp.concatenate(parts[:2], axis=1), jnp.concatenate(parts[2:], axis=1)]

    slab = []
    past = None
    now = rows(0)
    for z in range(slices):
        later = rows(z + 1) if z + 1 < slices else None
        for place in range(2):
            slab.append(now[place].astype(BF16))
            near = [side[place] for side in (past, later) if side is not None]
            base = (1.0 - 2.0 * tau_step * smooth_weight) * now[place]
            base = base + (tau_step * smooth_weight) * sum(near[1:], near[0])
            bases[place][z] = base.astype(bases[place].dtype)
        past, now = now, later
    for edge_ref, part in zip(edges, (slab[-2:], slab[:2])):
        edge_ref[...] = jnp.concatenate(part, axis=0)
    project_slices(
        jnp.concatenate(slab, axis=0), slices, share, as_tables(table_refs), consts, lines_refs
    )


def back_kernel(groups, *refs):
    spectra_refs, consts, table_refs, (out_ref,) = take(refs, groups, 4, 3 * groups, 1)
    forward_ref, inverse_ref, down_ref, up_ref = consts
    slices, pair, length = out_ref.shape
    half = length // 2
    here = lax.axis_index("ang")
    totals = None
    for table, spectra_ref in zip(as_tables(table_refs), spectra_refs):
        turned = []
        for z in range(slices):
            line = spectra_ref[pl.ds(z, 1), :]
            pieces = turn(line[:, :half], line[:, half:], *table.rows(), -1)
            turned.append(jnp.concatenate(pieces, axis=1).astype(BF16))
        spread = dot(jnp.concatenate(turned, axis=0), inverse_ref[...]).astype(BF16)
        columns = dot(down_ref[...], side_by_side(spread, slices))
        turned = [turn_columns(block_of(columns, i, slices, 1), table.columns(), -1) for i in range(slices)]
        second = dot(up_ref[here], jnp.concatenate(turned, axis=1)).astype(BF16)
        last = dot(stacked(second, slices), forward_ref[...])
        chip_rows = table.chip_rows(pair // 2)
        turned = [
            jnp.concatenate(turn_rows(block_of(last, i, slices, 0), chip_rows, -1), axis=1)
            for i in range(slices)
        ]
        totals = turned if totals is None else [old + new for old, new in zip(totals, turned)]
    total = jnp.concatenate([value.astype(BF16) for value in totals], axis=0)
    out_ref[...] = dot(total, inverse_ref[...]).astype(BF16).reshape(out_ref.shape)


def update_kernel(groups, first, last, aliased, *refs):
    bases, halos, shares, consts, table_refs, unused, (volume_ref,), lines_refs, sides = take(
        refs, 2, 2, 2, 4, 3 * groups, aliased, 1, groups, 2
    )
    own_ref, other_ref = bases
    mine_ref, theirs_ref = shares
    slices, share, length = own_ref.shape
    half = length // 2
    slab = []
    for z in range(slices):
        own = own_ref[z] - tau_step * (
            mine_ref[z, :share, :].astype(F32) + theirs_ref[z, share:, :].astype(F32)
        )
        other = other_ref[z].astype(F32) - tau_step * (
            mine_ref[z, share:, :].astype(F32) + theirs_ref[z, :share, :].astype(F32)
        )
        for needed, halo_ref in ((first and z == 0, halos[0]), (last and z == slices - 1, halos[1])):
            if needed:
                halo = (tau_step * smooth_weight) * halo_ref[...].astype(F32)
                own, other = own + halo[:share], other + halo[share:]
        for side in range(2):
            sides[side][pl.ds(z, share, stride=slices), :] = own[:, side * half : (side + 1) * half]
        slab += [own.astype(BF16), other.astype(BF16)]
    project_slices(
        jnp.concatenate(slab, axis=0), slices, share, as_tables(table_refs), consts, lines_refs
    )
    whole = jnp.concatenate([ref[...] for ref in sides], axis=1)
    volume_ref[...] = whole.reshape(volume_ref.shape)


def gradient_kernel(
    offsets_ref, image_ref, measured_ref, probe_r_ref, probe_i_ref,
    right_ref, left_ref, left_conj_ref, right_conj_ref, out_ref,
):
    positions, height, width = measured_ref.shape
    length = image_ref.shape[1]
    image = image_ref[...]
    cos_image, sin_image = jnp.cos(image), jnp.sin(image)
    probe_r, probe_i = probe_r_ref[...], probe_i_ref[...]
    waves = []
    for p in range(positions):
        back = length - offsets_ref[0, p]
        cos_p = pltpu.roll(cos_image, back, 1)[:, :width]
        sin_p = pltpu.roll(sin_image, back, 1)[:, :width]
        waves.append((probe_r * cos_p - probe_i * sin_p, probe_r * sin_p + probe_i * cos_p))

    def to_columns(value):
        parts = [block_of(value, p, positions, 0) for p in range(positions)]
        return jnp.concatenate(
            [jnp.concatenate([part[:, i * width : (i + 1) * width] for part in parts], axis=1) for i in range(2)],
            axis=0,
        )

    def to_rows(value):
        parts = [block_of(value, p, positions, 1) for p in range(positions)]
        return jnp.concatenate(
            [jnp.concatenate([part[:height], part[height:]], axis=1) for part in parts], axis=0
        )

    entry = jnp.concatenate([jnp.concatenate(wave, axis=1) for wave in waves], axis=0)
    far = dot_split(left_ref[...], to_columns(dot_split(entry, right_ref[...])))
    far_r, far_i = far[:height], far[height:]
    measured = jnp.concatenate([measured_ref[p] for p in range(positions)], axis=1)
    misfit = far_r * far_r + far_i * far_i - measured
    weighted = jnp.concatenate([misfit * far_r, misfit * far_i], axis=0)
    chi = dot_split(to_rows(dot_split(left_conj_ref[...], weighted)), right_conj_ref[...])
    total = jnp.zeros((height, length), F32)
    for p in range(positions):
        part = block_of(chi, p, positions, 0)
        wave_r, wave_i = waves[p]
        term = 2.0 * (part[:, width:] * wave_r - part[:, :width] * wave_i)
        padded = jnp.concatenate([term, jnp.zeros((height, length - width), F32)], axis=1)
        total = total + pltpu.roll(padded, offsets_ref[0, p], 1)
    out_ref[...] = total.astype(out_ref.dtype).reshape(out_ref.shape)


def projected(line_refs, inverse_ref):
    line = line_refs[0][...]
    for other in line_refs[1:]:
        line = line + other[...]
    return dot_split(line, inverse_ref[...]) * (1.0 / math.sqrt(line.shape[1]))


def line_kernel(peers, phase_ref, dual_ref, inverse_ref, *refs):
    line_refs, (phase_part_ref, resid_part_ref) = take(refs, peers, 2)
    proj_old = projected(line_refs, inverse_ref)
    phase, dual = phase_ref[...], dual_ref[...]
    phase_part = phase - eta_step * (dual + rho_weight * (phase - proj_old))
    phase_part_ref[...] = phase_part
    resid_part_ref[...] = rho_weight * (proj_old - phase_part) - dual


def phase_kernel(grad_ref, phase_part_ref, resid_part_ref, forward_ref, phase_new_ref, spectrum_ref):
    grad = grad_ref[0].astype(F32)
    for t in range(1, grad_ref.shape[0]):
        grad = grad + grad_ref[t].astype(F32)
    grad = eta_step * grad
    phase_new_ref[...] = phase_part_ref[...] - grad
    resid = resid_part_ref[...] + rho_weight * grad
    spectrum_ref[...] = dot_split(resid, forward_ref[...]) * (1.0 / math.sqrt(resid.shape[1]))


def dual_kernel(peers, phase_ref, dual_ref, inverse_ref, *refs):
    line_refs, (dual_new_ref,) = take(refs, peers, 1)
    proj_new = projected(line_refs, inverse_ref)
    dual_new_ref[...] = dual_ref[...] + rho_weight * (phase_ref[...] - proj_new)


def call(kernel, outs, args, specs=None, out_specs=None, scratch=(), flops=0, name=None, grid=(), aliases=None):
    return pl.pallas_call(
        kernel,
        grid=grid,
        out_shape=tuple(outs),
        in_specs=specs or [VMEM_SPEC] * len(args),
        out_specs=tuple(out_specs or [VMEM_SPEC] * len(outs)),
        scratch_shapes=list(scratch),
        input_output_aliases=aliases or {},
        cost_estimate=pl.CostEstimate(flops=flops, bytes_accessed=1 << 20, transcendentals=0),
        name=name,
        compiler_params=pltpu.CompilerParams(vmem_limit_bytes=VMEM_LIMIT),
    )(*args)


def shards(volume, phase, dual, probe_real, probe_imag, intensity, offsets, angle_index):
    share, slices, length = volume.shape
    width = probe_real.shape[1]
    half = length // 2
    ang = lax.axis_size("ang")
    tiles = lax.axis_size("tile")
    groups = ang // 2
    pair = 2 * share
    parts = 2 if slices % 16 == 0 else 1
    some = slices // parts
    shape = jax.ShapeDtypeStruct

    (forward_full, inverse_full), (forward, inverse) = packed_tables(length)
    forward_full, inverse_full = split_pair(forward_full), split_pair(inverse_full)
    down, up = forward.T, inverse.T
    owners = [
        np.r_[i * share : (i + 1) * share, (i ^ 1) * share : ((i ^ 1) + 1) * share] for i in range(ang)
    ]
    down_part = np.stack([down[:, rows] for rows in owners])
    up_part = np.stack([up[rows] for rows in owners])
    right, left, left_conj, right_conj = patch_tables(width)
    line = shape((slices, length), F32)
    work = 2 * 2 * length * length * length * slices * groups

    def swap(value):
        return lax.ppermute(value, "ang", [(i, i ^ 1) for i in range(ang)])

    def from_peer(value, j):
        return lax.ppermute(value, "ang", [((i + 2 * j) % ang, i) for i in range(ang)])

    def to_peer(value, j):
        return lax.ppermute(value, "ang", [(i, (i + 2 * j) % ang) for i in range(ang)])

    def lanes(side):
        return pl.BlockSpec((share * slices, half), lambda _: (0, side))

    def gathered(lines):
        return [lines[0]] + [to_peer(lines[j], j) for j in range(1, groups)]

    image = lax.all_to_all(
        jnp.broadcast_to(phase, (tiles, slices, length)), "tile", split_axis=0, concat_axis=0, tiled=True
    ).reshape(tiles * slices, length)
    flat = volume.reshape(share * slices, length)
    other = swap(flat)
    angles = [angle_index] + [from_peer(angle_index, j) for j in range(1, groups)]

    tables_shape = [
        shape((3, length, half), F32), shape((2, half, length), F32), shape((8, length), F32)
    ] * groups
    outs = call(
        functools.partial(project_kernel, groups, slices),
        [line] * groups
        + [shape((slices, share, length), F32), shape((slices, share, length), BF16)]
        + [shape((pair, length), BF16)] * 2
        + tables_shape,
        angles + [flat, flat, other, other, forward, inverse, down_part, up],
        [SMEM_SPEC] * groups + [lanes(0), lanes(1)] * 2 + [VMEM_SPEC] * 4,
        grid=(1,),
        flops=3 * work,
        name="project_old",
    )
    lines, bases, edges, tables = take(outs, groups, 2, 2, 3 * groups)
    old = gathered(lines)

    image, edges = lax.optimization_barrier((image, edges))
    (grad,) = call(
        gradient_kernel,
        [shape((tiles, slices, length), BF16)],
        [offsets, image, intensity[0], probe_real, probe_imag, right, left, left_conj, right_conj],
        [SMEM_SPEC] + [VMEM_SPEC] * 8,
        flops=2 * work,
        name="gradient",
    )
    grad, edges = lax.optimization_barrier((grad, edges))
    grad = lax.all_to_all(grad, "tile", split_axis=0, concat_axis=0, tiled=True)

    before = lax.ppermute(edges[0], "tile", [(i, i + 1) for i in range(tiles - 1)])
    after = lax.ppermute(edges[1], "tile", [(i + 1, i) for i in range(tiles - 1)])

    phase_part, resid_part = call(
        functools.partial(line_kernel, groups), [line, line], [phase[0], dual[0], inverse_full] + old,
        name="line_step",
    )
    grad, before, after = lax.optimization_barrier((grad, before, after))
    phase_new, spectrum = call(
        phase_kernel, [line, line], [grad, phase_part, resid_part, forward_full], name="phase_step"
    )
    spectra = [spectrum] + [from_peer(spectrum, j) for j in range(1, groups)]

    halves = []
    for h in range(parts):
        (mine,) = call(
            functools.partial(back_kernel, groups),
            [shape((some, pair, length), BF16)],
            spectra + [forward, inverse, down, up_part] + tables,
            [pl.BlockSpec((some, length), lambda _, h=h: (h, 0))] * groups + [VMEM_SPEC] * (4 + 3 * groups),
            grid=(1,),
            flops=3 * work // parts,
            name="backproject",
        )
        halves.append((mine, swap(mine)))

    results = []
    for h in range(parts):
        block = pl.BlockSpec((some, share, length), lambda _, h=h: (h, 0, 0))
        args = bases + [before, after] + list(halves[h]) + [forward, inverse, down_part, up] + tables
        results = call(
            functools.partial(update_kernel, groups, h == 0, h == parts - 1, len(results)),
            [shape((share, slices, length), F32)] + [line] * groups,
            args + list(results),
            [block] * 2 + [VMEM_SPEC] * (8 + 3 * groups) + [pl.BlockSpec(memory_space=pl.ANY)] * len(results),
            [pl.BlockSpec((share, some, length), lambda _, h=h: (0, h, 0))]
            + [pl.BlockSpec((some, length), lambda _, h=h: (h, 0))] * groups,
            scratch=[pltpu.VMEM((share * some, half), F32)] * 2,
            grid=(1,),
            flops=3 * work // parts,
            aliases={len(args) + i: i for i in range(len(results))},
            name="project_new",
        )
    volume_new, lines = results[0], results[1:]
    (dual_new,) = call(
        functools.partial(dual_kernel, groups), [line],
        [phase_new, dual[0], inverse_full] + gathered(lines),
        name="dual_step",
    )
    return phase_new[None], volume_new, dual_new[None]


def solution(mesh):
    placed = (
        P("ang", "tile", None),
        P("ang", "tile", None),
        P("ang", "tile", None),
        P(),
        P(),
        P("ang", "tile", None, None),
        P("ang", "tile"),
        P("ang"),
    )
    return jax.shard_map(
        shards,
        mesh=mesh,
        in_specs=placed,
        out_specs=(P("ang", "tile", None), P("ang", "tile", None), P("ang", "tile", None)),
        check_vma=False,
    )
```

time: 129 us -> 72.2 us (0.56); the launches traced: 127 us -> 71.6 us
  Pallas kernels: 76.7 us -> 25 us
  waiting for transfers between devices: 14.9 us -> 10.2 us
  local copies, waits for them, and re-layouts: 8.56 us -> 11.9 us
  other arithmetic: 2.59 us -> 0 us
    pallas_call x8 -> x9, Pallas kernels: 76.7 us -> 25 us  [call(): pl.pallas_call(kernel, grid=grid, out_shape=tuple(outs), in_specs=specs o...]
    unnamed x20 -> x60, local copies, waits for them, and re-layouts: 4.43 us -> 10.5 us
    squeeze x3 -> x0, local copies, waits for them, and re-layouts: 3.45 us -> none  [the longest x1 1.34 us: shards(): old = [lines[0]] + [to_peer(lines[j], j) for j in range(1, groups)]]
    all_to_all x1, starting transfers between devices: 3.35 us -> 6.13 us  [shards(): grad = lax.all_to_all(grad, 'tile', split_axis=0, concat_axis=0, tiled=True)]
    all_to_all x1, waiting for transfers between devices: 2.77 us -> 0.01 us  [shards(): lax.all_to_all(jnp.broadcast_to(phase, (tiles, slices, length)), 'tile',...]
    ppermute x3, waiting for transfers between devices: 2.12 us -> 0.01 us  [swap(): return lax.ppermute(value, 'ang', [(i, i ^ 1) for i in range(ang)])]
    ppermute x2, waiting for transfers between devices: 4.49 us -> 6.39 us  [to_peer(): lax.ppermute(value, 'ang', [(i, (i + 2 * j) % ang) for i in range(ang)])]
    ppermute x2, starting transfers between devices: 2.98 us -> 1.16 us  [to_peer(): lax.ppermute(value, 'ang', [(i, (i + 2 * j) % ang) for i in range(ang)])]
  transfers between devices with their start and end apart: 11 -> 11, of which waited for: 7 -> 4; matrix products, arithmetic and copies ran while one was open for 3% -> 2% of each run, Pallas kernels for 22% -> 20%
where the time goes in v1:
time: 72.2 us; the launch traced here: 71.6 us
  Pallas kernels  25 us (35%)
  starting transfers between devices  22.9 us (32%)
  local copies, waits for them, and re-layouts  11.9 us (16%)
  waiting for transfers between devices  10.2 us (14%)
  between operations  1.53 us (2%)
    pallas_call x9, Pallas kernels, call(): pl.pallas_call(kernel, grid=grid, out_shape=tuple(outs), in_specs=specs o...  25 us
    unnamed x60, local copies, waits for them, and re-layouts  10.5 us
    ppermute x2, waiting for transfers between devices, to_peer(): lax.ppermute(value, 'ang', [(i, (i + 2 * j) % ang) for i in range(ang)])  6.39 us
    all_to_all x1, starting transfers between devices, shards(): grad = lax.all_to_all(grad, 'tile', split_axis=0, concat_axis=0, tiled=True)  6.13 us
    all_to_all x1, starting transfers between devices, shards(): lax.all_to_all(jnp.broadcast_to(phase, (tiles, slices, length)), 'tile',...  5.97 us
    ppermute x1, starting transfers between devices, shards(): lax.ppermute(edges[0], 'tile', [(i, i + 1) for i in range(tiles - 1)])  3.92 us
    ppermute x2, waiting for transfers between devices, from_peer(): lax.ppermute(value, 'ang', [((i + 2 * j) % ang, i) for i in range(ang)])  3.2 us
    ppermute x2, starting transfers between devices, from_peer(): lax.ppermute(value, 'ang', [((i + 2 * j) % ang, i) for i in range(ang)])  3.11 us
  transfers between devices with their start and end apart: 11, of which 4 were waited for; matrix products, arithmetic and copies ran while one was open for 2% of the time, Pallas kernels for 20%

profile of v1, /device:TPU:0, one launch (start us, length us, event | category | flops | bytes accessed | tf_op | source)
XLA Modules:
  0.0 71.6 jit_solution(5913387257488244907)
XLA Ops:
  0.6 0.0 copy-start.10
  0.6 0.5 collective-permute-start.1
  1.2 2.6 %collective-permute-start = (s32[1]{0:T(128)}, s32[1]{0:T(128)}, u32[]{:S(2)}, u32[]{:S(2)}) collective-permute-start(s32[1]{0:T(128)} %param.27), channel_id=1, source_target_pairs={{16,0},{24,8},{0,16},{8,24},{17,1},{25,9},{1,17},{9,25},{18,2},{26... | collective-permute-start | bytes 20 | tf_op jit(solution)/shard_map/ppermute | solution.py:422
  3.7 1.4 %broadcast_in_dim.14 = f32[8,16,256]{2,1,0:T(8,128)} broadcast(f32[16,256]{1,0:T(8,128)} %bitcast.8), dimensions={1,2} | broadcast | bytes 147456 | tf_op jit(solution)/shard_map/broadcast_in_dim | solution.py:434
  5.1 6.0 %all-to-all-start = ((f32[8,16,256]{2,1,0:T(8,128)}), f32[8,16,256]{2,1,0:T(8,128)S(1)}, u32[]{:S(2)}, u32[]{:S(2)}) async-start(f32[8,16,256]{2,1,0:T(8,128)} %broadcast_in_dim.14), calls=%async_computation | async-start | bytes 262144 | tf_op jit(solution)/shard_map/all_to_all | solution.py:433
  11.7 0.0 collective-permute-done.refs_1_
  11.7 0.0 collective-permute-done.1.refs_4_.refs_5_
  11.8 0.0 copy-start.5
  11.8 1.2 %copy-done.5 = f32[64,16,256]{2,1,0:T(8,128)S(1)} copy-done((f32[64,16,256]{2,1,0:T(8,128)S(1)}, f32[64,16,256]{2,1,0:T(8,128)}, u32[]{:S(2)}) %copy-start.5) | copy-done | bytes 1048600
  13.0 0.9 %copy-done.15 = bf16[256,256]{1,0:T(8,128)(2,1)S(1)} copy-done((bf16[256,256]{1,0:T(8,128)(2,1)S(1)}, bf16[256,256]{1,0:T(8,128)(2,1)}, u32[]{:S(2)}) %copy-start.15) | copy-done | bytes 131096
  13.9 0.9 %copy-done.17 = bf16[256,256]{1,0:T(8,128)(2,1)S(1)} copy-done((bf16[256,256]{1,0:T(8,128)(2,1)S(1)}, bf16[256,256]{1,0:T(8,128)(2,1)}, u32[]{:S(2)}) %copy-start.17) | copy-done | bytes 131096
  14.8 0.0 copy-start.13
  14.8 8.5 %project_old.1 = (f32[16,256]{1,0:T(8,128)S(1)}, f32[16,256]{1,0:T(8,128)S(1)}, f32[16,64,256]{2,1,0:T(8,128)S(1)}, bf16[16,64,256]{2,1,0:T(8,128)(2,1)S(1)}, bf...) custom-call(s32[1]{0:T(128)S(6)} %copy.29.refs_0_, ...), custom_call_target="tpu_custom_call" | custom-call | flops 6442450944 | bytes 1048576 | tf_op jit(solution)/shard_map/project_old/pallas_call | solution.py:380
  23.3 0.0 copy-start.20
  23.3 1.0 %copy-done.20 = f32[16,64,256]{2,1,0:T(8,128)} copy-done((f32[16,64,256]{2,1,0:T(8,128)}, f32[16,64,256]{2,1,0:T(8,128)S(1)}, u32[]{:S(2)}) %copy-start.20) | copy-done | bytes 1048600
  24.3 0.7 %copy-done.22 = f32[3,256,128]{2,1,0:T(8,128)} copy-done((f32[3,256,128]{2,1,0:T(8,128)}, f32[3,256,128]{2,1,0:T(8,128)S(1)}, u32[]{:S(2)}) %copy-start.22) | copy-done | bytes 393240
  25.0 0.8 %copy-done.24 = f32[3,256,128]{2,1,0:T(8,128)} copy-done((f32[3,256,128]{2,1,0:T(8,128)}, f32[3,256,128]{2,1,0:T(8,128)S(1)}, u32[]{:S(2)}) %copy-start.24) | copy-done | bytes 393240
  25.8 0.7 copy-done.26
  26.5 0.7 copy-done.28
  27.2 0.6 copy-done.9
  27.9 3.5 %gradient.1 = bf16[8,16,256]{2,1,0:T(8,128)(2,1)} custom-call(s32[1,4]{1,0:T(1,128)S(1)} %copy-done.9, f32[128,256]{1,0:T(8,128)S(1)} %bitcast.7, f32[4,128,128]{2,1,0:T(8,128)S(1)} %bitcast.16, f32[128,128]{1,0:T(8,128)S(1)} %copy-done.7, f32[128,128]{1,0:T(8,128)S(1)} %copy-done.8, bf16[2,256,256]{2,1,0:T(8,128)(2,1)S(1)} %copy-done.13, ...), custom_call_target="tpu_custom_call" | custom-call | flops 4294967296 | bytes 1048576 | tf_op jit(solution)/shard_map/gradient/pallas_call | solution.py:380
  31.3 6.1 %all-to-all-start.1 = ((bf16[8,16,256]{2,1,0:T(8,128)(2,1)}), bf16[8,16,256]{2,1,0:T(8,128)(2,1)S(1)}, u32[]{:S(2)}, u32[]{:S(2)}) async-start(bf16[8,16,256]{2,1,0:T(8,128)(2,1)} %gradient.1), calls=%async_computation.1 | async-start | bytes 131072 | tf_op jit(solution)/shard_map/all_to_all | solution.py:468
  37.5 3.9 %collective-permute-start.2 = (bf16[128,256]{1,0:T(8,128)(2,1)S(1)}, bf16[128,256]{1,0:T(8,128)(2,1)S(1)}, u32[]{:S(2)}, u32[]{:S(2)}) collective-permute-start(bf16[128,256]{1,0:T(8,128)(2,1)S(1)} %get-tuple-element.40), channel_id=1, source_target_pairs={{0,1},{1,2},{2,3},{3,4},{4,5},{5,6},{6,7},{8,9},{9,10},{10,11},{11... | collective-permute-start | bytes 196616 | tf_op jit(solution)/shard_map/ppermute | solution.py:470
  41.4 1.5 %collective-permute-start.3 = (bf16[128,256]{1,0:T(8,128)(2,1)S(1)}, bf16[128,256]{1,0:T(8,128)(2,1)S(1)}, u32[]{:S(2)}, u32[]{:S(2)}) collective-permute-start(bf16[128,256]{1,0:T(8,128)(2,1)S(1)} %get-tuple-element.41), channel_id=1, source_target_pairs={{1,0},{2,1},{3,2},{4,3},{5,4},{6,5},{7,6},{9,8},{10,9},{11,10},{12... | collective-permute-start | bytes 196616 | tf_op jit(solution)/shard_map/ppermute | solution.py:471
  42.9 0.6 collective-permute-start.4
  43.5 3.2 %collective-permute-done.4.refs_1_ = f32[16,256]{1,0:T(8,128)S(1)} collective-permute-done((f32[16,256]{1,0:T(8,128)S(1)}, f32[16,256]{1,0:T(8,128)S(1)}, u32[]{:S(2)}, u32[]{:S(2)}) %collective-permute-start.4) | collective-permute-done | bytes 16416 | tf_op jit(solution)/shard_map/ppermute | solution.py:425
  46.7 0.2 line_step.1
  46.9 0.0 copy-start.11
  46.9 0.0 collective-permute-done.2.refs_2_
  46.9 0.6 collective-permute-done.3.refs_3_
  47.5 0.6 phase_step.1
  48.2 0.5 collective-permute-start.5
  48.7 3.2 %collective-permute-done.5.refs_1_ = f32[16,256]{1,0:T(8,128)S(1)} collective-permute-done((f32[16,256]{1,0:T(8,128)S(1)}, f32[16,256]{1,0:T(8,128)S(1)}, u32[]{:S(2)}, u32[]{:S(2)}) %collective-permute-start.5) | collective-permute-done | bytes 16416 | tf_op jit(solution)/shard_map/ppermute | solution.py:422
  52.0 1.0 %copy-done.25 = f32[3,256,128]{2,1,0:T(8,128)S(1)} copy-done((f32[3,256,128]{2,1,0:T(8,128)S(1)}, f32[3,256,128]{2,1,0:T(8,128)}, u32[]{:S(2)}) %copy-start.25) | copy-done | bytes 393240
  52.9 0.9 %copy-done.27 = f32[2,128,256]{2,1,0:T(8,128)S(1)} copy-done((f32[2,128,256]{2,1,0:T(8,128)S(1)}, f32[2,128,256]{2,1,0:T(8,128)}, u32[]{:S(2)}) %copy-start.27) | copy-done | bytes 262168
  53.9 0.9 %copy-done.29 = f32[2,128,256]{2,1,0:T(8,128)S(1)} copy-done((f32[2,128,256]{2,1,0:T(8,128)S(1)}, f32[2,128,256]{2,1,0:T(8,128)}, u32[]{:S(2)}) %copy-start.29) | copy-done | bytes 262168
  54.8 2.5 %backproject.3.refs_4_ = bf16[8,128,256]{2,1,0:T(8,128)(2,1)S(1)} custom-call(f32[16,256]{1,0:T(8,128)S(1)} %get-tuple-element.52.refs_0_, f32[16,256]{1,0:T(8,128)S(1)} %collective-permute-done.5.refs_1_, bf16[256,256]{1,0:T(8,128)(2,1)S(1)} %copy-done.16, bf16[256,256]{1,0:T(8,128)(2,1)S(1)} %copy-done.14, bf16[256,256]{1,0:T(8,128)(2,1)S(1)} %copy-done.19, ...), custom_call_target="tpu_custom_call" | custom-call | flops 3221225472 | bytes 1048576 | tf_op jit(solution)/shard_map/backproject/pallas_call | solution.py:380
  57.4 0.0 copy-start.18
  57.4 0.0 copy-start.21
  57.4 0.1 collective-permute-start.7
  57.5 2.5 %backproject.2.refs_4_ = bf16[8,128,256]{2,1,0:T(8,128)(2,1)S(1)} custom-call(f32[16,256]{1,0:T(8,128)S(1)} %get-tuple-element.52.refs_0_, f32[16,256]{1,0:T(8,128)S(1)} %collective-permute-done.5.refs_1_, bf16[256,256]{1,0:T(8,128)(2,1)S(1)} %copy-done.16, bf16[256,256]{1,0:T(8,128)(2,1)S(1)} %copy-done.14, bf16[256,256]{1,0:T(8,128)(2,1)S(1)} %copy-done.19, ...), custom_call_target="tpu_custom_call" | custom-call | flops 3221225472 | bytes 1048576 | tf_op jit(solution)/shard_map/backproject/pallas_call | solution.py:380
  60.0 0.6 collective-permute-start.6
  60.6 3.1 %project_new.2 = (f32[64,16,256]{2,1,0:T(8,128)}, f32[16,256]{1,0:T(8,128)S(1)}, f32[16,256]{1,0:T(8,128)S(1)}) custom-call(f32[16,64,256]{2,1,0:T(8,128)S(1)} %copy-done.21, bf16[16,64,256]{2,1,0:T(8,128)(2,1)S(1)} %get-tuple-element.49.refs_1_, bf16[128,256]{1,0:T(8,128)(2,1)S(1)} %collective-permute-done.2.refs_2_, ...), custom_call_target="tpu_custom_call" | custom-call | flops 3221225472 | bytes 1048576 | tf_op jit(solution)/shard_map/project_new/pallas_call | solution.py:380
  63.7 0.0 copy-start.4
  63.7 3.3 %project_new.3 = (f32[64,16,256]{2,1,0:T(8,128)}, f32[16,256]{1,0:T(8,128)S(1)}, f32[16,256]{1,0:T(8,128)S(1)}) custom-call(f32[16,64,256]{2,1,0:T(8,128)S(1)} %copy-done.21, bf16[16,64,256]{2,1,0:T(8,128)(2,1)S(1)} %get-tuple-element.49.refs_1_, ...), custom_call_target="tpu_custom_call", output_to_operand_aliasing={{0}: (16, {}), {1}: (17, {}), {2}: (18, {})} | custom-call | flops 3221225472 | bytes 1048576 | tf_op jit(solution)/shard_map/project_new/pallas_call | solution.py:380
  67.0 0.5 collective-permute-start.8
  67.6 3.2 %collective-permute-done.8.refs_1_ = f32[16,256]{1,0:T(8,128)S(1)} collective-permute-done((f32[16,256]{1,0:T(8,128)S(1)}, f32[16,256]{1,0:T(8,128)S(1)}, u32[]{:S(2)}, u32[]{:S(2)}) %collective-permute-start.8) | collective-permute-done | bytes 16416 | tf_op jit(solution)/shard_map/ppermute | solution.py:425
  70.8 0.8 %dual_step.1 = f32[16,256]{1,0:T(8,128)} custom-call(f32[16,256]{1,0:T(8,128)S(1)} %copy-done.4, f32[16,256]{1,0:T(8,128)S(1)} %bitcast.11, bf16[2,256,256]{2,1,0:T(8,128)(2,1)S(1)} %copy-done, f32[16,256]{1,0:T(8,128)S(1)} %get-tuple-element.63.refs_0_, f32[16,256]{1,0:T(8,128)S(1)} %collective-permute-done.8.refs_1_), custom_call_target="tpu_custom_call" | custom-call | bytes 1048576 | tf_op jit(solution)/shard_map/dual_step/pallas_call | solution.py:380
  (44 shorter events, 0.1 us)
Async XLA Ops:
  0.6 11.1 %copy-start.10 = (bf16[4,256,128]{2,1,0:T(8,128)(2,1)S(1)}, bf16[4,256,128]{2,1,0:T(8,128)(2,1)}, u32[]{:S(2)}) copy-start(bf16[4,256,128]{2,1,0:T(8,128)(2,1)} %constant.22.clone.refs_8_) | copy-start | bytes 786436
  0.6 11.1 %collective-permute-start.1 = (f32[1024,256]{1,0:T(8,128)}, f32[1024,256]{1,0:T(8,128)S(1)}, u32[]{:S(2)}, u32[]{:S(2)}) collective-permute-start(f32[1024,256]{1,0:T(8,128)} %bitcast.13), channel_id=1, source_target_pairs={{0,8},{8,0},{16,24},{24,16},{1,9},{9,1},{17,25},{25,17},{2,10},{10... | collective-permute-start | bytes 3145736 | tf_op jit(solution)/shard_map/ppermute | solution.py:419
  1.2 10.6 %collective-permute-start = (s32[1]{0:T(128)}, s32[1]{0:T(128)}, u32[]{:S(2)}, u32[]{:S(2)}) collective-permute-start(s32[1]{0:T(128)} %param.27), channel_id=1, source_target_pairs={{16,0},{24,8},{0,16},{8,24},{17,1},{25,9},{1,17},{9,25},{18,2},{26... | collective-permute-start | bytes 20 | tf_op jit(solution)/shard_map/ppermute | solution.py:422
  5.1 6.7 %copy-start.14 = (bf16[256,256]{1,0:T(8,128)(2,1)S(1)}, bf16[256,256]{1,0:T(8,128)(2,1)}, u32[]{:S(2)}) copy-start(bf16[256,256]{1,0:T(8,128)(2,1)} %constant.21.clone.refs_7_.refs_3_) | copy-start | bytes 393220
  5.1 22.1 %all-to-all-start = ((f32[8,16,256]{2,1,0:T(8,128)}), f32[8,16,256]{2,1,0:T(8,128)S(1)}, u32[]{:S(2)}, u32[]{:S(2)}) async-start(f32[8,16,256]{2,1,0:T(8,128)} %broadcast_in_dim.14), calls=%async_computation | async-start | bytes 262144 | tf_op jit(solution)/shard_map/all_to_all | solution.py:433
  11.8 1.2 %copy-start.5 = (f32[64,16,256]{2,1,0:T(8,128)S(1)}, f32[64,16,256]{2,1,0:T(8,128)}, u32[]{:S(2)}) copy-start(f32[64,16,256]{2,1,0:T(8,128)} %param.20) | copy-start | bytes 3145732
  13.0 0.9 %copy-start.15 = (bf16[256,256]{1,0:T(8,128)(2,1)S(1)}, bf16[256,256]{1,0:T(8,128)(2,1)}, u32[]{:S(2)}) copy-start(bf16[256,256]{1,0:T(8,128)(2,1)} %constant.20.clone.refs_6_.refs_2_) | copy-start | bytes 393220
  13.9 0.9 %copy-start.17 = (bf16[256,256]{1,0:T(8,128)(2,1)S(1)}, bf16[256,256]{1,0:T(8,128)(2,1)}, u32[]{:S(2)}) copy-start(bf16[256,256]{1,0:T(8,128)(2,1)} %constant.23.clone.refs_9_) | copy-start | bytes 393220
  14.8 12.4 %copy-start.6 = (f32[1,4,128,128]{3,2,1,0:T(8,128)S(1)}, f32[1,4,128,128]{3,2,1,0:T(8,128)}, u32[]{:S(2)}) copy-start(f32[1,4,128,128]{3,2,1,0:T(8,128)} %param.25) | copy-start | bytes 786436
  14.8 12.4 %copy-start.7 = (f32[128,128]{1,0:T(8,128)S(1)}, f32[128,128]{1,0:T(8,128)}, u32[]{:S(2)}) copy-start(f32[128,128]{1,0:T(8,128)} %probe_r_ref.1) | copy-start | bytes 196612
  14.8 12.4 %copy-start.8 = (f32[128,128]{1,0:T(8,128)S(1)}, f32[128,128]{1,0:T(8,128)}, u32[]{:S(2)}) copy-start(f32[128,128]{1,0:T(8,128)} %probe_i_ref.1) | copy-start | bytes 196612
  14.8 12.4 %copy-start.12 = (bf16[2,256,256]{2,1,0:T(8,128)(2,1)S(1)}, bf16[2,256,256]{2,1,0:T(8,128)(2,1)}, u32[]{:S(2)}) copy-start(bf16[2,256,256]{2,1,0:T(8,128)(2,1)} %constant.25.clone.left_ref.right_conj_ref) | copy-start | bytes 786436
  14.8 12.4 %copy-start.13 = (bf16[2,256,256]{2,1,0:T(8,128)(2,1)S(1)}, bf16[2,256,256]{2,1,0:T(8,128)(2,1)}, u32[]{:S(2)}) copy-start(bf16[2,256,256]{2,1,0:T(8,128)(2,1)} %constant.24.clone.right_ref.left_conj_ref) | copy-start | bytes 786436
  23.3 1.0 %copy-start.20 = (f32[16,64,256]{2,1,0:T(8,128)}, f32[16,64,256]{2,1,0:T(8,128)S(1)}, u32[]{:S(2)}) copy-start(f32[16,64,256]{2,1,0:T(8,128)S(1)} %get-tuple-element.48.refs_0_) | copy-start | bytes 3145732
  24.3 0.7 %copy-start.22 = (f32[3,256,128]{2,1,0:T(8,128)}, f32[3,256,128]{2,1,0:T(8,128)S(1)}, u32[]{:S(2)}) copy-start(f32[3,256,128]{2,1,0:T(8,128)S(1)} %get-tuple-element.53.refs_6_.refs_10_) | copy-start | bytes 1179652
  25.0 0.8 %copy-start.24 = (f32[3,256,128]{2,1,0:T(8,128)}, f32[3,256,128]{2,1,0:T(8,128)S(1)}, u32[]{:S(2)}) copy-start(f32[3,256,128]{2,1,0:T(8,128)S(1)} %get-tuple-element.56.refs_9_.refs_13_) | copy-start | bytes 1179652
  25.8 0.7 copy-start.26
  26.5 0.7 copy-start.28
  27.2 0.7 copy-start.9
  27.9 18.8 %copy-start = (bf16[2,256,256]{2,1,0:T(8,128)(2,1)S(1)}, bf16[2,256,256]{2,1,0:T(8,128)(2,1)}, u32[]{:S(2)}) copy-start(bf16[2,256,256]{2,1,0:T(8,128)(2,1)} %constant.26.clone.inverse_ref) | copy-start | bytes 786436
  27.9 18.8 %copy-start.2 = (f32[1,16,256]{2,1,0:T(8,128)S(1)}, f32[1,16,256]{2,1,0:T(8,128)}, u32[]{:S(2)}) copy-start(f32[1,16,256]{2,1,0:T(8,128)} %param.21) | copy-start | bytes 49156
  27.9 18.8 %copy-start.3 = (f32[1,16,256]{2,1,0:T(8,128)S(1)}, f32[1,16,256]{2,1,0:T(8,128)}, u32[]{:S(2)}) copy-start(f32[1,16,256]{2,1,0:T(8,128)} %param.22) | copy-start | bytes 49156
  27.9 24.1 %copy-start.23 = (f32[3,256,128]{2,1,0:T(8,128)S(1)}, f32[3,256,128]{2,1,0:T(8,128)}, u32[]{:S(2)}) copy-start(f32[3,256,128]{2,1,0:T(8,128)} %copy-done.22) | copy-start | bytes 1179652
  31.3 16.2 %copy-start.1 = (bf16[2,256,256]{2,1,0:T(8,128)(2,1)S(1)}, bf16[2,256,256]{2,1,0:T(8,128)(2,1)}, u32[]{:S(2)}) copy-start(bf16[2,256,256]{2,1,0:T(8,128)(2,1)} %constant.27.clone.forward_ref) | copy-start | bytes 786436
  31.3 20.6 %copy-start.16 = (bf16[256,256]{1,0:T(8,128)(2,1)S(1)}, bf16[256,256]{1,0:T(8,128)(2,1)}, u32[]{:S(2)}) copy-start(bf16[256,256]{1,0:T(8,128)(2,1)} %constant.20.clone.refs_6_.refs_2_) | copy-start | bytes 393220
  31.3 20.6 %copy-start.19 = (bf16[256,256]{1,0:T(8,128)(2,1)S(1)}, bf16[256,256]{1,0:T(8,128)(2,1)}, u32[]{:S(2)}) copy-start(bf16[256,256]{1,0:T(8,128)(2,1)} %constant.28.clone.refs_4_) | copy-start | bytes 393220
  31.3 16.2 %all-to-all-start.1 = ((bf16[8,16,256]{2,1,0:T(8,128)(2,1)}), bf16[8,16,256]{2,1,0:T(8,128)(2,1)S(1)}, u32[]{:S(2)}, u32[]{:S(2)}) async-start(bf16[8,16,256]{2,1,0:T(8,128)(2,1)} %gradient.1), calls=%async_computation.1 | async-start | bytes 131072 | tf_op jit(solution)/shard_map/all_to_all | solution.py:468
  37.5 9.4 %collective-permute-start.2 = (bf16[128,256]{1,0:T(8,128)(2,1)S(1)}, bf16[128,256]{1,0:T(8,128)(2,1)S(1)}, u32[]{:S(2)}, u32[]{:S(2)}) collective-permute-start(bf16[128,256]{1,0:T(8,128)(2,1)S(1)} %get-tuple-element.40), channel_id=1, source_target_pairs={{0,1},{1,2},{2,3},{3,4},{4,5},{5,6},{6,7},{8,9},{9,10},{10,11},{11... | collective-permute-start | bytes 196616 | tf_op jit(solution)/shard_map/ppermute | solution.py:470
  41.4 6.2 %collective-permute-start.3 = (bf16[128,256]{1,0:T(8,128)(2,1)S(1)}, bf16[128,256]{1,0:T(8,128)(2,1)S(1)}, u32[]{:S(2)}, u32[]{:S(2)}) collective-permute-start(bf16[128,256]{1,0:T(8,128)(2,1)S(1)} %get-tuple-element.41), channel_id=1, source_target_pairs={{1,0},{2,1},{3,2},{4,3},{5,4},{6,5},{7,6},{9,8},{10,9},{11,10},{12... | collective-permute-start | bytes 196616 | tf_op jit(solution)/shard_map/ppermute | solution.py:471
  42.9 3.8 %collective-permute-start.4 = (f32[16,256]{1,0:T(8,128)S(1)}, f32[16,256]{1,0:T(8,128)S(1)}, u32[]{:S(2)}, u32[]{:S(2)}) collective-permute-start(f32[16,256]{1,0:T(8,128)S(1)} %get-tuple-element.44), channel_id=1, source_target_pairs={{0,16},{8,24},{16,0},{24,8},{1,17},{9,25},{17,1},{25,9},{2,18},{10... | collective-permute-start | bytes 49160 | tf_op jit(solution)/shard_map/ppermute | solution.py:425
  46.9 5.1 %copy-start.11 = (bf16[4,128,256]{2,1,0:T(8,128)(2,1)S(1)}, bf16[4,128,256]{2,1,0:T(8,128)(2,1)}, u32[]{:S(2)}) copy-start(bf16[4,128,256]{2,1,0:T(8,128)(2,1)} %constant.29.clone.refs_5_) | copy-start | bytes 786436
  48.2 3.7 %collective-permute-start.5 = (f32[16,256]{1,0:T(8,128)S(1)}, f32[16,256]{1,0:T(8,128)S(1)}, u32[]{:S(2)}, u32[]{:S(2)}) collective-permute-start(f32[16,256]{1,0:T(8,128)S(1)} %get-tuple-element.52.refs_0_), channel_id=1, source_target_pairs={{16,0},{24,8},{0,16},{8,24},{17,1},{25,9},{1,17},{9,25},{18,2},{26... | collective-permute-start | bytes 49160 | tf_op jit(solution)/shard_map/ppermute | solution.py:422
  51.9 1.0 %copy-start.25 = (f32[3,256,128]{2,1,0:T(8,128)S(1)}, f32[3,256,128]{2,1,0:T(8,128)}, u32[]{:S(2)}) copy-start(f32[3,256,128]{2,1,0:T(8,128)} %copy-done.24) | copy-start | bytes 1179652
  52.9 0.9 %copy-start.27 = (f32[2,128,256]{2,1,0:T(8,128)S(1)}, f32[2,128,256]{2,1,0:T(8,128)}, u32[]{:S(2)}) copy-start(f32[2,128,256]{2,1,0:T(8,128)} %copy-done.26) | copy-start | bytes 786436
  53.9 0.9 %copy-start.29 = (f32[2,128,256]{2,1,0:T(8,128)S(1)}, f32[2,128,256]{2,1,0:T(8,128)}, u32[]{:S(2)}) copy-start(f32[2,128,256]{2,1,0:T(8,128)} %copy-done.28) | copy-start | bytes 786436
  57.4 3.2 %copy-start.18 = (bf16[256,256]{1,0:T(8,128)(2,1)S(1)}, bf16[256,256]{1,0:T(8,128)(2,1)}, u32[]{:S(2)}) copy-start(bf16[256,256]{1,0:T(8,128)(2,1)} %constant.23.clone.refs_9_) | copy-start | bytes 393220
  57.4 3.2 %copy-start.21 = (f32[16,64,256]{2,1,0:T(8,128)S(1)}, f32[16,64,256]{2,1,0:T(8,128)}, u32[]{:S(2)}) copy-start(f32[16,64,256]{2,1,0:T(8,128)} %copy-done.20) | copy-start | bytes 3145732
  57.4 3.2 %collective-permute-start.7 = (bf16[8,128,256]{2,1,0:T(8,128)(2,1)S(1)}, bf16[8,128,256]{2,1,0:T(8,128)(2,1)S(1)}, u32[]{:S(2)}, u32[]{:S(2)}) collective-permute-start(bf16[8,128,256]{2,1,0:T(8,128)(2,1)S(1)} %backproject.3.refs_4_), channel_id=1, source_target_pairs={{0,8},{8,0},{16,24},{24,16},{1,9},{9,1},{17,25},{25,17},{2,10},{10... | collective-permute-start | bytes 1572872 | tf_op jit(solution)/shard_map/ppermute | solution.py:419
  60.0 3.7 %collective-permute-start.6 = (bf16[8,128,256]{2,1,0:T(8,128)(2,1)S(1)}, bf16[8,128,256]{2,1,0:T(8,128)(2,1)S(1)}, u32[]{:S(2)}, u32[]{:S(2)}) collective-permute-start(bf16[8,128,256]{2,1,0:T(8,128)(2,1)S(1)} %backproject.2.refs_4_), channel_id=1, source_target_pairs={{0,8},{8,0},{16,24},{24,16},{1,9},{9,1},{17,25},{25,17},{2,10},{10... | collective-permute-start | bytes 1572872 | tf_op jit(solution)/shard_map/ppermute | solution.py:419
  63.7 7.1 %copy-start.4 = (f32[16,256]{1,0:T(8,128)S(1)}, f32[16,256]{1,0:T(8,128)}, u32[]{:S(2)}) copy-start(f32[16,256]{1,0:T(8,128)} %get-tuple-element.47.phase_ref) | copy-start | bytes 49156
  67.0 3.7 %collective-permute-start.8 = (f32[16,256]{1,0:T(8,128)S(1)}, f32[16,256]{1,0:T(8,128)S(1)}, u32[]{:S(2)}, u32[]{:S(2)}) collective-permute-start(f32[16,256]{1,0:T(8,128)S(1)} %get-tuple-element.64), channel_id=1, source_target_pairs={{0,16},{8,24},{16,0},{24,8},{1,17},{9,25},{17,1},{25,9},{2,18},{10... | collective-permute-start | bytes 49160 | tf_op jit(solution)/shard_map/ppermute | solution.py:425

commit v2 on v1

--- a/solution.py
+++ b/solution.py
@@ -19,7 +19,7 @@
 BF16 = jnp.bfloat16
 VMEM_SPEC = pl.BlockSpec(memory_space=pltpu.VMEM)
 SMEM_SPEC = pl.BlockSpec(memory_space=pltpu.SMEM)
-VMEM_LIMIT = 40 * 1024 * 1024
+MIB = 1024 * 1024
 
 
 def table_pair(length):
@@ -376,7 +376,7 @@
     dual_new_ref[...] = dual_ref[...] + rho_weight * (phase_ref[...] - proj_new)
 
 
-def call(kernel, outs, args, specs=None, out_specs=None, scratch=(), flops=0, name=None, grid=(), aliases=None):
+def call(kernel, outs, args, specs=None, out_specs=None, scratch=(), flops=0, name=None, grid=(), aliases=None, vmem=4):
     return pl.pallas_call(
         kernel,
         grid=grid,
@@ -387,7 +387,7 @@
         input_output_aliases=aliases or {},
         cost_estimate=pl.CostEstimate(flops=flops, bytes_accessed=1 << 20, transcendentals=0),
         name=name,
-        compiler_params=pltpu.CompilerParams(vmem_limit_bytes=VMEM_LIMIT),
+        compiler_params=pltpu.CompilerParams(vmem_limit_bytes=vmem * MIB),
     )(*args)
 
 
@@ -450,6 +450,7 @@
         [SMEM_SPEC] * groups + [lanes(0), lanes(1)] * 2 + [VMEM_SPEC] * 4,
         grid=(1,),
         flops=3 * work,
+        vmem=28,
         name="project_old",
     )
     lines, bases, edges, tables = take(outs, groups, 2, 2, 3 * groups)
@@ -462,9 +463,10 @@
         [offsets, image, intensity[0], probe_real, probe_imag, right, left, left_conj, right_conj],
         [SMEM_SPEC] + [VMEM_SPEC] * 8,
         flops=2 * work,
+        vmem=12,
         name="gradient",
     )
-    grad, edges = lax.optimization_barrier((grad, edges))
+    grad, edges, old = lax.optimization_barrier((grad, edges, old))
     grad = lax.all_to_all(grad, "tile", split_axis=0, concat_axis=0, tiled=True)
 
     before = lax.ppermute(edges[0], "tile", [(i, i + 1) for i in range(tiles - 1)])
@@ -489,6 +491,7 @@
             [pl.BlockSpec((some, length), lambda _, h=h: (h, 0))] * groups + [VMEM_SPEC] * (4 + 3 * groups),
             grid=(1,),
             flops=3 * work // parts,
+            vmem=24,
             name="backproject",
         )
         halves.append((mine, swap(mine)))
@@ -507,6 +510,7 @@
             scratch=[pltpu.VMEM((share * some, half), F32)] * 2,
             grid=(1,),
             flops=3 * work // parts,
+            vmem=24,
             aliases={len(args) + i: i for i in range(len(results))},
             name="project_new",
         )

time: 72.2 us -> 72.2 us (level)
  starting transfers between devices: 22.9 us -> 24.6 us
  waiting for transfers between devices: 10.2 us -> 9.05 us
    ppermute x2, waiting for transfers between devices: 6.39 us -> 2.3 us  [to_peer(): lax.ppermute(value, 'ang', [(i, (i + 2 * j) % ang) for i in range(ang)])]
    ppermute x1, waiting for transfers between devices: 0.64 us -> 4.27 us  [shards(): lax.ppermute(edges[1], 'tile', [(i + 1, i) for i in range(tiles - 1)])]
    ppermute x2, waiting for transfers between devices: 3.2 us -> 2.3 us  [from_peer(): lax.ppermute(value, 'ang', [((i + 2 * j) % ang, i) for i in range(ang)])]
    ppermute x2, starting transfers between devices: 3.11 us -> 4.01 us  [from_peer(): lax.ppermute(value, 'ang', [((i + 2 * j) % ang, i) for i in range(ang)])]
    ppermute x2, starting transfers between devices: 1.16 us -> 1.98 us  [to_peer(): lax.ppermute(value, 'ang', [(i, (i + 2 * j) % ang) for i in range(ang)])]
  transfers between devices with their start and end apart: 11 -> 11, of which waited for: 4 -> 4; matrix products, arithmetic and copies ran while one was open for 2% -> 2% of each run, Pallas kernels for 20% -> 25%
where the time goes in v2:
time: 72.2 us; the launch traced here: 71.6 us
  Pallas kernels  25 us (35%)
  starting transfers between devices  24.6 us (34%)
  local copies, waits for them, and re-layouts  11.4 us (16%)
  waiting for transfers between devices  9.05 us (13%)
  between operations  1.53 us (2%)
    pallas_call x9, Pallas kernels, call(): pl.pallas_call(kernel, grid=grid, out_shape=tuple(outs), in_specs=specs o...  25 us
    unnamed x60, local copies, waits for them, and re-layouts  9.98 us
    all_to_all x1, starting transfers between devices, shards(): grad = lax.all_to_all(grad, 'tile', split_axis=0, concat_axis=0, tiled=True)  6.14 us
    all_to_all x1, starting transfers between devices, shards(): lax.all_to_all(jnp.broadcast_to(phase, (tiles, slices, length)), 'tile',...  5.97 us
    ppermute x1, waiting for transfers between devices, shards(): lax.ppermute(edges[1], 'tile', [(i + 1, i) for i in range(tiles - 1)])  4.27 us
    ppermute x2, starting transfers between devices, from_peer(): lax.ppermute(value, 'ang', [((i + 2 * j) % ang, i) for i in range(ang)])  4.01 us
    ppermute x1, starting transfers between devices, shards(): lax.ppermute(edges[0], 'tile', [(i, i + 1) for i in range(tiles - 1)])  3.92 us
    ppermute x2, waiting for transfers between devices, to_peer(): lax.ppermute(value, 'ang', [(i, (i + 2 * j) % ang) for i in range(ang)])  2.3 us
  transfers between devices with their start and end apart: 11, of which 4 were waited for; matrix products, arithmetic and copies ran while one was open for 2% of the time, Pallas kernels for 25%

profile of v2, /device:TPU:0, one launch (start us, length us, event | category | flops | bytes accessed | tf_op | source)
XLA Modules:
  0.0 71.6 jit_solution(10042750552607777969)
XLA Ops:
  0.6 0.0 copy-start.10
  0.6 0.5 collective-permute-start.1
  1.2 2.6 %collective-permute-start = (s32[1]{0:T(128)}, s32[1]{0:T(128)}, u32[]{:S(2)}, u32[]{:S(2)}) collective-permute-start(s32[1]{0:T(128)} %param.27), channel_id=1, source_target_pairs={{16,0},{24,8},{0,16},{8,24},{17,1},{25,9},{1,17},{9,25},{18,2},{26... | collective-permute-start | bytes 20 | tf_op jit(solution)/shard_map/ppermute | solution.py:422
  3.7 1.4 %broadcast_in_dim.14 = f32[8,16,256]{2,1,0:T(8,128)} broadcast(f32[16,256]{1,0:T(8,128)} %bitcast.8), dimensions={1,2} | broadcast | bytes 147456 | tf_op jit(solution)/shard_map/broadcast_in_dim | solution.py:434
  5.1 6.0 %all-to-all-start = ((f32[8,16,256]{2,1,0:T(8,128)}), f32[8,16,256]{2,1,0:T(8,128)S(1)}, u32[]{:S(2)}, u32[]{:S(2)}) async-start(f32[8,16,256]{2,1,0:T(8,128)} %broadcast_in_dim.14), calls=%async_computation | async-start | bytes 262144 | tf_op jit(solution)/shard_map/all_to_all | solution.py:433
  11.7 0.0 collective-permute-done.refs_1_
  11.7 0.0 collective-permute-done.1.refs_4_.refs_5_
  11.8 0.0 copy-start.5
  11.8 1.2 %copy-done.5 = f32[64,16,256]{2,1,0:T(8,128)S(1)} copy-done((f32[64,16,256]{2,1,0:T(8,128)S(1)}, f32[64,16,256]{2,1,0:T(8,128)}, u32[]{:S(2)}) %copy-start.5) | copy-done | bytes 1048600
  13.0 0.9 %copy-done.15 = bf16[256,256]{1,0:T(8,128)(2,1)S(1)} copy-done((bf16[256,256]{1,0:T(8,128)(2,1)S(1)}, bf16[256,256]{1,0:T(8,128)(2,1)}, u32[]{:S(2)}) %copy-start.15) | copy-done | bytes 131096
  13.9 0.9 %copy-done.17 = bf16[256,256]{1,0:T(8,128)(2,1)S(1)} copy-done((bf16[256,256]{1,0:T(8,128)(2,1)S(1)}, bf16[256,256]{1,0:T(8,128)(2,1)}, u32[]{:S(2)}) %copy-start.17) | copy-done | bytes 131096
  14.8 0.0 copy-start.13
  14.8 8.5 %project_old.1 = (f32[16,256]{1,0:T(8,128)S(1)}, f32[16,256]{1,0:T(8,128)S(1)}, f32[16,64,256]{2,1,0:T(8,128)S(1)}, bf16[16,64,256]{2,1,0:T(8,128)(2,1)S(1)}, bf...) custom-call(s32[1]{0:T(128)S(6)} %copy.29.refs_0_, ...), custom_call_target="tpu_custom_call" | custom-call | flops 6442450944 | bytes 1048576 | tf_op jit(solution)/shard_map/project_old/pallas_call | solution.py:380
  23.3 0.0 copy-start.20
  23.3 1.0 %copy-done.20 = f32[16,64,256]{2,1,0:T(8,128)} copy-done((f32[16,64,256]{2,1,0:T(8,128)}, f32[16,64,256]{2,1,0:T(8,128)S(1)}, u32[]{:S(2)}) %copy-start.20) | copy-done | bytes 1048600
  24.3 0.7 %copy-done.22 = f32[3,256,128]{2,1,0:T(8,128)} copy-done((f32[3,256,128]{2,1,0:T(8,128)}, f32[3,256,128]{2,1,0:T(8,128)S(1)}, u32[]{:S(2)}) %copy-start.22) | copy-done | bytes 393240
  25.0 0.8 %copy-done.24 = f32[3,256,128]{2,1,0:T(8,128)} copy-done((f32[3,256,128]{2,1,0:T(8,128)}, f32[3,256,128]{2,1,0:T(8,128)S(1)}, u32[]{:S(2)}) %copy-start.24) | copy-done | bytes 393240
  25.8 0.7 copy-done.26
  26.5 0.7 copy-done.28
  27.2 0.5 collective-permute-start.2
  27.8 0.1 copy-done.9
  27.9 3.5 %gradient.1 = bf16[8,16,256]{2,1,0:T(8,128)(2,1)} custom-call(s32[1,4]{1,0:T(1,128)S(1)} %copy-done.9, f32[128,256]{1,0:T(8,128)S(1)} %bitcast.7, f32[4,128,128]{2,1,0:T(8,128)S(1)} %bitcast.16, f32[128,128]{1,0:T(8,128)S(1)} %copy-done.7, f32[128,128]{1,0:T(8,128)S(1)} %copy-done.8, bf16[2,256,256]{2,1,0:T(8,128)(2,1)S(1)} %copy-done.13, ...), custom_call_target="tpu_custom_call" | custom-call | flops 4294967296 | bytes 1048576 | tf_op jit(solution)/shard_map/gradient/pallas_call | solution.py:380
  31.3 6.1 %all-to-all-start.1 = ((bf16[8,16,256]{2,1,0:T(8,128)(2,1)}), bf16[8,16,256]{2,1,0:T(8,128)(2,1)S(1)}, u32[]{:S(2)}, u32[]{:S(2)}) async-start(bf16[8,16,256]{2,1,0:T(8,128)(2,1)} %gradient.1), calls=%async_computation.1 | async-start | bytes 131072 | tf_op jit(solution)/shard_map/all_to_all | solution.py:470
  37.5 3.9 %collective-permute-start.3 = (bf16[128,256]{1,0:T(8,128)(2,1)S(1)}, bf16[128,256]{1,0:T(8,128)(2,1)S(1)}, u32[]{:S(2)}, u32[]{:S(2)}) collective-permute-start(bf16[128,256]{1,0:T(8,128)(2,1)S(1)} %get-tuple-element.44), channel_id=1, source_target_pairs={{0,1},{1,2},{2,3},{3,4},{4,5},{5,6},{6,7},{8,9},{9,10},{10,11},{11... | collective-permute-start | bytes 196616 | tf_op jit(solution)/shard_map/ppermute | solution.py:472
  41.4 1.5 %collective-permute-start.4 = (bf16[128,256]{1,0:T(8,128)(2,1)S(1)}, bf16[128,256]{1,0:T(8,128)(2,1)S(1)}, u32[]{:S(2)}, u32[]{:S(2)}) collective-permute-start(bf16[128,256]{1,0:T(8,128)(2,1)S(1)} %get-tuple-element.45), channel_id=1, source_target_pairs={{1,0},{2,1},{3,2},{4,3},{5,4},{6,5},{7,6},{9,8},{10,9},{11,10},{12... | collective-permute-start | bytes 196616 | tf_op jit(solution)/shard_map/ppermute | solution.py:473
  42.9 0.2 line_step.1
  43.1 0.0 copy-start.11
  43.1 0.2 collective-permute-done.3.refs_2_
  43.3 4.3 %collective-permute-done.4.refs_3_ = bf16[128,256]{1,0:T(8,128)(2,1)S(1)} collective-permute-done((bf16[128,256]{1,0:T(8,128)(2,1)S(1)}, bf16[128,256]{1,0:T(8,128)(2,1)S(1)}, u32[]{:S(2)}, u32[]{:S(2)}) %collective-permute-start.4) | collective-permute-done | bytes 65568 | tf_op jit(solution)/shard_map/ppermute | solution.py:473
  47.6 0.6 phase_step.1
  48.2 1.4 %collective-permute-start.5 = (f32[16,256]{1,0:T(8,128)S(1)}, f32[16,256]{1,0:T(8,128)S(1)}, u32[]{:S(2)}, u32[]{:S(2)}) collective-permute-start(f32[16,256]{1,0:T(8,128)S(1)} %get-tuple-element.56.refs_0_), channel_id=1, source_target_pairs={{16,0},{24,8},{0,16},{8,24},{17,1},{25,9},{1,17},{9,25},{18,2},{26... | collective-permute-start | bytes 49160 | tf_op jit(solution)/shard_map/ppermute | solution.py:422
  49.6 2.3 %collective-permute-done.5.refs_1_ = f32[16,256]{1,0:T(8,128)S(1)} collective-permute-done((f32[16,256]{1,0:T(8,128)S(1)}, f32[16,256]{1,0:T(8,128)S(1)}, u32[]{:S(2)}, u32[]{:S(2)}) %collective-permute-start.5) | collective-permute-done | bytes 16416 | tf_op jit(solution)/shard_map/ppermute | solution.py:422
  52.0 1.0 %copy-done.25 = f32[3,256,128]{2,1,0:T(8,128)S(1)} copy-done((f32[3,256,128]{2,1,0:T(8,128)S(1)}, f32[3,256,128]{2,1,0:T(8,128)}, u32[]{:S(2)}) %copy-start.25) | copy-done | bytes 393240
  53.0 0.9 %copy-done.27 = f32[2,128,256]{2,1,0:T(8,128)S(1)} copy-done((f32[2,128,256]{2,1,0:T(8,128)S(1)}, f32[2,128,256]{2,1,0:T(8,128)}, u32[]{:S(2)}) %copy-start.27) | copy-done | bytes 262168
  53.9 0.9 %copy-done.29 = f32[2,128,256]{2,1,0:T(8,128)S(1)} copy-done((f32[2,128,256]{2,1,0:T(8,128)S(1)}, f32[2,128,256]{2,1,0:T(8,128)}, u32[]{:S(2)}) %copy-start.29) | copy-done | bytes 262168
  54.9 2.5 %backproject.3.refs_4_ = bf16[8,128,256]{2,1,0:T(8,128)(2,1)S(1)} custom-call(f32[16,256]{1,0:T(8,128)S(1)} %get-tuple-element.56.refs_0_, f32[16,256]{1,0:T(8,128)S(1)} %collective-permute-done.5.refs_1_, bf16[256,256]{1,0:T(8,128)(2,1)S(1)} %copy-done.16, bf16[256,256]{1,0:T(8,128)(2,1)S(1)} %copy-done.14, bf16[256,256]{1,0:T(8,128)(2,1)S(1)} %copy-done.19, ...), custom_call_target="tpu_custom_call" | custom-call | flops 3221225472 | bytes 1048576 | tf_op jit(solution)/shard_map/backproject/pallas_call | solution.py:380
  57.4 0.0 copy-start.18
  57.4 0.0 copy-start.21
  57.4 0.1 collective-permute-start.7
  57.5 2.5 %backproject.2.refs_4_ = bf16[8,128,256]{2,1,0:T(8,128)(2,1)S(1)} custom-call(f32[16,256]{1,0:T(8,128)S(1)} %get-tuple-element.56.refs_0_, f32[16,256]{1,0:T(8,128)S(1)} %collective-permute-done.5.refs_1_, bf16[256,256]{1,0:T(8,128)(2,1)S(1)} %copy-done.16, bf16[256,256]{1,0:T(8,128)(2,1)S(1)} %copy-done.14, bf16[256,256]{1,0:T(8,128)(2,1)S(1)} %copy-done.19, ...), custom_call_target="tpu_custom_call" | custom-call | flops 3221225472 | bytes 1048576 | tf_op jit(solution)/shard_map/backproject/pallas_call | solution.py:380
  60.0 0.6 collective-permute-start.6
  60.6 0.0 collective-permute-done.7.refs_5_
  60.6 3.1 %project_new.2 = (f32[64,16,256]{2,1,0:T(8,128)}, f32[16,256]{1,0:T(8,128)S(1)}, f32[16,256]{1,0:T(8,128)S(1)}) custom-call(f32[16,64,256]{2,1,0:T(8,128)S(1)} %copy-done.21, bf16[16,64,256]{2,1,0:T(8,128)(2,1)S(1)} %get-tuple-element.53.refs_1_, bf16[128,256]{1,0:T(8,128)(2,1)S(1)} %collective-permute-done.3.refs_2_, ...), custom_call_target="tpu_custom_call" | custom-call | flops 3221225472 | bytes 1048576 | tf_op jit(solution)/shard_map/project_new/pallas_call | solution.py:380
  63.7 0.0 copy-start.4
  63.7 3.3 %project_new.3 = (f32[64,16,256]{2,1,0:T(8,128)}, f32[16,256]{1,0:T(8,128)S(1)}, f32[16,256]{1,0:T(8,128)S(1)}) custom-call(f32[16,64,256]{2,1,0:T(8,128)S(1)} %copy-done.21, bf16[16,64,256]{2,1,0:T(8,128)(2,1)S(1)} %get-tuple-element.53.refs_1_, ...), custom_call_target="tpu_custom_call", output_to_operand_aliasing={{0}: (16, {}), {1}: (17, {}), {2}: (18, {})} | custom-call | flops 3221225472 | bytes 1048576 | tf_op jit(solution)/shard_map/project_new/pallas_call | solution.py:380
  67.0 1.4 %collective-permute-start.8 = (f32[16,256]{1,0:T(8,128)S(1)}, f32[16,256]{1,0:T(8,128)S(1)}, u32[]{:S(2)}, u32[]{:S(2)}) collective-permute-start(f32[16,256]{1,0:T(8,128)S(1)} %get-tuple-element.68), channel_id=1, source_target_pairs={{0,16},{8,24},{16,0},{24,8},{1,17},{9,25},{17,1},{25,9},{2,18},{10... | collective-permute-start | bytes 49160 | tf_op jit(solution)/shard_map/ppermute | solution.py:425
  68.5 2.3 %collective-permute-done.8.refs_1_ = f32[16,256]{1,0:T(8,128)S(1)} collective-permute-done((f32[16,256]{1,0:T(8,128)S(1)}, f32[16,256]{1,0:T(8,128)S(1)}, u32[]{:S(2)}, u32[]{:S(2)}) %collective-permute-start.8) | collective-permute-done | bytes 16416 | tf_op jit(solution)/shard_map/ppermute | solution.py:425
  70.8 0.8 %dual_step.1 = f32[16,256]{1,0:T(8,128)} custom-call(f32[16,256]{1,0:T(8,128)S(1)} %copy-done.4, f32[16,256]{1,0:T(8,128)S(1)} %bitcast.11, bf16[2,256,256]{2,1,0:T(8,128)(2,1)S(1)} %copy-done, f32[16,256]{1,0:T(8,128)S(1)} %get-tuple-element.67.refs_0_, f32[16,256]{1,0:T(8,128)S(1)} %collective-permute-done.8.refs_1_), custom_call_target="tpu_custom_call" | custom-call | bytes 1048576 | tf_op jit(solution)/shard_map/dual_step/pallas_call | solution.py:380
  (44 shorter events, 0.1 us)
Async XLA Ops:
  0.6 11.1 %copy-start.10 = (bf16[4,256,128]{2,1,0:T(8,128)(2,1)S(1)}, bf16[4,256,128]{2,1,0:T(8,128)(2,1)}, u32[]{:S(2)}) copy-start(bf16[4,256,128]{2,1,0:T(8,128)(2,1)} %constant.22.clone.refs_8_) | copy-start | bytes 786436
  0.6 11.1 %collective-permute-start.1 = (f32[1024,256]{1,0:T(8,128)}, f32[1024,256]{1,0:T(8,128)S(1)}, u32[]{:S(2)}, u32[]{:S(2)}) collective-permute-start(f32[1024,256]{1,0:T(8,128)} %bitcast.13), channel_id=1, source_target_pairs={{0,8},{8,0},{16,24},{24,16},{1,9},{9,1},{17,25},{25,17},{2,10},{10... | collective-permute-start | bytes 3145736 | tf_op jit(solution)/shard_map/ppermute | solution.py:419
  1.2 10.6 %collective-permute-start = (s32[1]{0:T(128)}, s32[1]{0:T(128)}, u32[]{:S(2)}, u32[]{:S(2)}) collective-permute-start(s32[1]{0:T(128)} %param.27), channel_id=1, source_target_pairs={{16,0},{24,8},{0,16},{8,24},{17,1},{25,9},{1,17},{9,25},{18,2},{26... | collective-permute-start | bytes 20 | tf_op jit(solution)/shard_map/ppermute | solution.py:422
  5.1 6.7 %copy-start.14 = (bf16[256,256]{1,0:T(8,128)(2,1)S(1)}, bf16[256,256]{1,0:T(8,128)(2,1)}, u32[]{:S(2)}) copy-start(bf16[256,256]{1,0:T(8,128)(2,1)} %constant.21.clone.refs_7_.refs_3_) | copy-start | bytes 393220
  5.1 22.1 %all-to-all-start = ((f32[8,16,256]{2,1,0:T(8,128)}), f32[8,16,256]{2,1,0:T(8,128)S(1)}, u32[]{:S(2)}, u32[]{:S(2)}) async-start(f32[8,16,256]{2,1,0:T(8,128)} %broadcast_in_dim.14), calls=%async_computation | async-start | bytes 262144 | tf_op jit(solution)/shard_map/all_to_all | solution.py:433
  11.8 1.2 %copy-start.5 = (f32[64,16,256]{2,1,0:T(8,128)S(1)}, f32[64,16,256]{2,1,0:T(8,128)}, u32[]{:S(2)}) copy-start(f32[64,16,256]{2,1,0:T(8,128)} %param.20) | copy-start | bytes 3145732
  13.0 0.9 %copy-start.15 = (bf16[256,256]{1,0:T(8,128)(2,1)S(1)}, bf16[256,256]{1,0:T(8,128)(2,1)}, u32[]{:S(2)}) copy-start(bf16[256,256]{1,0:T(8,128)(2,1)} %constant.20.clone.refs_6_.refs_2_) | copy-start | bytes 393220
  13.9 0.9 %copy-start.17 = (bf16[256,256]{1,0:T(8,128)(2,1)S(1)}, bf16[256,256]{1,0:T(8,128)(2,1)}, u32[]{:S(2)}) copy-start(bf16[256,256]{1,0:T(8,128)(2,1)} %constant.23.clone.refs_9_) | copy-start | bytes 393220
  14.8 12.9 %copy-start.6 = (f32[1,4,128,128]{3,2,1,0:T(8,128)S(1)}, f32[1,4,128,128]{3,2,1,0:T(8,128)}, u32[]{:S(2)}) copy-start(f32[1,4,128,128]{3,2,1,0:T(8,128)} %param.25) | copy-start | bytes 786436
  14.8 12.9 %copy-start.7 = (f32[128,128]{1,0:T(8,128)S(1)}, f32[128,128]{1,0:T(8,128)}, u32[]{:S(2)}) copy-start(f32[128,128]{1,0:T(8,128)} %probe_r_ref.1) | copy-start | bytes 196612
  14.8 12.9 %copy-start.8 = (f32[128,128]{1,0:T(8,128)S(1)}, f32[128,128]{1,0:T(8,128)}, u32[]{:S(2)}) copy-start(f32[128,128]{1,0:T(8,128)} %probe_i_ref.1) | copy-start | bytes 196612
  14.8 12.9 %copy-start.12 = (bf16[2,256,256]{2,1,0:T(8,128)(2,1)S(1)}, bf16[2,256,256]{2,1,0:T(8,128)(2,1)}, u32[]{:S(2)}) copy-start(bf16[2,256,256]{2,1,0:T(8,128)(2,1)} %constant.25.clone.left_ref.right_conj_ref) | copy-start | bytes 786436
  14.8 12.9 %copy-start.13 = (bf16[2,256,256]{2,1,0:T(8,128)(2,1)S(1)}, bf16[2,256,256]{2,1,0:T(8,128)(2,1)}, u32[]{:S(2)}) copy-start(bf16[2,256,256]{2,1,0:T(8,128)(2,1)} %constant.24.clone.right_ref.left_conj_ref) | copy-start | bytes 786436
  23.3 1.0 %copy-start.20 = (f32[16,64,256]{2,1,0:T(8,128)}, f32[16,64,256]{2,1,0:T(8,128)S(1)}, u32[]{:S(2)}) copy-start(f32[16,64,256]{2,1,0:T(8,128)S(1)} %get-tuple-element.52.refs_0_) | copy-start | bytes 3145732
  24.3 0.7 %copy-start.22 = (f32[3,256,128]{2,1,0:T(8,128)}, f32[3,256,128]{2,1,0:T(8,128)S(1)}, u32[]{:S(2)}) copy-start(f32[3,256,128]{2,1,0:T(8,128)S(1)} %get-tuple-element.57.refs_6_.refs_10_) | copy-start | bytes 1179652
  25.0 0.8 %copy-start.24 = (f32[3,256,128]{2,1,0:T(8,128)}, f32[3,256,128]{2,1,0:T(8,128)S(1)}, u32[]{:S(2)}) copy-start(f32[3,256,128]{2,1,0:T(8,128)S(1)} %get-tuple-element.60.refs_9_.refs_13_) | copy-start | bytes 1179652
  25.8 0.7 copy-start.26
  26.5 0.7 copy-start.28
  27.2 0.7 copy-start.9
  27.2 4.1 %collective-permute-start.2 = (f32[16,256]{1,0:T(8,128)S(1)}, f32[16,256]{1,0:T(8,128)S(1)}, u32[]{:S(2)}, u32[]{:S(2)}) collective-permute-start(f32[16,256]{1,0:T(8,128)S(1)} %get-tuple-element.42), channel_id=1, source_target_pairs={{0,16},{8,24},{16,0},{24,8},{1,17},{9,25},{17,1},{25,9},{2,18},{10... | collective-permute-start | bytes 49160 | tf_op jit(solution)/shard_map/ppermute | solution.py:425
  27.9 15.0 %copy-start = (bf16[2,256,256]{2,1,0:T(8,128)(2,1)S(1)}, bf16[2,256,256]{2,1,0:T(8,128)(2,1)}, u32[]{:S(2)}) copy-start(bf16[2,256,256]{2,1,0:T(8,128)(2,1)} %constant.26.clone.inverse_ref) | copy-start | bytes 786436
  27.9 15.0 %copy-start.2 = (f32[1,16,256]{2,1,0:T(8,128)S(1)}, f32[1,16,256]{2,1,0:T(8,128)}, u32[]{:S(2)}) copy-start(f32[1,16,256]{2,1,0:T(8,128)} %param.21) | copy-start | bytes 49156
  27.9 15.0 %copy-start.3 = (f32[1,16,256]{2,1,0:T(8,128)S(1)}, f32[1,16,256]{2,1,0:T(8,128)}, u32[]{:S(2)}) copy-start(f32[1,16,256]{2,1,0:T(8,128)} %param.22) | copy-start | bytes 49156
  27.9 24.1 %copy-start.23 = (f32[3,256,128]{2,1,0:T(8,128)S(1)}, f32[3,256,128]{2,1,0:T(8,128)}, u32[]{:S(2)}) copy-start(f32[3,256,128]{2,1,0:T(8,128)} %copy-done.22) | copy-start | bytes 1179652
  31.3 16.2 %copy-start.1 = (bf16[2,256,256]{2,1,0:T(8,128)(2,1)S(1)}, bf16[2,256,256]{2,1,0:T(8,128)(2,1)}, u32[]{:S(2)}) copy-start(bf16[2,256,256]{2,1,0:T(8,128)(2,1)} %constant.27.clone.forward_ref) | copy-start | bytes 786436
  31.3 20.6 %copy-start.16 = (bf16[256,256]{1,0:T(8,128)(2,1)S(1)}, bf16[256,256]{1,0:T(8,128)(2,1)}, u32[]{:S(2)}) copy-start(bf16[256,256]{1,0:T(8,128)(2,1)} %constant.20.clone.refs_6_.refs_2_) | copy-start | bytes 393220
  31.3 20.6 %copy-start.19 = (bf16[256,256]{1,0:T(8,128)(2,1)S(1)}, bf16[256,256]{1,0:T(8,128)(2,1)}, u32[]{:S(2)}) copy-start(bf16[256,256]{1,0:T(8,128)(2,1)} %constant.28.clone.refs_4_) | copy-start | bytes 393220
  31.3 16.2 %all-to-all-start.1 = ((bf16[8,16,256]{2,1,0:T(8,128)(2,1)}), bf16[8,16,256]{2,1,0:T(8,128)(2,1)S(1)}, u32[]{:S(2)}, u32[]{:S(2)}) async-start(bf16[8,16,256]{2,1,0:T(8,128)(2,1)} %gradient.1), calls=%async_computation.1 | async-start | bytes 131072 | tf_op jit(solution)/shard_map/all_to_all | solution.py:470
  37.5 5.8 %collective-permute-start.3 = (bf16[128,256]{1,0:T(8,128)(2,1)S(1)}, bf16[128,256]{1,0:T(8,128)(2,1)S(1)}, u32[]{:S(2)}, u32[]{:S(2)}) collective-permute-start(bf16[128,256]{1,0:T(8,128)(2,1)S(1)} %get-tuple-element.44), channel_id=1, source_target_pairs={{0,1},{1,2},{2,3},{3,4},{4,5},{5,6},{6,7},{8,9},{9,10},{10,11},{11... | collective-permute-start | bytes 196616 | tf_op jit(solution)/shard_map/ppermute | solution.py:472
  41.4 6.2 %collective-permute-start.4 = (bf16[128,256]{1,0:T(8,128)(2,1)S(1)}, bf16[128,256]{1,0:T(8,128)(2,1)S(1)}, u32[]{:S(2)}, u32[]{:S(2)}) collective-permute-start(bf16[128,256]{1,0:T(8,128)(2,1)S(1)} %get-tuple-element.45), channel_id=1, source_target_pairs={{1,0},{2,1},{3,2},{4,3},{5,4},{6,5},{7,6},{9,8},{10,9},{11,10},{12... | collective-permute-start | bytes 196616 | tf_op jit(solution)/shard_map/ppermute | solution.py:473
  43.1 8.9 %copy-start.11 = (bf16[4,128,256]{2,1,0:T(8,128)(2,1)S(1)}, bf16[4,128,256]{2,1,0:T(8,128)(2,1)}, u32[]{:S(2)}) copy-start(bf16[4,128,256]{2,1,0:T(8,128)(2,1)} %constant.29.clone.refs_5_) | copy-start | bytes 786436
  48.2 3.7 %collective-permute-start.5 = (f32[16,256]{1,0:T(8,128)S(1)}, f32[16,256]{1,0:T(8,128)S(1)}, u32[]{:S(2)}, u32[]{:S(2)}) collective-permute-start(f32[16,256]{1,0:T(8,128)S(1)} %get-tuple-element.56.refs_0_), channel_id=1, source_target_pairs={{16,0},{24,8},{0,16},{8,24},{17,1},{25,9},{1,17},{9,25},{18,2},{26... | collective-permute-start | bytes 49160 | tf_op jit(solution)/shard_map/ppermute | solution.py:422
  52.0 1.0 %copy-start.25 = (f32[3,256,128]{2,1,0:T(8,128)S(1)}, f32[3,256,128]{2,1,0:T(8,128)}, u32[]{:S(2)}) copy-start(f32[3,256,128]{2,1,0:T(8,128)} %copy-done.24) | copy-start | bytes 1179652
  53.0 0.9 %copy-start.27 = (f32[2,128,256]{2,1,0:T(8,128)S(1)}, f32[2,128,256]{2,1,0:T(8,128)}, u32[]{:S(2)}) copy-start(f32[2,128,256]{2,1,0:T(8,128)} %copy-done.26) | copy-start | bytes 786436
  53.9 0.9 %copy-start.29 = (f32[2,128,256]{2,1,0:T(8,128)S(1)}, f32[2,128,256]{2,1,0:T(8,128)}, u32[]{:S(2)}) copy-start(f32[2,128,256]{2,1,0:T(8,128)} %copy-done.28) | copy-start | bytes 786436
  57.4 3.2 %copy-start.18 = (bf16[256,256]{1,0:T(8,128)(2,1)S(1)}, bf16[256,256]{1,0:T(8,128)(2,1)}, u32[]{:S(2)}) copy-start(bf16[256,256]{1,0:T(8,128)(2,1)} %constant.23.clone.refs_9_) | copy-start | bytes 393220
  57.4 3.2 %copy-start.21 = (f32[16,64,256]{2,1,0:T(8,128)S(1)}, f32[16,64,256]{2,1,0:T(8,128)}, u32[]{:S(2)}) copy-start(f32[16,64,256]{2,1,0:T(8,128)} %copy-done.20) | copy-start | bytes 3145732
  57.4 3.2 %collective-permute-start.7 = (bf16[8,128,256]{2,1,0:T(8,128)(2,1)S(1)}, bf16[8,128,256]{2,1,0:T(8,128)(2,1)S(1)}, u32[]{:S(2)}, u32[]{:S(2)}) collective-permute-start(bf16[8,128,256]{2,1,0:T(8,128)(2,1)S(1)} %backproject.3.refs_4_), channel_id=1, source_target_pairs={{0,8},{8,0},{16,24},{24,16},{1,9},{9,1},{17,25},{25,17},{2,10},{10... | collective-permute-start | bytes 1572872 | tf_op jit(solution)/shard_map/ppermute | solution.py:419
  60.0 3.7 %collective-permute-start.6 = (bf16[8,128,256]{2,1,0:T(8,128)(2,1)S(1)}, bf16[8,128,256]{2,1,0:T(8,128)(2,1)S(1)}, u32[]{:S(2)}, u32[]{:S(2)}) collective-permute-start(bf16[8,128,256]{2,1,0:T(8,128)(2,1)S(1)} %backproject.2.refs_4_), channel_id=1, source_target_pairs={{0,8},{8,0},{16,24},{24,16},{1,9},{9,1},{17,25},{25,17},{2,10},{10... | collective-permute-start | bytes 1572872 | tf_op jit(solution)/shard_map/ppermute | solution.py:419
  63.7 7.1 %copy-start.4 = (f32[16,256]{1,0:T(8,128)S(1)}, f32[16,256]{1,0:T(8,128)}, u32[]{:S(2)}) copy-start(f32[16,256]{1,0:T(8,128)} %get-tuple-element.51.phase_ref) | copy-start | bytes 49156
  67.0 3.7 %collective-permute-start.8 = (f32[16,256]{1,0:T(8,128)S(1)}, f32[16,256]{1,0:T(8,128)S(1)}, u32[]{:S(2)}, u32[]{:S(2)}) collective-permute-start(f32[16,256]{1,0:T(8,128)S(1)} %get-tuple-element.68), channel_id=1, source_target_pairs={{0,16},{8,24},{16,0},{24,8},{1,17},{9,25},{17,1},{25,9},{2,18},{10... | collective-permute-start | bytes 49160 | tf_op jit(solution)/shard_map/ppermute | solution.py:425

commit v3 on v2

--- a/solution.py
+++ b/solution.py
@@ -208,24 +208,34 @@
     return [Tables(*refs[i : i + 3]) for i in range(0, len(refs), 3)]
 
 
-def project_kernel(groups, slices, *refs):
-    angle_refs, sides, consts, lines_refs, bases, edges, table_refs = take(
-        refs, groups, 4, 4, groups, 2, 2, 3 * groups
-    )
-    share = sides[0].shape[0] // slices
-    length = consts[0].shape[0]
+def tables_kernel(groups, *refs):
+    angle_refs, table_refs = take(refs, groups, 3 * groups)
     for g in range(groups):
-        fill_turn_tables(angle_refs[g][0], length, *table_refs[3 * g : 3 * g + 3])
+        row_ref, col_ref, nyq_ref = table_refs[3 * g : 3 * g + 3]
+        fill_turn_tables(angle_refs[g][0], row_ref.shape[1], row_ref, col_ref, nyq_ref)
+
+
+def project_kernel(groups, slices, part, parts, aliased, *refs):
+    angle_refs, sides, (const_ref, down_ref), unused, lines_refs, bases, rest = take(
+        refs, groups, 4, 2, aliased, groups, 2, len(refs)
+    )
+    edges, table_refs = take(rest, 2 if part == 0 else 0, 3 * groups)
+    some, share, length = bases[0].shape
+    tables_kernel(groups, *angle_refs, *table_refs)
 
     def rows(z):
-        parts = [ref[pl.ds(z, share, stride=slices), :] for ref in sides]
-        return [jnp.concatenate(parts[:2], axis=1), jnp.concatenate(parts[2:], axis=1)]
-
+        pieces = [ref[pl.ds(z, share, stride=slices), :] for ref in sides]
+        return [jnp.concatenate(pieces[:2], axis=1), jnp.concatenate(pieces[2:], axis=1)]
+
+    if part == 0:
+        for edge_ref, z in zip(edges, (slices - 1, 0)):
+            edge_ref[...] = jnp.concatenate(rows(z), axis=0).astype(BF16)
     slab = []
-    past = None
-    now = rows(0)
-    for z in range(slices):
-        later = rows(z + 1) if z + 1 < slices else None
+    start = part * some
+    past = rows(start - 1) if start > 0 else None
+    now = rows(start)
+    for z in range(some):
+        later = rows(start + z + 1) if start + z + 1 < slices else None
         for place in range(2):
             slab.append(now[place].astype(BF16))
             near = [side[place] for side in (past, later) if side is not None]
@@ -233,16 +243,15 @@
             base = base + (tau_step * smooth_weight) * sum(near[1:], near[0])
             bases[place][z] = base.astype(bases[place].dtype)
         past, now = now, later
-    for edge_ref, part in zip(edges, (slab[-2:], slab[:2])):
-        edge_ref[...] = jnp.concatenate(part, axis=0)
+    consts = [const_ref.at[0], const_ref.at[1], down_ref, const_ref.at[3]]
     project_slices(
-        jnp.concatenate(slab, axis=0), slices, share, as_tables(table_refs), consts, lines_refs
+        jnp.concatenate(slab, axis=0), some, share, as_tables(table_refs), consts, lines_refs
     )
 
 
 def back_kernel(groups, *refs):
-    spectra_refs, consts, table_refs, (out_ref,) = take(refs, groups, 4, 3 * groups, 1)
-    forward_ref, inverse_ref, down_ref, up_ref = consts
+    spectra_refs, (const_ref, up_ref), table_refs, (out_ref,) = take(refs, groups, 2, 3 * groups, 1)
+    forward_ref, inverse_ref, down_ref = const_ref.at[0], const_ref.at[1], const_ref.at[2]
     slices, pair, length = out_ref.shape
     half = length // 2
     here = lax.axis_index("ang")
@@ -269,9 +278,10 @@
 
 
 def update_kernel(groups, first, last, aliased, *refs):
-    bases, halos, shares, consts, table_refs, unused, (volume_ref,), lines_refs, sides = take(
-        refs, 2, 2, 2, 4, 3 * groups, aliased, 1, groups, 2
-    )
+    bases, halos, shares, (const_ref, down_ref), table_refs, unused, (volume_ref,), lines_refs, sides = take(
+        refs, 2, 2, 2, 2, 3 * groups, aliased, 1, groups, 2
+    )
+    consts = [const_ref.at[0], const_ref.at[1], down_ref, const_ref.at[3]]
     own_ref, other_ref = bases
     mine_ref, theirs_ref = shares
     slices, share, length = own_ref.shape
@@ -411,6 +421,7 @@
     ]
     down_part = np.stack([down[:, rows] for rows in owners])
     up_part = np.stack([up[rows] for rows in owners])
+    square = np.stack([forward, inverse, down, up])
     right, left, left_conj, right_conj = patch_tables(width)
     line = shape((slices, length), F32)
     work = 2 * 2 * length * length * length * slices * groups
@@ -429,6 +440,13 @@
 
     def gathered(lines):
         return [lines[0]] + [to_peer(lines[j], j) for j in range(1, groups)]
+
+    tables_shape = [
+        shape((3, length, half), F32), shape((2, half, length), F32), shape((8, length), F32)
+    ] * groups
+    block_lines = [
+        pl.BlockSpec((some, length), functools.partial(lambda h, _: (h, 0), h)) for h in range(parts)
+    ]
 
     image = lax.all_to_all(
         jnp.broadcast_to(phase, (tiles, slices, length)), "tile", split_axis=0, concat_axis=0, tiled=True
@@ -437,26 +455,31 @@
     other = swap(flat)
     angles = [angle_index] + [from_peer(angle_index, j) for j in range(1, groups)]
 
-    tables_shape = [
-        shape((3, length, half), F32), shape((2, half, length), F32), shape((8, length), F32)
-    ] * groups
-    outs = call(
-        functools.partial(project_kernel, groups, slices),
-        [line] * groups
-        + [shape((slices, share, length), F32), shape((slices, share, length), BF16)]
-        + [shape((pair, length), BF16)] * 2
-        + tables_shape,
-        angles + [flat, flat, other, other, forward, inverse, down_part, up],
-        [SMEM_SPEC] * groups + [lanes(0), lanes(1)] * 2 + [VMEM_SPEC] * 4,
-        grid=(1,),
-        flops=3 * work,
-        vmem=28,
-        name="project_old",
-    )
-    lines, bases, edges, tables = take(outs, groups, 2, 2, 3 * groups)
-    old = gathered(lines)
-
-    image, edges = lax.optimization_barrier((image, edges))
+    def project_part(h, lines, angles):
+        outs = [line] * groups + [shape((some, share, length), F32), shape((some, share, length), BF16)]
+        outs = outs + [shape((pair, length), BF16)] * (2 if h == 0 else 0)
+        extra = len(outs) - groups
+        args = angles + [flat, flat, other, other, square, down_part]
+        outs = call(
+            functools.partial(project_kernel, groups, slices, h, parts, len(lines)),
+            outs,
+            args + lines,
+            [SMEM_SPEC] * groups + [lanes(0), lanes(1)] * 2 + [VMEM_SPEC] * 2
+            + [pl.BlockSpec(memory_space=pl.ANY)] * len(lines),
+            [block_lines[h]] * groups + [VMEM_SPEC] * extra,
+            scratch=[pltpu.VMEM(t.shape, F32) for t in tables_shape],
+            grid=(1,),
+            flops=3 * work // parts,
+            vmem=24,
+            aliases={len(args) + i: i for i in range(len(lines))},
+            name="project_old",
+        )
+        return take(outs, groups, 2, 2)
+
+    bases = []
+    lines, base, edges = project_part(0, [], angles)
+    bases.append(base)
+    image, lines = lax.optimization_barrier((image, lines))
     (grad,) = call(
         gradient_kernel,
         [shape((tiles, slices, length), BF16)],
@@ -466,8 +489,12 @@
         vmem=12,
         name="gradient",
     )
-    grad, edges, old = lax.optimization_barrier((grad, edges, old))
+    grad, lines, edges = lax.optimization_barrier((grad, lines, edges))
     grad = lax.all_to_all(grad, "tile", split_axis=0, concat_axis=0, tiled=True)
+    for h in range(1, parts):
+        lines, base, _ = project_part(h, lines, angles)
+        bases.append(base)
+    old = gathered(lines)
 
     before = lax.ppermute(edges[0], "tile", [(i, i + 1) for i in range(tiles - 1)])
     after = lax.ppermute(edges[1], "tile", [(i + 1, i) for i in range(tiles - 1)])
@@ -476,10 +503,15 @@
         functools.partial(line_kernel, groups), [line, line], [phase[0], dual[0], inverse_full] + old,
         name="line_step",
     )
-    grad, before, after = lax.optimization_barrier((grad, before, after))
     phase_new, spectrum = call(
         phase_kernel, [line, line], [grad, phase_part, resid_part, forward_full], name="phase_step"
     )
+    spectrum, angles = lax.optimization_barrier((spectrum, angles))
+    tables = call(
+        functools.partial(tables_kernel, groups), tables_shape, angles, [SMEM_SPEC] * groups,
+        flops=work, name="turn_tables",
+    )
+    tables = list(tables)
     spectra = [spectrum] + [from_peer(spectrum, j) for j in range(1, groups)]
 
     halves = []
@@ -487,8 +519,8 @@
         (mine,) = call(
             functools.partial(back_kernel, groups),
             [shape((some, pair, length), BF16)],
-            spectra + [forward, inverse, down, up_part] + tables,
-            [pl.BlockSpec((some, length), lambda _, h=h: (h, 0))] * groups + [VMEM_SPEC] * (4 + 3 * groups),
+            spectra + [square, up_part] + tables,
+            [block_lines[h]] * groups + [VMEM_SPEC] * (2 + 3 * groups),
             grid=(1,),
             flops=3 * work // parts,
             vmem=24,
@@ -498,15 +530,14 @@
 
     results = []
     for h in range(parts):
-        block = pl.BlockSpec((some, share, length), lambda _, h=h: (h, 0, 0))
-        args = bases + [before, after] + list(halves[h]) + [forward, inverse, down_part, up] + tables
+        args = bases[h] + [before, after] + list(halves[h]) + [square, down_part] + tables
         results = call(
             functools.partial(update_kernel, groups, h == 0, h == parts - 1, len(results)),
             [shape((share, slices, length), F32)] + [line] * groups,
             args + list(results),
-            [block] * 2 + [VMEM_SPEC] * (8 + 3 * groups) + [pl.BlockSpec(memory_space=pl.ANY)] * len(results),
+            [VMEM_SPEC] * len(args) + [pl.BlockSpec(memory_space=pl.ANY)] * len(results),
             [pl.BlockSpec((share, some, length), lambda _, h=h: (0, h, 0))]
-            + [pl.BlockSpec((some, length), lambda _, h=h: (h, 0))] * groups,
+            + [block_lines[h]] * groups,
             scratch=[pltpu.VMEM((share * some, half), F32)] * 2,
             grid=(1,),
             flops=3 * work // parts,

time: 72.2 us -> 74.9 us (1.037)
  waiting for transfers between devices: 9.05 us -> 12.9 us
  starting transfers between devices: 24.6 us -> 22.6 us
  Pallas kernels: 25 us -> 26.9 us
  local copies, waits for them, and re-layouts: 11.4 us -> 10.2 us
    ppermute x2, waiting for transfers between devices: 2.3 us -> 6.37 us  [to_peer(): lax.ppermute(value, 'ang', [(i, (i + 2 * j) % ang) for i in range(ang)])]
    pallas_call x9 -> x11, Pallas kernels: 25 us -> 26.9 us  [call(): pl.pallas_call(kernel, grid=grid, out_shape=tuple(outs), in_specs=specs o...]
    unnamed x60 -> x54, local copies, waits for them, and re-layouts: 9.98 us -> 8.84 us
    ppermute x2, starting transfers between devices: 4.01 us -> 3.12 us  [from_peer(): lax.ppermute(value, 'ang', [((i + 2 * j) % ang, i) for i in range(ang)])]
    ppermute x2, starting transfers between devices: 1.98 us -> 1.1 us  [to_peer(): lax.ppermute(value, 'ang', [(i, (i + 2 * j) % ang) for i in range(ang)])]
  transfers between devices with their start and end apart: 11 -> 11, of which waited for: 4 -> 5; matrix products, arithmetic and copies ran while one was open for 2% -> 2% of each run, Pallas kernels for 25% -> 22%
where the time goes in v3:
time: 74.9 us; the launch traced here: 74.2 us
  Pallas kernels  26.9 us (36%)
  starting transfers between devices  22.6 us (30%)
  waiting for transfers between devices  12.9 us (17%)
  local copies, waits for them, and re-layouts  10.2 us (14%)
  between operations  1.55 us (2%)
    pallas_call x11, Pallas kernels, call(): pl.pallas_call(kernel, grid=grid, out_shape=tuple(outs), in_specs=specs o...  26.9 us
    unnamed x54, local copies, waits for them, and re-layouts  8.84 us
    ppermute x2, waiting for transfers between devices, to_peer(): lax.ppermute(value, 'ang', [(i, (i + 2 * j) % ang) for i in range(ang)])  6.37 us
    all_to_all x1, starting transfers between devices, shards(): grad = lax.all_to_all(grad, 'tile', split_axis=0, concat_axis=0, tiled=True)  6 us
    all_to_all x1, starting transfers between devices, shards(): lax.all_to_all(jnp.broadcast_to(phase, (tiles, slices, length)), 'tile',...  5.83 us
    ppermute x1, waiting for transfers between devices, shards(): lax.ppermute(edges[1], 'tile', [(i + 1, i) for i in range(tiles - 1)])  4.27 us
    ppermute x1, starting transfers between devices, shards(): lax.ppermute(edges[0], 'tile', [(i, i + 1) for i in range(tiles - 1)])  3.91 us
    ppermute x2, starting transfers between devices, from_peer(): lax.ppermute(value, 'ang', [((i + 2 * j) % ang, i) for i in range(ang)])  3.12 us
  transfers between devices with their start and end apart: 11, of which 5 were waited for; matrix products, arithmetic and copies ran while one was open for 2% of the time, Pallas kernels for 22%

profile of v3, /device:TPU:0, one launch (start us, length us, event | category | flops | bytes accessed | tf_op | source)
XLA Modules:
  0.0 74.2 jit_solution(3536102108218198696)
XLA Ops:
  0.6 0.0 copy-start.13
  0.6 0.5 collective-permute-start.1
  1.2 2.6 %collective-permute-start = (s32[1]{0:T(128)}, s32[1]{0:T(128)}, u32[]{:S(2)}, u32[]{:S(2)}) collective-permute-start(s32[1]{0:T(128)} %param.24), channel_id=1, source_target_pairs={{16,0},{24,8},{0,16},{8,24},{17,1},{25,9},{1,17},{9,25},{18,2},{26... | collective-permute-start | bytes 20 | tf_op jit(solution)/shard_map/ppermute | solution.py:433
  3.7 1.4 %broadcast_in_dim.14 = f32[8,16,256]{2,1,0:T(8,128)} broadcast(f32[16,256]{1,0:T(8,128)} %bitcast.8), dimensions={1,2} | broadcast | bytes 147456 | tf_op jit(solution)/shard_map/broadcast_in_dim | solution.py:452
  5.1 5.8 %all-to-all-start = ((f32[8,16,256]{2,1,0:T(8,128)}), f32[8,16,256]{2,1,0:T(8,128)S(1)}, u32[]{:S(2)}, u32[]{:S(2)}) async-start(f32[8,16,256]{2,1,0:T(8,128)} %broadcast_in_dim.14), calls=%async_computation | async-start | bytes 262144 | tf_op jit(solution)/shard_map/all_to_all | solution.py:451
  11.6 0.0 collective-permute-done.1.refs_4_.refs_5_
  11.6 0.0 copy-start.5
  11.6 1.2 %copy-done.5 = f32[64,16,256]{2,1,0:T(8,128)S(1)} copy-done((f32[64,16,256]{2,1,0:T(8,128)S(1)}, f32[64,16,256]{2,1,0:T(8,128)}, u32[]{:S(2)}) %copy-start.5) | copy-done | bytes 1048600
  12.8 1.0 %copy-done.11 = bf16[4,256,256]{2,1,0:T(8,128)(2,1)S(1)} copy-done((bf16[4,256,256]{2,1,0:T(8,128)(2,1)S(1)}, bf16[4,256,256]{2,1,0:T(8,128)(2,1)}, u32[]{:S(2)}) %copy-start.11) | copy-done | bytes 524312
  13.9 4.7 %project_old.2 = (f32[16,256]{1,0:T(8,128)S(1)}, f32[16,256]{1,0:T(8,128)S(1)}, f32[8,64,256]{2,1,0:T(8,128)S(1)}, bf16[8,64,256]{2,1,0:T(8,128)(2,1)S(1)}, bf16...) custom-call(s32[1]{0:T(128)S(6)} %copy.30.refs_0_, s32[1]{0:T(128)} %collective-permute-done.refs_1_, ...), custom_call_target="tpu_custom_call" | custom-call | flops 3221225472 | bytes 1048576 | tf_op jit(solution)/shard_map/project_old/pallas_call | solution.py:390
  18.6 0.0 copy-start.21
  18.6 0.8 %copy-done.21 = f32[8,64,256]{2,1,0:T(8,128)} copy-done((f32[8,64,256]{2,1,0:T(8,128)}, f32[8,64,256]{2,1,0:T(8,128)S(1)}, u32[]{:S(2)}) %copy-start.21) | copy-done | bytes 524312
  19.4 0.7 copy-done.25
  20.1 0.0 all-to-all-done
  20.2 0.6 copy-done.10
  20.8 0.9 %copy-done.17 = bf16[2,256,256]{2,1,0:T(8,128)(2,1)S(1)} copy-done((bf16[2,256,256]{2,1,0:T(8,128)(2,1)S(1)}, bf16[2,256,256]{2,1,0:T(8,128)(2,1)}, u32[]{:S(2)}) %copy-start.17) | copy-done | bytes 262168
  21.8 0.9 %copy-done.18 = bf16[2,256,256]{2,1,0:T(8,128)(2,1)S(1)} copy-done((bf16[2,256,256]{2,1,0:T(8,128)(2,1)S(1)}, bf16[2,256,256]{2,1,0:T(8,128)(2,1)}, u32[]{:S(2)}) %copy-start.18) | copy-done | bytes 262168
  22.7 3.5 %gradient.1 = bf16[8,16,256]{2,1,0:T(8,128)(2,1)} custom-call(s32[1,4]{1,0:T(1,128)S(1)} %copy-done.10, f32[128,256]{1,0:T(8,128)S(1)} %bitcast.7, f32[4,128,128]{2,1,0:T(8,128)S(1)} %bitcast.18, f32[128,128]{1,0:T(8,128)S(1)} %copy-done.8, f32[128,128]{1,0:T(8,128)S(1)} %copy-done.9, bf16[2,256,256]{2,1,0:T(8,128)(2,1)S(1)} %copy-done.17, ...), custom_call_target="tpu_custom_call" | custom-call | flops 4294967296 | bytes 1048576 | tf_op jit(solution)/shard_map/gradient/pallas_call | solution.py:390
  26.2 6.0 %all-to-all-start.1 = ((bf16[8,16,256]{2,1,0:T(8,128)(2,1)}), bf16[8,16,256]{2,1,0:T(8,128)(2,1)S(1)}, u32[]{:S(2)}, u32[]{:S(2)}) async-start(bf16[8,16,256]{2,1,0:T(8,128)(2,1)} %gradient.1), calls=%async_computation.1 | async-start | bytes 131072 | tf_op jit(solution)/shard_map/all_to_all | solution.py:493
  32.2 0.0 copy-start.14
  32.2 0.9 %copy-done.14 = bf16[4,256,128]{2,1,0:T(8,128)(2,1)S(1)} copy-done((bf16[4,256,128]{2,1,0:T(8,128)(2,1)S(1)}, bf16[4,256,128]{2,1,0:T(8,128)(2,1)}, u32[]{:S(2)}) %copy-start.14) | copy-done | bytes 262168
  33.2 4.6 %project_old.3 = (f32[16,256]{1,0:T(8,128)S(1)}, f32[16,256]{1,0:T(8,128)S(1)}, f32[8,64,256]{2,1,0:T(8,128)S(1)}, bf16[8,64,256]{2,1,0:T(8,128)(2,1)S(1)}) custom-call(s32[1]{0:T(128)S(6)} %copy.30.refs_0_, s32[1]{0:T(128)} %collective-permute-done.refs_1_, f32[1024,256]{1,0:T(8,128)S(1)} %bitcast.16, ...), custom_call_target="tpu_custom_call", output_to_operand_aliasing={{0}: (8, {}), {1}: (9, {})} | custom-call | flops 3221225472 | bytes 1048576 | tf_op jit(solution)/shard_map/project_old/pallas_call | solution.py:390
  37.8 0.8 %copy-done.19 = f32[8,64,256]{2,1,0:T(8,128)} copy-done((f32[8,64,256]{2,1,0:T(8,128)}, f32[8,64,256]{2,1,0:T(8,128)S(1)}, u32[]{:S(2)}) %copy-start.19) | copy-done | bytes 524312
  38.6 0.7 copy-done.23
  39.3 0.6 collective-permute-start.2
  39.9 3.2 %collective-permute-done.2.refs_1_ = f32[16,256]{1,0:T(8,128)S(1)} collective-permute-done((f32[16,256]{1,0:T(8,128)S(1)}, f32[16,256]{1,0:T(8,128)S(1)}, u32[]{:S(2)}, u32[]{:S(2)}) %collective-permute-start.2) | collective-permute-done | bytes 16416 | tf_op jit(solution)/shard_map/ppermute | solution.py:436
  43.1 0.2 line_step.1
  43.3 0.6 phase_step.1
  43.9 0.6 collective-permute-start.5
  44.5 1.3 %turn_tables.1 = (f32[3,256,128]{2,1,0:T(8,128)S(1)}, f32[2,128,256]{2,1,0:T(8,128)S(1)}, f32[8,256]{1,0:T(8,128)S(1)}, f32[3,256,128]{2,1,0:T(8,128)S(1)}, f32[...) custom-call(s32[1]{0:T(128)S(6)} %copy.30.refs_0_, s32[1]{0:T(128)} %collective-permute-done.refs_1_), custom_call_target="tpu_custom_call" | custom-call | flops 2147483648 | bytes 1048576 | tf_op jit(solution)/shard_map/turn_tables/pallas_call | solution.py:390
  45.8 1.9 %collective-permute-done.5.refs_1_ = f32[16,256]{1,0:T(8,128)S(1)} collective-permute-done((f32[16,256]{1,0:T(8,128)S(1)}, f32[16,256]{1,0:T(8,128)S(1)}, u32[]{:S(2)}, u32[]{:S(2)}) %collective-permute-start.5) | collective-permute-done | bytes 16416 | tf_op jit(solution)/shard_map/ppermute | solution.py:433
  47.7 2.4 %backproject.3.refs_4_ = bf16[8,128,256]{2,1,0:T(8,128)(2,1)S(1)} custom-call(f32[16,256]{1,0:T(8,128)S(1)} %get-tuple-element.60.refs_0_, f32[16,256]{1,0:T(8,128)S(1)} %collective-permute-done.5.refs_1_, bf16[4,256,256]{2,1,0:T(8,128)(2,1)S(1)} %copy-done.12, bf16[4,128,256]{2,1,0:T(8,128)(2,1)S(1)} %copy-done.16, ...), custom_call_target="tpu_custom_call" | custom-call | flops 3221225472 | bytes 1048576 | tf_op jit(solution)/shard_map/backproject/pallas_call | solution.py:390
  50.1 0.0 copy-start.15
  50.1 0.0 copy-start.22
  50.1 0.1 collective-permute-start.7
  50.2 2.4 %backproject.2.refs_4_ = bf16[8,128,256]{2,1,0:T(8,128)(2,1)S(1)} custom-call(f32[16,256]{1,0:T(8,128)S(1)} %get-tuple-element.60.refs_0_, f32[16,256]{1,0:T(8,128)S(1)} %collective-permute-done.5.refs_1_, bf16[4,256,256]{2,1,0:T(8,128)(2,1)S(1)} %copy-done.12, bf16[4,128,256]{2,1,0:T(8,128)(2,1)S(1)} %copy-done.16, ...), custom_call_target="tpu_custom_call" | custom-call | flops 3221225472 | bytes 1048576 | tf_op jit(solution)/shard_map/backproject/pallas_call | solution.py:390
  52.7 0.6 collective-permute-start.6
  53.2 3.9 %collective-permute-start.3 = (bf16[128,256]{1,0:T(8,128)(2,1)S(1)}, bf16[128,256]{1,0:T(8,128)(2,1)S(1)}, u32[]{:S(2)}, u32[]{:S(2)}) collective-permute-start(bf16[128,256]{1,0:T(8,128)(2,1)S(1)} %get-tuple-element.57), channel_id=1, source_target_pairs={{0,1},{1,2},{2,3},{3,4},{4,5},{5,6},{6,7},{8,9},{9,10},{10,11},{11... | collective-permute-start | bytes 196616 | tf_op jit(solution)/shard_map/ppermute | solution.py:499
  57.1 1.5 %collective-permute-start.4 = (bf16[128,256]{1,0:T(8,128)(2,1)S(1)}, bf16[128,256]{1,0:T(8,128)(2,1)S(1)}, u32[]{:S(2)}, u32[]{:S(2)}) collective-permute-start(bf16[128,256]{1,0:T(8,128)(2,1)S(1)} %get-tuple-element.58), channel_id=1, source_target_pairs={{1,0},{2,1},{3,2},{4,3},{5,4},{6,5},{7,6},{9,8},{10,9},{11,10},{12... | collective-permute-start | bytes 196616 | tf_op jit(solution)/shard_map/ppermute | solution.py:500
  58.7 0.4 collective-permute-done.3.refs_2_
  59.0 4.3 %collective-permute-done.4.refs_3_ = bf16[128,256]{1,0:T(8,128)(2,1)S(1)} collective-permute-done((bf16[128,256]{1,0:T(8,128)(2,1)S(1)}, bf16[128,256]{1,0:T(8,128)(2,1)S(1)}, u32[]{:S(2)}, u32[]{:S(2)}) %collective-permute-start.4) | collective-permute-done | bytes 65568 | tf_op jit(solution)/shard_map/ppermute | solution.py:500
  63.3 3.1 %project_new.2 = (f32[64,16,256]{2,1,0:T(8,128)}, f32[16,256]{1,0:T(8,128)S(1)}, f32[16,256]{1,0:T(8,128)S(1)}) custom-call(f32[8,64,256]{2,1,0:T(8,128)S(1)} %copy-done.22, bf16[8,64,256]{2,1,0:T(8,128)(2,1)S(1)} %copy-done.26, bf16[128,256]{1,0:T(8,128)(2,1)S(1)} %collective-permute-done.3.refs_2_, bf16[128,256]{1,0:T(8,128)(2,1)S(1)} %collective-permute-done.4.refs_3_, ...), custom_call_target="tpu_custom_call" | custom-call | flops 3221225472 | bytes 1048576 | tf_op jit(solution)/shard_map/project_new/pallas_call | solution.py:390
  66.4 0.0 collective-permute-done.6.refs_5_
  66.5 0.0 copy-start.4
  66.5 3.2 %project_new.3 = (f32[64,16,256]{2,1,0:T(8,128)}, f32[16,256]{1,0:T(8,128)S(1)}, f32[16,256]{1,0:T(8,128)S(1)}) custom-call(f32[8,64,256]{2,1,0:T(8,128)S(1)} %copy-done.20, bf16[8,64,256]{2,1,0:T(8,128)(2,1)S(1)} %copy-done.24, bf16[128,256]{1,0:T(8,128)(2,1)S(1)} %collective-permute-done.3.refs_2_, ...), custom_call_target="tpu_custom_call", output_to_operand_aliasing={{0}: (14, {}), {1}: (15, {}), {2}: (16, {})} | custom-call | flops 3221225472 | bytes 1048576 | tf_op jit(solution)/shard_map/project_new/pallas_call | solution.py:390
  69.7 0.5 collective-permute-start.8
  70.3 3.2 %collective-permute-done.8.refs_1_ = f32[16,256]{1,0:T(8,128)S(1)} collective-permute-done((f32[16,256]{1,0:T(8,128)S(1)}, f32[16,256]{1,0:T(8,128)S(1)}, u32[]{:S(2)}, u32[]{:S(2)}) %collective-permute-start.8) | collective-permute-done | bytes 16416 | tf_op jit(solution)/shard_map/ppermute | solution.py:436
  73.4 0.8 %dual_step.1 = f32[16,256]{1,0:T(8,128)} custom-call(f32[16,256]{1,0:T(8,128)S(1)} %copy-done.4, f32[16,256]{1,0:T(8,128)S(1)} %bitcast.11, bf16[2,256,256]{2,1,0:T(8,128)(2,1)S(1)} %copy-done, f32[16,256]{1,0:T(8,128)S(1)} %get-tuple-element.75.refs_0_, f32[16,256]{1,0:T(8,128)S(1)} %collective-permute-done.8.refs_1_), custom_call_target="tpu_custom_call" | custom-call | bytes 1048576 | tf_op jit(solution)/shard_map/dual_step/pallas_call | solution.py:390
  (40 shorter events, 0.1 us)
Async XLA Ops:
  0.6 11.0 %copy-start.13 = (bf16[4,256,128]{2,1,0:T(8,128)(2,1)S(1)}, bf16[4,256,128]{2,1,0:T(8,128)(2,1)}, u32[]{:S(2)}) copy-start(bf16[4,256,128]{2,1,0:T(8,128)(2,1)} %constant.15.clone.refs_7_) | copy-start | bytes 786436
  0.6 11.0 %collective-permute-start.1 = (f32[1024,256]{1,0:T(8,128)}, f32[1024,256]{1,0:T(8,128)S(1)}, u32[]{:S(2)}, u32[]{:S(2)}) collective-permute-start(f32[1024,256]{1,0:T(8,128)} %bitcast.13), channel_id=1, source_target_pairs={{0,8},{8,0},{16,24},{24,16},{1,9},{9,1},{17,25},{25,17},{2,10},{10... | collective-permute-start | bytes 3145736 | tf_op jit(solution)/shard_map/ppermute | solution.py:430
  1.2 10.4 %collective-permute-start = (s32[1]{0:T(128)}, s32[1]{0:T(128)}, u32[]{:S(2)}, u32[]{:S(2)}) collective-permute-start(s32[1]{0:T(128)} %param.24), channel_id=1, source_target_pairs={{16,0},{24,8},{0,16},{8,24},{17,1},{25,9},{1,17},{9,25},{18,2},{26... | collective-permute-start | bytes 20 | tf_op jit(solution)/shard_map/ppermute | solution.py:433
  5.1 15.0 %all-to-all-start = ((f32[8,16,256]{2,1,0:T(8,128)}), f32[8,16,256]{2,1,0:T(8,128)S(1)}, u32[]{:S(2)}, u32[]{:S(2)}) async-start(f32[8,16,256]{2,1,0:T(8,128)} %broadcast_in_dim.14), calls=%async_computation | async-start | bytes 262144 | tf_op jit(solution)/shard_map/all_to_all | solution.py:451
  11.6 1.2 %copy-start.5 = (f32[64,16,256]{2,1,0:T(8,128)S(1)}, f32[64,16,256]{2,1,0:T(8,128)}, u32[]{:S(2)}) copy-start(f32[64,16,256]{2,1,0:T(8,128)} %param.17) | copy-start | bytes 3145732
  12.8 1.0 %copy-start.11 = (bf16[4,256,256]{2,1,0:T(8,128)(2,1)S(1)}, bf16[4,256,256]{2,1,0:T(8,128)(2,1)}, u32[]{:S(2)}) copy-start(bf16[4,256,256]{2,1,0:T(8,128)(2,1)} %constant.14.clone.refs_6_.refs_2_) | copy-start | bytes 1572868
  13.9 6.3 %copy-start.7 = (f32[1,4,128,128]{3,2,1,0:T(8,128)S(1)}, f32[1,4,128,128]{3,2,1,0:T(8,128)}, u32[]{:S(2)}) copy-start(f32[1,4,128,128]{3,2,1,0:T(8,128)} %param.22) | copy-start | bytes 786436
  13.9 6.3 %copy-start.8 = (f32[128,128]{1,0:T(8,128)S(1)}, f32[128,128]{1,0:T(8,128)}, u32[]{:S(2)}) copy-start(f32[128,128]{1,0:T(8,128)} %probe_r_ref.1) | copy-start | bytes 196612
  13.9 6.3 %copy-start.9 = (f32[128,128]{1,0:T(8,128)S(1)}, f32[128,128]{1,0:T(8,128)}, u32[]{:S(2)}) copy-start(f32[128,128]{1,0:T(8,128)} %probe_i_ref.1) | copy-start | bytes 196612
  18.6 0.8 %copy-start.21 = (f32[8,64,256]{2,1,0:T(8,128)}, f32[8,64,256]{2,1,0:T(8,128)S(1)}, u32[]{:S(2)}) copy-start(f32[8,64,256]{2,1,0:T(8,128)S(1)} %get-tuple-element.69.refs_0_) | copy-start | bytes 1572868
  19.4 0.7 copy-start.25
  20.1 0.7 copy-start.10
  20.8 0.9 %copy-start.17 = (bf16[2,256,256]{2,1,0:T(8,128)(2,1)S(1)}, bf16[2,256,256]{2,1,0:T(8,128)(2,1)}, u32[]{:S(2)}) copy-start(bf16[2,256,256]{2,1,0:T(8,128)(2,1)} %constant.16.clone.right_ref.left_conj_ref) | copy-start | bytes 786436
  21.8 0.9 %copy-start.18 = (bf16[2,256,256]{2,1,0:T(8,128)(2,1)S(1)}, bf16[2,256,256]{2,1,0:T(8,128)(2,1)}, u32[]{:S(2)}) copy-start(bf16[2,256,256]{2,1,0:T(8,128)(2,1)} %constant.17.clone.left_ref.right_conj_ref) | copy-start | bytes 786436
  22.7 9.5 %copy-start.6 = (f32[64,16,256]{2,1,0:T(8,128)S(1)}, f32[64,16,256]{2,1,0:T(8,128)}, u32[]{:S(2)}) copy-start(f32[64,16,256]{2,1,0:T(8,128)} %param.17) | copy-start | bytes 3145732
  22.7 9.5 %copy-start.12 = (bf16[4,256,256]{2,1,0:T(8,128)(2,1)S(1)}, bf16[4,256,256]{2,1,0:T(8,128)(2,1)}, u32[]{:S(2)}) copy-start(bf16[4,256,256]{2,1,0:T(8,128)(2,1)} %constant.14.clone.refs_6_.refs_2_) | copy-start | bytes 1572868
  26.2 17.1 %all-to-all-start.1 = ((bf16[8,16,256]{2,1,0:T(8,128)(2,1)}), bf16[8,16,256]{2,1,0:T(8,128)(2,1)S(1)}, u32[]{:S(2)}, u32[]{:S(2)}) async-start(bf16[8,16,256]{2,1,0:T(8,128)(2,1)} %gradient.1), calls=%async_computation.1 | async-start | bytes 131072 | tf_op jit(solution)/shard_map/all_to_all | solution.py:493
  32.2 1.0 %copy-start.14 = (bf16[4,256,128]{2,1,0:T(8,128)(2,1)S(1)}, bf16[4,256,128]{2,1,0:T(8,128)(2,1)}, u32[]{:S(2)}) copy-start(bf16[4,256,128]{2,1,0:T(8,128)(2,1)} %constant.15.clone.refs_7_) | copy-start | bytes 786436
  33.1 9.9 %copy-start = (bf16[2,256,256]{2,1,0:T(8,128)(2,1)S(1)}, bf16[2,256,256]{2,1,0:T(8,128)(2,1)}, u32[]{:S(2)}) copy-start(bf16[2,256,256]{2,1,0:T(8,128)(2,1)} %constant.18.clone.inverse_ref) | copy-start | bytes 786436
  33.1 9.9 %copy-start.2 = (f32[1,16,256]{2,1,0:T(8,128)S(1)}, f32[1,16,256]{2,1,0:T(8,128)}, u32[]{:S(2)}) copy-start(f32[1,16,256]{2,1,0:T(8,128)} %param.18) | copy-start | bytes 49156
  33.1 9.9 %copy-start.3 = (f32[1,16,256]{2,1,0:T(8,128)S(1)}, f32[1,16,256]{2,1,0:T(8,128)}, u32[]{:S(2)}) copy-start(f32[1,16,256]{2,1,0:T(8,128)} %param.19) | copy-start | bytes 49156
  37.8 0.8 %copy-start.19 = (f32[8,64,256]{2,1,0:T(8,128)}, f32[8,64,256]{2,1,0:T(8,128)S(1)}, u32[]{:S(2)}) copy-start(f32[8,64,256]{2,1,0:T(8,128)S(1)} %get-tuple-element.55.refs_0_) | copy-start | bytes 1572868
  38.6 0.7 copy-start.23
  39.3 4.0 %copy-start.1 = (bf16[2,256,256]{2,1,0:T(8,128)(2,1)S(1)}, bf16[2,256,256]{2,1,0:T(8,128)(2,1)}, u32[]{:S(2)}) copy-start(bf16[2,256,256]{2,1,0:T(8,128)(2,1)} %constant.19.clone.forward_ref) | copy-start | bytes 786436
  39.3 3.7 %collective-permute-start.2 = (f32[16,256]{1,0:T(8,128)S(1)}, f32[16,256]{1,0:T(8,128)S(1)}, u32[]{:S(2)}, u32[]{:S(2)}) collective-permute-start(f32[16,256]{1,0:T(8,128)S(1)} %get-tuple-element.51), channel_id=1, source_target_pairs={{0,16},{8,24},{16,0},{24,8},{1,17},{9,25},{17,1},{25,9},{2,18},{10... | collective-permute-start | bytes 49160 | tf_op jit(solution)/shard_map/ppermute | solution.py:436
  43.9 3.7 %copy-start.16 = (bf16[4,128,256]{2,1,0:T(8,128)(2,1)S(1)}, bf16[4,128,256]{2,1,0:T(8,128)(2,1)}, u32[]{:S(2)}) copy-start(bf16[4,128,256]{2,1,0:T(8,128)(2,1)} %constant.20.clone.refs_3_) | copy-start | bytes 786436
  43.9 3.7 %collective-permute-start.5 = (f32[16,256]{1,0:T(8,128)S(1)}, f32[16,256]{1,0:T(8,128)S(1)}, u32[]{:S(2)}, u32[]{:S(2)}) collective-permute-start(f32[16,256]{1,0:T(8,128)S(1)} %get-tuple-element.60.refs_0_), channel_id=1, source_target_pairs={{16,0},{24,8},{0,16},{8,24},{17,1},{25,9},{1,17},{9,25},{18,2},{26... | collective-permute-start | bytes 49160 | tf_op jit(solution)/shard_map/ppermute | solution.py:433
  50.1 13.2 %copy-start.15 = (bf16[4,256,128]{2,1,0:T(8,128)(2,1)S(1)}, bf16[4,256,128]{2,1,0:T(8,128)(2,1)}, u32[]{:S(2)}) copy-start(bf16[4,256,128]{2,1,0:T(8,128)(2,1)} %constant.15.clone.refs_7_) | copy-start | bytes 786436
  50.1 13.2 %copy-start.22 = (f32[8,64,256]{2,1,0:T(8,128)S(1)}, f32[8,64,256]{2,1,0:T(8,128)}, u32[]{:S(2)}) copy-start(f32[8,64,256]{2,1,0:T(8,128)} %copy-done.21) | copy-start | bytes 1572868
  50.1 13.2 %copy-start.26 = (bf16[8,64,256]{2,1,0:T(8,128)(2,1)S(1)}, bf16[8,64,256]{2,1,0:T(8,128)(2,1)}, u32[]{:S(2)}) copy-start(bf16[8,64,256]{2,1,0:T(8,128)(2,1)} %copy-done.25) | copy-start | bytes 786436
  50.1 13.2 %collective-permute-start.7 = (bf16[8,128,256]{2,1,0:T(8,128)(2,1)S(1)}, bf16[8,128,256]{2,1,0:T(8,128)(2,1)S(1)}, u32[]{:S(2)}, u32[]{:S(2)}) collective-permute-start(bf16[8,128,256]{2,1,0:T(8,128)(2,1)S(1)} %backproject.3.refs_4_), channel_id=1, source_target_pairs={{0,8},{8,0},{16,24},{24,16},{1,9},{9,1},{17,25},{25,17},{2,10},{10... | collective-permute-start | bytes 1572872 | tf_op jit(solution)/shard_map/ppermute | solution.py:430
  52.7 13.8 %collective-permute-start.6 = (bf16[8,128,256]{2,1,0:T(8,128)(2,1)S(1)}, bf16[8,128,256]{2,1,0:T(8,128)(2,1)S(1)}, u32[]{:S(2)}, u32[]{:S(2)}) collective-permute-start(bf16[8,128,256]{2,1,0:T(8,128)(2,1)S(1)} %backproject.2.refs_4_), channel_id=1, source_target_pairs={{0,8},{8,0},{16,24},{24,16},{1,9},{9,1},{17,25},{25,17},{2,10},{10... | collective-permute-start | bytes 1572872 | tf_op jit(solution)/shard_map/ppermute | solution.py:430
  53.2 5.8 %collective-permute-start.3 = (bf16[128,256]{1,0:T(8,128)(2,1)S(1)}, bf16[128,256]{1,0:T(8,128)(2,1)S(1)}, u32[]{:S(2)}, u32[]{:S(2)}) collective-permute-start(bf16[128,256]{1,0:T(8,128)(2,1)S(1)} %get-tuple-element.57), channel_id=1, source_target_pairs={{0,1},{1,2},{2,3},{3,4},{4,5},{5,6},{6,7},{8,9},{9,10},{10,11},{11... | collective-permute-start | bytes 196616 | tf_op jit(solution)/shard_map/ppermute | solution.py:499
  57.1 6.2 %collective-permute-start.4 = (bf16[128,256]{1,0:T(8,128)(2,1)S(1)}, bf16[128,256]{1,0:T(8,128)(2,1)S(1)}, u32[]{:S(2)}, u32[]{:S(2)}) collective-permute-start(bf16[128,256]{1,0:T(8,128)(2,1)S(1)} %get-tuple-element.58), channel_id=1, source_target_pairs={{1,0},{2,1},{3,2},{4,3},{5,4},{6,5},{7,6},{9,8},{10,9},{11,10},{12... | collective-permute-start | bytes 196616 | tf_op jit(solution)/shard_map/ppermute | solution.py:500
  63.3 3.1 %copy-start.20 = (f32[8,64,256]{2,1,0:T(8,128)S(1)}, f32[8,64,256]{2,1,0:T(8,128)}, u32[]{:S(2)}) copy-start(f32[8,64,256]{2,1,0:T(8,128)} %copy-done.19) | copy-start | bytes 1572868
  63.3 3.1 %copy-start.24 = (bf16[8,64,256]{2,1,0:T(8,128)(2,1)S(1)}, bf16[8,64,256]{2,1,0:T(8,128)(2,1)}, u32[]{:S(2)}) copy-start(bf16[8,64,256]{2,1,0:T(8,128)(2,1)} %copy-done.23) | copy-start | bytes 786436
  66.5 7.0 %copy-start.4 = (f32[16,256]{1,0:T(8,128)S(1)}, f32[16,256]{1,0:T(8,128)}, u32[]{:S(2)}) copy-start(f32[16,256]{1,0:T(8,128)} %get-tuple-element.54.phase_ref) | copy-start | bytes 49156
  69.7 3.7 %collective-permute-start.8 = (f32[16,256]{1,0:T(8,128)S(1)}, f32[16,256]{1,0:T(8,128)S(1)}, u32[]{:S(2)}, u32[]{:S(2)}) collective-permute-start(f32[16,256]{1,0:T(8,128)S(1)} %get-tuple-element.76), channel_id=1, source_target_pairs={{0,16},{8,24},{16,0},{24,8},{1,17},{9,25},{17,1},{25,9},{2,18},{10... | collective-permute-start | bytes 49160 | tf_op jit(solution)/shard_map/ppermute | solution.py:436

commit v4 on v3

--- a/solution.py
+++ b/solution.py
@@ -56,9 +56,7 @@
     s = sin_t / np.float32(math.sqrt(width))
     right = np.block([[c, -s], [s, c]])
     left = np.block([[c, s], [-s, c]])
-    right_conj = np.block([[c, s], [-s, c]])
-    left_conj = np.block([[c, -s], [s, c]])
-    return tuple(split_pair(m.astype(np.float32)) for m in (right, left, left_conj, right_conj))
+    return split_pair(right.astype(np.float32)), split_pair(left.astype(np.float32))
 
 
 def dot(left, right):
@@ -215,27 +213,30 @@
         fill_turn_tables(angle_refs[g][0], row_ref.shape[1], row_ref, col_ref, nyq_ref)
 
 
-def project_kernel(groups, slices, part, parts, aliased, *refs):
-    angle_refs, sides, (const_ref, down_ref), unused, lines_refs, bases, rest = take(
-        refs, groups, 4, 2, aliased, groups, 2, len(refs)
-    )
-    edges, table_refs = take(rest, 2 if part == 0 else 0, 3 * groups)
-    some, share, length = bases[0].shape
+def edge_kernel(slices, *refs):
+    sides, edges = take(refs, 4, 2)
+    share = sides[0].shape[0] // slices
+    for edge_ref, z in zip(edges, (slices - 1, 0)):
+        pieces = [ref[pl.ds(z, share, stride=slices), :].astype(BF16) for ref in sides]
+        edge_ref[:share, :] = jnp.concatenate(pieces[:2], axis=1)
+        edge_ref[share:, :] = jnp.concatenate(pieces[2:], axis=1)
+
+
+def project_kernel(groups, slices, *refs):
+    angle_refs, sides, (const_ref, down_ref), lines_refs, bases, table_refs = take(
+        refs, groups, 4, 2, groups, 2, 3 * groups
+    )
+    share = sides[0].shape[0] // slices
     tables_kernel(groups, *angle_refs, *table_refs)
 
     def rows(z):
         pieces = [ref[pl.ds(z, share, stride=slices), :] for ref in sides]
         return [jnp.concatenate(pieces[:2], axis=1), jnp.concatenate(pieces[2:], axis=1)]
 
-    if part == 0:
-        for edge_ref, z in zip(edges, (slices - 1, 0)):
-            edge_ref[...] = jnp.concatenate(rows(z), axis=0).astype(BF16)
     slab = []
-    start = part * some
-    past = rows(start - 1) if start > 0 else None
-    now = rows(start)
-    for z in range(some):
-        later = rows(start + z + 1) if start + z + 1 < slices else None
+    past, now = None, rows(0)
+    for z in range(slices):
+        later = rows(z + 1) if z + 1 < slices else None
         for place in range(2):
             slab.append(now[place].astype(BF16))
             near = [side[place] for side in (past, later) if side is not None]
@@ -245,7 +246,7 @@
         past, now = now, later
     consts = [const_ref.at[0], const_ref.at[1], down_ref, const_ref.at[3]]
     project_slices(
-        jnp.concatenate(slab, axis=0), some, share, as_tables(table_refs), consts, lines_refs
+        jnp.concatenate(slab, axis=0), slices, share, as_tables(table_refs), consts, lines_refs
     )
 
 
@@ -310,8 +311,10 @@
 
 def gradient_kernel(
     offsets_ref, image_ref, measured_ref, probe_r_ref, probe_i_ref,
-    right_ref, left_ref, left_conj_ref, right_conj_ref, out_ref,
+    const_ref, out_ref,
 ):
+    right_ref, left_ref = const_ref.at[0], const_ref.at[1]
+    left_conj_ref, right_conj_ref = right_ref, left_ref
     positions, height, width = measured_ref.shape
     length = image_ref.shape[1]
     image = image_ref[...]
@@ -422,7 +425,7 @@
     down_part = np.stack([down[:, rows] for rows in owners])
     up_part = np.stack([up[rows] for rows in owners])
     square = np.stack([forward, inverse, down, up])
-    right, left, left_conj, right_conj = patch_tables(width)
+    right, left = patch_tables(width)
     line = shape((slices, length), F32)
     work = 2 * 2 * length * length * length * slices * groups
 
@@ -448,56 +451,53 @@
         pl.BlockSpec((some, length), functools.partial(lambda h, _: (h, 0), h)) for h in range(parts)
     ]
 
-    image = lax.all_to_all(
-        jnp.broadcast_to(phase, (tiles, slices, length)), "tile", split_axis=0, concat_axis=0, tiled=True
-    ).reshape(tiles * slices, length)
+    phases = jnp.broadcast_to(phase, (tiles, slices, length))
+    phases, volume = lax.optimization_barrier((phases, volume))
+    image = lax.all_to_all(phases, "tile", split_axis=0, concat_axis=0, tiled=True)
+    image = image.reshape(tiles * slices, length)
+
     flat = volume.reshape(share * slices, length)
     other = swap(flat)
+    edges = call(
+        functools.partial(edge_kernel, slices),
+        [shape((pair, length), BF16)] * 2,
+        [flat, flat, other, other],
+        [lanes(0), lanes(1)] * 2,
+        grid=(1,),
+        vmem=6,
+        name="edges",
+    )
+    before = lax.ppermute(edges[0], "tile", [(i, i + 1) for i in range(tiles - 1)])
+    after = lax.ppermute(edges[1], "tile", [(i + 1, i) for i in range(tiles - 1)])
+    angle_index, edges = lax.optimization_barrier((angle_index, edges))
     angles = [angle_index] + [from_peer(angle_index, j) for j in range(1, groups)]
-
-    def project_part(h, lines, angles):
-        outs = [line] * groups + [shape((some, share, length), F32), shape((some, share, length), BF16)]
-        outs = outs + [shape((pair, length), BF16)] * (2 if h == 0 else 0)
-        extra = len(outs) - groups
-        args = angles + [flat, flat, other, other, square, down_part]
-        outs = call(
-            functools.partial(project_kernel, groups, slices, h, parts, len(lines)),
-            outs,
-            args + lines,
-            [SMEM_SPEC] * groups + [lanes(0), lanes(1)] * 2 + [VMEM_SPEC] * 2
-            + [pl.BlockSpec(memory_space=pl.ANY)] * len(lines),
-            [block_lines[h]] * groups + [VMEM_SPEC] * extra,
-            scratch=[pltpu.VMEM(t.shape, F32) for t in tables_shape],
-            grid=(1,),
-            flops=3 * work // parts,
-            vmem=24,
-            aliases={len(args) + i: i for i in range(len(lines))},
-            name="project_old",
-        )
-        return take(outs, groups, 2, 2)
-
-    bases = []
-    lines, base, edges = project_part(0, [], angles)
-    bases.append(base)
-    image, lines = lax.optimization_barrier((image, lines))
+    image, before, after, angles = lax.optimization_barrier((image, before, after, angles))
+
     (grad,) = call(
         gradient_kernel,
         [shape((tiles, slices, length), BF16)],
-        [offsets, image, intensity[0], probe_real, probe_imag, right, left, left_conj, right_conj],
-        [SMEM_SPEC] + [VMEM_SPEC] * 8,
+        [offsets, image, intensity[0], probe_real, probe_imag, np.stack([right, left])],
+        [SMEM_SPEC] + [VMEM_SPEC] * 5,
         flops=2 * work,
         vmem=12,
         name="gradient",
     )
-    grad, lines, edges = lax.optimization_barrier((grad, lines, edges))
+    grad, angles = lax.optimization_barrier((grad, angles))
     grad = lax.all_to_all(grad, "tile", split_axis=0, concat_axis=0, tiled=True)
-    for h in range(1, parts):
-        lines, base, _ = project_part(h, lines, angles)
-        bases.append(base)
+
+    outs = call(
+        functools.partial(project_kernel, groups, slices),
+        [line] * groups + [shape((slices, share, length), F32), shape((slices, share, length), BF16)],
+        angles + [flat, flat, other, other, square, down_part],
+        [SMEM_SPEC] * groups + [lanes(0), lanes(1)] * 2 + [VMEM_SPEC] * 2,
+        scratch=[pltpu.VMEM(t.shape, F32) for t in tables_shape],
+        grid=(1,),
+        flops=3 * work,
+        vmem=28,
+        name="project_old",
+    )
+    lines, bases = take(outs, groups, 2)
     old = gathered(lines)
-
-    before = lax.ppermute(edges[0], "tile", [(i, i + 1) for i in range(tiles - 1)])
-    after = lax.ppermute(edges[1], "tile", [(i + 1, i) for i in range(tiles - 1)])
 
     phase_part, resid_part = call(
         functools.partial(line_kernel, groups), [line, line], [phase[0], dual[0], inverse_full] + old,
@@ -530,12 +530,13 @@
 
     results = []
     for h in range(parts):
-        args = bases[h] + [before, after] + list(halves[h]) + [square, down_part] + tables
+        args = bases + [before, after] + list(halves[h]) + [square, down_part] + tables
         results = call(
             functools.partial(update_kernel, groups, h == 0, h == parts - 1, len(results)),
             [shape((share, slices, length), F32)] + [line] * groups,
             args + list(results),
-            [VMEM_SPEC] * len(args) + [pl.BlockSpec(memory_space=pl.ANY)] * len(results),
+            [pl.BlockSpec((some, share, length), lambda _, h=h: (h, 0, 0))] * 2
+            + [VMEM_SPEC] * (len(args) - 2) + [pl.BlockSpec(memory_space=pl.ANY)] * len(results),
             [pl.BlockSpec((share, some, length), lambda _, h=h: (0, h, 0))]
             + [block_lines[h]] * groups,
             scratch=[pltpu.VMEM((share * some, half), F32)] * 2,

time: 74.9 us -> 67 us (0.89)
  waiting for transfers between devices: 12.9 us -> 8.08 us
  local copies, waits for them, and re-layouts: 10.2 us -> 6.12 us
  starting transfers between devices: 22.6 us -> 25.4 us
  Pallas kernels: 26.9 us -> 25.3 us
    unnamed x54 -> x38, local copies, waits for them, and re-layouts: 8.84 us -> 4.73 us
    ppermute x1, waiting for transfers between devices: 4.27 us -> 0.36 us  [shards(): lax.ppermute(edges[1], 'tile', [(i + 1, i) for i in range(tiles - 1)])]
    ppermute x2, waiting for transfers between devices: 6.37 us -> 4.48 us  [to_peer(): lax.ppermute(value, 'ang', [(i, (i + 2 * j) % ang) for i in range(ang)])]
    ppermute x2, starting transfers between devices: 1.1 us -> 3 us  [to_peer(): lax.ppermute(value, 'ang', [(i, (i + 2 * j) % ang) for i in range(ang)])]
    pallas_call x11, Pallas kernels: 26.9 us -> 25.3 us  [call(): pl.pallas_call(kernel, grid=grid, out_shape=tuple(outs), in_specs=specs o...]
    ppermute x2, waiting for transfers between devices: 1.9 us -> 3.22 us  [from_peer(): lax.ppermute(value, 'ang', [((i + 2 * j) % ang, i) for i in range(ang)])]
    all_to_all x1, starting transfers between devices: 5.83 us -> 6.83 us  [shards(): lax.all_to_all(phases, 'tile', split_axis=0, concat_axis=0, tiled=True)]
  transfers between devices with their start and end apart: 11 -> 11, of which waited for: 5 -> 5; matrix products, arithmetic and copies ran while one was open for 2% -> 0% of each run, Pallas kernels for 22% -> 22%
where the time goes in v4:
time: 67 us; the launch traced here: 66.4 us
  starting transfers between devices  25.4 us (38%)
  Pallas kernels  25.3 us (38%)
  waiting for transfers between devices  8.08 us (12%)
  local copies, waits for them, and re-layouts  6.12 us (9%)
  between operations  1.47 us (2%)
    pallas_call x11, Pallas kernels, call(): pl.pallas_call(kernel, grid=grid, out_shape=tuple(outs), in_specs=specs o...  25.3 us
    all_to_all x1, starting transfers between devices, shards(): lax.all_to_all(phases, 'tile', split_axis=0, concat_axis=0, tiled=True)  6.83 us
    all_to_all x1, starting transfers between devices, shards(): grad = lax.all_to_all(grad, 'tile', split_axis=0, concat_axis=0, tiled=True)  6.26 us
    unnamed x38, local copies, waits for them, and re-layouts  4.73 us
    ppermute x2, waiting for transfers between devices, to_peer(): lax.ppermute(value, 'ang', [(i, (i + 2 * j) % ang) for i in range(ang)])  4.48 us
    ppermute x1, starting transfers between devices, shards(): lax.ppermute(edges[0], 'tile', [(i, i + 1) for i in range(tiles - 1)])  3.92 us
    ppermute x2, waiting for transfers between devices, from_peer(): lax.ppermute(value, 'ang', [((i + 2 * j) % ang, i) for i in range(ang)])  3.22 us
    ppermute x2, starting transfers between devices, from_peer(): lax.ppermute(value, 'ang', [((i + 2 * j) % ang, i) for i in range(ang)])  3.06 us
  transfers between devices with their start and end apart: 11, of which 5 were waited for; matrix products, arithmetic and copies ran while one was open for 0% of the time, Pallas kernels for 22%

profile of v4, /device:TPU:0, one launch (start us, length us, event | category | flops | bytes accessed | tf_op | source)
XLA Modules:
  0.0 66.4 jit_solution(17658551337246483279)
XLA Ops:
  0.6 1.4 %broadcast_in_dim.14 = f32[8,16,256]{2,1,0:T(8,128)} broadcast(f32[16,256]{1,0:T(8,128)} %bitcast.13), dimensions={1,2} | broadcast | bytes 147456 | tf_op jit(solution)/shard_map/broadcast_in_dim | solution.py:454
  2.0 0.5 collective-permute-start
  2.5 6.8 %all-to-all-start = ((f32[8,16,256]{2,1,0:T(8,128)}), f32[8,16,256]{2,1,0:T(8,128)S(1)}, u32[]{:S(2)}, u32[]{:S(2)}) async-start(f32[8,16,256]{2,1,0:T(8,128)} %broadcast_in_dim.14), calls=%async_computation | async-start | bytes 262144 | tf_op jit(solution)/shard_map/all_to_all | solution.py:456
  9.3 0.0 collective-permute-done.refs_2_.refs_3_.refs_4_.refs_5_
  9.3 0.0 copy-start
  9.3 1.2 %copy-done = f32[64,16,256]{2,1,0:T(8,128)S(1)} copy-done((f32[64,16,256]{2,1,0:T(8,128)S(1)}, f32[64,16,256]{2,1,0:T(8,128)}, u32[]{:S(2)}) %copy-start) | copy-done | bytes 1048600
  10.5 0.3 edges.1
  10.8 3.9 %collective-permute-start.1 = (bf16[128,256]{1,0:T(8,128)(2,1)S(1)}, bf16[128,256]{1,0:T(8,128)(2,1)S(1)}, u32[]{:S(2)}, u32[]{:S(2)}) collective-permute-start(bf16[128,256]{1,0:T(8,128)(2,1)S(1)} %get-tuple-element.41), channel_id=1, source_target_pairs={{0,1},{1,2},{2,3},{3,4},{4,5},{5,6},{6,7},{8,9},{9,10},{10,11},{11... | collective-permute-start | bytes 196616 | tf_op jit(solution)/shard_map/ppermute | solution.py:470
  14.7 1.3 %collective-permute-start.2 = (bf16[128,256]{1,0:T(8,128)(2,1)S(1)}, bf16[128,256]{1,0:T(8,128)(2,1)S(1)}, u32[]{:S(2)}, u32[]{:S(2)}) collective-permute-start(bf16[128,256]{1,0:T(8,128)(2,1)S(1)} %get-tuple-element.42), channel_id=1, source_target_pairs={{1,0},{2,1},{3,2},{4,3},{5,4},{6,5},{7,6},{9,8},{10,9},{11,10},{12... | collective-permute-start | bytes 196616 | tf_op jit(solution)/shard_map/ppermute | solution.py:471
  16.7 1.6 %collective-permute-start.3 = (s32[1]{0:T(128)}, s32[1]{0:T(128)}, u32[]{:S(2)}, u32[]{:S(2)}) collective-permute-start(s32[1]{0:T(128)} %param.21), channel_id=1, source_target_pairs={{16,0},{24,8},{0,16},{8,24},{17,1},{25,9},{1,17},{9,25},{18,2},{26... | collective-permute-start | bytes 20 | tf_op jit(solution)/shard_map/ppermute | solution.py:436
  18.2 0.0 all-to-all-done
  18.2 2.3 %collective-permute-done.3.refs_1_ = s32[1]{0:T(128)} collective-permute-done((s32[1]{0:T(128)}, s32[1]{0:T(128)}, u32[]{:S(2)}, u32[]{:S(2)}) %collective-permute-start.3) | collective-permute-done | bytes 36 | tf_op jit(solution)/shard_map/ppermute | solution.py:436
  20.5 0.0 collective-permute-done.1.refs_2_
  20.5 0.4 collective-permute-done.2.refs_3_
  20.9 0.0 copy-done.7
  20.9 0.6 copy-done.10
  21.6 1.0 %copy-done.12 = bf16[2,2,256,256]{3,2,1,0:T(8,128)(2,1)S(1)} copy-done((bf16[2,2,256,256]{3,2,1,0:T(8,128)(2,1)S(1)}, bf16[2,2,256,256]{3,2,1,0:T(8,128)(2,1)}, u32[]{:S(2)}) %copy-start.12) | copy-done | bytes 524312
  22.6 3.5 %gradient.1 = bf16[8,16,256]{2,1,0:T(8,128)(2,1)} custom-call(s32[1,4]{1,0:T(1,128)S(1)} %copy-done.10, f32[128,256]{1,0:T(8,128)S(1)} %bitcast.12, f32[4,128,128]{2,1,0:T(8,128)S(1)} %bitcast.18, f32[128,128]{1,0:T(8,128)S(1)} %copy-done.8, f32[128,128]{1,0:T(8,128)S(1)} %copy-done.9, bf16[2,2,256,256]{3,2,1,0:T(8,128)(2,1)S(1)} %copy-done.12), custom_call_target="tpu_custom_call" | custom-call | flops 4294967296 | bytes 1048576 | tf_op jit(solution)/shard_map/gradient/pallas_call | solution.py:393
  26.1 6.3 %all-to-all-start.1 = ((bf16[8,16,256]{2,1,0:T(8,128)(2,1)}), bf16[8,16,256]{2,1,0:T(8,128)(2,1)S(1)}, u32[]{:S(2)}, u32[]{:S(2)}) async-start(bf16[8,16,256]{2,1,0:T(8,128)(2,1)} %gradient.1), calls=%async_computation.1 | async-start | bytes 131072 | tf_op jit(solution)/shard_map/all_to_all | solution.py:486
  32.3 0.0 copy-done.1
  32.3 0.0 copy-start.2
  32.4 0.0 copy-start.4
  32.4 0.0 copy-start.5
  32.4 7.5 %project_old.1 = (f32[16,256]{1,0:T(8,128)S(1)}, f32[16,256]{1,0:T(8,128)S(1)}, f32[16,64,256]{2,1,0:T(8,128)S(1)}, bf16[16,64,256]{2,1,0:T(8,128)(2,1)S(1)}) custom-call(s32[1]{0:T(128)S(6)} %copy.23.refs_0_, s32[1]{0:T(128)} %collective-permute-done.3.refs_1_, f32[1024,256]{1,0:T(8,128)S(1)} %bitcast.10, f32[1024,256]{1,0:T(8,128)S(1)} %bitcast.11, ...), custom_call_target="tpu_custom_call" | custom-call | flops 6442450944 | bytes 1048576 | tf_op jit(solution)/shard_map/project_old/pallas_call | solution.py:393
  39.8 0.0 copy-start.15
  39.9 1.0 %copy-done.15 = f32[16,64,256]{2,1,0:T(8,128)} copy-done((f32[16,64,256]{2,1,0:T(8,128)}, f32[16,64,256]{2,1,0:T(8,128)S(1)}, u32[]{:S(2)}) %copy-start.15) | copy-done | bytes 1048600
  40.8 0.8 %copy-done.17 = bf16[16,64,256]{2,1,0:T(8,128)(2,1)} copy-done((bf16[16,64,256]{2,1,0:T(8,128)(2,1)}, bf16[16,64,256]{2,1,0:T(8,128)(2,1)S(1)}, u32[]{:S(2)}) %copy-start.17) | copy-done | bytes 524312
  41.6 1.5 %collective-permute-start.4 = (f32[16,256]{1,0:T(8,128)S(1)}, f32[16,256]{1,0:T(8,128)S(1)}, u32[]{:S(2)}, u32[]{:S(2)}) collective-permute-start(f32[16,256]{1,0:T(8,128)S(1)} %get-tuple-element.51), channel_id=1, source_target_pairs={{0,16},{8,24},{16,0},{24,8},{1,17},{9,25},{17,1},{25,9},{2,18},{10... | collective-permute-start | bytes 49160 | tf_op jit(solution)/shard_map/ppermute | solution.py:439
  43.1 2.2 %collective-permute-done.4.refs_1_ = f32[16,256]{1,0:T(8,128)S(1)} collective-permute-done((f32[16,256]{1,0:T(8,128)S(1)}, f32[16,256]{1,0:T(8,128)S(1)}, u32[]{:S(2)}, u32[]{:S(2)}) %collective-permute-start.4) | collective-permute-done | bytes 16416 | tf_op jit(solution)/shard_map/ppermute | solution.py:439
  45.4 0.2 line_step.1
  45.6 0.0 all-to-all-done.1.grad_ref
  45.6 0.6 phase_step.1
  46.2 1.5 %collective-permute-start.5 = (f32[16,256]{1,0:T(8,128)S(1)}, f32[16,256]{1,0:T(8,128)S(1)}, u32[]{:S(2)}, u32[]{:S(2)}) collective-permute-start(f32[16,256]{1,0:T(8,128)S(1)} %get-tuple-element.60.refs_0_), channel_id=1, source_target_pairs={{16,0},{24,8},{0,16},{8,24},{17,1},{25,9},{1,17},{9,25},{18,2},{26... | collective-permute-start | bytes 49160 | tf_op jit(solution)/shard_map/ppermute | solution.py:436
  47.7 1.3 %turn_tables.1 = (f32[3,256,128]{2,1,0:T(8,128)S(1)}, f32[2,128,256]{2,1,0:T(8,128)S(1)}, f32[8,256]{1,0:T(8,128)S(1)}, f32[3,256,128]{2,1,0:T(8,128)S(1)}, f32[...) custom-call(s32[1]{0:T(128)S(6)} %copy.23.refs_0_, s32[1]{0:T(128)} %collective-permute-done.3.refs_1_), custom_call_target="tpu_custom_call" | custom-call | flops 2147483648 | bytes 1048576 | tf_op jit(solution)/shard_map/turn_tables/pallas_call | solution.py:393
  49.0 0.9 %collective-permute-done.5.refs_1_ = f32[16,256]{1,0:T(8,128)S(1)} collective-permute-done((f32[16,256]{1,0:T(8,128)S(1)}, f32[16,256]{1,0:T(8,128)S(1)}, u32[]{:S(2)}, u32[]{:S(2)}) %collective-permute-start.5) | collective-permute-done | bytes 16416 | tf_op jit(solution)/shard_map/ppermute | solution.py:436
  50.0 2.4 %backproject.3.refs_4_ = bf16[8,128,256]{2,1,0:T(8,128)(2,1)S(1)} custom-call(f32[16,256]{1,0:T(8,128)S(1)} %get-tuple-element.60.refs_0_, f32[16,256]{1,0:T(8,128)S(1)} %collective-permute-done.5.refs_1_, bf16[4,256,256]{2,1,0:T(8,128)(2,1)S(1)} %copy-done.11, bf16[4,128,256]{2,1,0:T(8,128)(2,1)S(1)} %copy-done.14, ...), custom_call_target="tpu_custom_call" | custom-call | flops 3221225472 | bytes 1048576 | tf_op jit(solution)/shard_map/backproject/pallas_call | solution.py:393
  52.4 0.0 copy-start.16
  52.4 0.1 collective-permute-start.7
  52.5 2.6 %backproject.2.refs_4_ = bf16[8,128,256]{2,1,0:T(8,128)(2,1)S(1)} custom-call(f32[16,256]{1,0:T(8,128)S(1)} %get-tuple-element.60.refs_0_, f32[16,256]{1,0:T(8,128)S(1)} %collective-permute-done.5.refs_1_, bf16[4,256,256]{2,1,0:T(8,128)(2,1)S(1)} %copy-done.11, bf16[4,128,256]{2,1,0:T(8,128)(2,1)S(1)} %copy-done.14, ...), custom_call_target="tpu_custom_call" | custom-call | flops 3221225472 | bytes 1048576 | tf_op jit(solution)/shard_map/backproject/pallas_call | solution.py:393
  55.1 0.6 collective-permute-start.6
  55.6 0.0 collective-permute-done.7.refs_5_
  55.7 3.0 %project_new.2 = (f32[64,16,256]{2,1,0:T(8,128)}, f32[16,256]{1,0:T(8,128)S(1)}, f32[16,256]{1,0:T(8,128)S(1)}) custom-call(f32[16,64,256]{2,1,0:T(8,128)S(1)} %copy-done.16, bf16[16,64,256]{2,1,0:T(8,128)(2,1)S(1)} %copy-done.18, bf16[128,256]{1,0:T(8,128)(2,1)S(1)} %collective-permute-done.1.refs_2_, bf16[128,256]{1,0:T(8,128)(2,1)S(1)} %collective-permute-done.2.refs_3_, ...), custom_call_target="tpu_custom_call" | custom-call | flops 3221225472 | bytes 1048576 | tf_op jit(solution)/shard_map/project_new/pallas_call | solution.py:393
  58.7 0.0 collective-permute-done.6.refs_5_
  58.7 0.0 copy-start.6
  58.7 3.2 %project_new.3 = (f32[64,16,256]{2,1,0:T(8,128)}, f32[16,256]{1,0:T(8,128)S(1)}, f32[16,256]{1,0:T(8,128)S(1)}) custom-call(f32[16,64,256]{2,1,0:T(8,128)S(1)} %copy-done.16, bf16[16,64,256]{2,1,0:T(8,128)(2,1)S(1)} %copy-done.18, bf16[128,256]{1,0:T(8,128)(2,1)S(1)} %collective-permute-done.1.refs_2_, ...), custom_call_target="tpu_custom_call", output_to_operand_aliasing={{0}: (14, {}), {1}: (15, {}), {2}: (16, {})} | custom-call | flops 3221225472 | bytes 1048576 | tf_op jit(solution)/shard_map/project_new/pallas_call | solution.py:393
  61.9 1.5 %collective-permute-start.8 = (f32[16,256]{1,0:T(8,128)S(1)}, f32[16,256]{1,0:T(8,128)S(1)}, u32[]{:S(2)}, u32[]{:S(2)}) collective-permute-start(f32[16,256]{1,0:T(8,128)S(1)} %get-tuple-element.74), channel_id=1, source_target_pairs={{0,16},{8,24},{16,0},{24,8},{1,17},{9,25},{17,1},{25,9},{2,18},{10... | collective-permute-start | bytes 49160 | tf_op jit(solution)/shard_map/ppermute | solution.py:439
  63.4 2.2 %collective-permute-done.8.refs_1_ = f32[16,256]{1,0:T(8,128)S(1)} collective-permute-done((f32[16,256]{1,0:T(8,128)S(1)}, f32[16,256]{1,0:T(8,128)S(1)}, u32[]{:S(2)}, u32[]{:S(2)}) %collective-permute-start.8) | collective-permute-done | bytes 16416 | tf_op jit(solution)/shard_map/ppermute | solution.py:439
  65.7 0.8 %dual_step.1 = f32[16,256]{1,0:T(8,128)} custom-call(f32[16,256]{1,0:T(8,128)S(1)} %copy-done.6, f32[16,256]{1,0:T(8,128)S(1)} %bitcast.16, bf16[2,256,256]{2,1,0:T(8,128)(2,1)S(1)} %copy-done.2, f32[16,256]{1,0:T(8,128)S(1)} %get-tuple-element.73.refs_0_, f32[16,256]{1,0:T(8,128)S(1)} %collective-permute-done.8.refs_1_), custom_call_target="tpu_custom_call" | custom-call | bytes 1048576 | tf_op jit(solution)/shard_map/dual_step/pallas_call | solution.py:393
  (24 shorter events, 0.0 us)
Async XLA Ops:
  2.0 7.3 %collective-permute-start = (f32[1024,256]{1,0:T(8,128)}, f32[1024,256]{1,0:T(8,128)S(1)}, u32[]{:S(2)}, u32[]{:S(2)}) collective-permute-start(f32[1024,256]{1,0:T(8,128)} %bitcast.7), channel_id=1, source_target_pairs={{0,8},{8,0},{16,24},{24,16},{1,9},{9,1},{17,25},{25,17},{2,10},{10... | collective-permute-start | bytes 3145736 | tf_op jit(solution)/shard_map/ppermute | solution.py:433
  2.5 15.8 %all-to-all-start = ((f32[8,16,256]{2,1,0:T(8,128)}), f32[8,16,256]{2,1,0:T(8,128)S(1)}, u32[]{:S(2)}, u32[]{:S(2)}) async-start(f32[8,16,256]{2,1,0:T(8,128)} %broadcast_in_dim.14), calls=%async_computation | async-start | bytes 262144 | tf_op jit(solution)/shard_map/all_to_all | solution.py:456
  9.3 1.2 %copy-start = (f32[64,16,256]{2,1,0:T(8,128)S(1)}, f32[64,16,256]{2,1,0:T(8,128)}, u32[]{:S(2)}) copy-start(f32[64,16,256]{2,1,0:T(8,128)} %param.14) | copy-start | bytes 3145732
  10.5 10.4 %copy-start.7 = (f32[1,4,128,128]{3,2,1,0:T(8,128)S(1)}, f32[1,4,128,128]{3,2,1,0:T(8,128)}, u32[]{:S(2)}) copy-start(f32[1,4,128,128]{3,2,1,0:T(8,128)} %param.19) | copy-start | bytes 786436
  10.5 10.4 %copy-start.8 = (f32[128,128]{1,0:T(8,128)S(1)}, f32[128,128]{1,0:T(8,128)}, u32[]{:S(2)}) copy-start(f32[128,128]{1,0:T(8,128)} %probe_r_ref.1) | copy-start | bytes 196612
  10.5 10.4 %copy-start.9 = (f32[128,128]{1,0:T(8,128)S(1)}, f32[128,128]{1,0:T(8,128)}, u32[]{:S(2)}) copy-start(f32[128,128]{1,0:T(8,128)} %probe_i_ref.1) | copy-start | bytes 196612
  10.8 9.7 %collective-permute-start.1 = (bf16[128,256]{1,0:T(8,128)(2,1)S(1)}, bf16[128,256]{1,0:T(8,128)(2,1)S(1)}, u32[]{:S(2)}, u32[]{:S(2)}) collective-permute-start(bf16[128,256]{1,0:T(8,128)(2,1)S(1)} %get-tuple-element.41), channel_id=1, source_target_pairs={{0,1},{1,2},{2,3},{3,4},{4,5},{5,6},{6,7},{8,9},{9,10},{10,11},{11... | collective-permute-start | bytes 196616 | tf_op jit(solution)/shard_map/ppermute | solution.py:470
  14.7 6.2 %collective-permute-start.2 = (bf16[128,256]{1,0:T(8,128)(2,1)S(1)}, bf16[128,256]{1,0:T(8,128)(2,1)S(1)}, u32[]{:S(2)}, u32[]{:S(2)}) collective-permute-start(bf16[128,256]{1,0:T(8,128)(2,1)S(1)} %get-tuple-element.42), channel_id=1, source_target_pairs={{1,0},{2,1},{3,2},{4,3},{5,4},{6,5},{7,6},{9,8},{10,9},{11,10},{12... | collective-permute-start | bytes 196616 | tf_op jit(solution)/shard_map/ppermute | solution.py:471
  16.7 3.8 %collective-permute-start.3 = (s32[1]{0:T(128)}, s32[1]{0:T(128)}, u32[]{:S(2)}, u32[]{:S(2)}) collective-permute-start(s32[1]{0:T(128)} %param.21), channel_id=1, source_target_pairs={{16,0},{24,8},{0,16},{8,24},{17,1},{25,9},{1,17},{9,25},{18,2},{26... | collective-permute-start | bytes 20 | tf_op jit(solution)/shard_map/ppermute | solution.py:436
  20.9 0.7 copy-start.10
  21.5 1.0 %copy-start.12 = (bf16[2,2,256,256]{3,2,1,0:T(8,128)(2,1)S(1)}, bf16[2,2,256,256]{3,2,1,0:T(8,128)(2,1)}, u32[]{:S(2)}) copy-start(bf16[2,2,256,256]{3,2,1,0:T(8,128)(2,1)} %constant.12.clone.const_ref) | copy-start | bytes 1572868
  22.6 9.7 %copy-start.1 = (f32[64,16,256]{2,1,0:T(8,128)S(1)}, f32[64,16,256]{2,1,0:T(8,128)}, u32[]{:S(2)}) copy-start(f32[64,16,256]{2,1,0:T(8,128)} %param.14) | copy-start | bytes 3145732
  22.6 9.7 %copy-start.11 = (bf16[4,256,256]{2,1,0:T(8,128)(2,1)S(1)}, bf16[4,256,256]{2,1,0:T(8,128)(2,1)}, u32[]{:S(2)}) copy-start(bf16[4,256,256]{2,1,0:T(8,128)(2,1)} %constant.13.clone.refs_6_.refs_2_) | copy-start | bytes 1572868
  22.6 9.7 %copy-start.13 = (bf16[4,256,128]{2,1,0:T(8,128)(2,1)S(1)}, bf16[4,256,128]{2,1,0:T(8,128)(2,1)}, u32[]{:S(2)}) copy-start(bf16[4,256,128]{2,1,0:T(8,128)(2,1)} %constant.14.clone.refs_7_) | copy-start | bytes 786436
  26.1 19.5 %all-to-all-start.1 = ((bf16[8,16,256]{2,1,0:T(8,128)(2,1)}), bf16[8,16,256]{2,1,0:T(8,128)(2,1)S(1)}, u32[]{:S(2)}, u32[]{:S(2)}) async-start(bf16[8,16,256]{2,1,0:T(8,128)(2,1)} %gradient.1), calls=%async_computation.1 | async-start | bytes 131072 | tf_op jit(solution)/shard_map/all_to_all | solution.py:486
  32.3 13.0 %copy-start.2 = (bf16[2,256,256]{2,1,0:T(8,128)(2,1)S(1)}, bf16[2,256,256]{2,1,0:T(8,128)(2,1)}, u32[]{:S(2)}) copy-start(bf16[2,256,256]{2,1,0:T(8,128)(2,1)} %constant.15.clone.inverse_ref) | copy-start | bytes 786436
  32.4 13.0 %copy-start.4 = (f32[1,16,256]{2,1,0:T(8,128)S(1)}, f32[1,16,256]{2,1,0:T(8,128)}, u32[]{:S(2)}) copy-start(f32[1,16,256]{2,1,0:T(8,128)} %param.15) | copy-start | bytes 49156
  32.4 13.0 %copy-start.5 = (f32[1,16,256]{2,1,0:T(8,128)S(1)}, f32[1,16,256]{2,1,0:T(8,128)}, u32[]{:S(2)}) copy-start(f32[1,16,256]{2,1,0:T(8,128)} %param.16) | copy-start | bytes 49156
  39.8 1.0 %copy-start.15 = (f32[16,64,256]{2,1,0:T(8,128)}, f32[16,64,256]{2,1,0:T(8,128)S(1)}, u32[]{:S(2)}) copy-start(f32[16,64,256]{2,1,0:T(8,128)S(1)} %get-tuple-element.55.refs_0_) | copy-start | bytes 3145732
  40.8 0.8 %copy-start.17 = (bf16[16,64,256]{2,1,0:T(8,128)(2,1)}, bf16[16,64,256]{2,1,0:T(8,128)(2,1)S(1)}, u32[]{:S(2)}) copy-start(bf16[16,64,256]{2,1,0:T(8,128)(2,1)S(1)} %get-tuple-element.56.refs_1_) | copy-start | bytes 1572868
  41.6 4.0 %copy-start.3 = (bf16[2,256,256]{2,1,0:T(8,128)(2,1)S(1)}, bf16[2,256,256]{2,1,0:T(8,128)(2,1)}, u32[]{:S(2)}) copy-start(bf16[2,256,256]{2,1,0:T(8,128)(2,1)} %constant.16.clone.forward_ref) | copy-start | bytes 786436
  41.6 3.7 %collective-permute-start.4 = (f32[16,256]{1,0:T(8,128)S(1)}, f32[16,256]{1,0:T(8,128)S(1)}, u32[]{:S(2)}, u32[]{:S(2)}) collective-permute-start(f32[16,256]{1,0:T(8,128)S(1)} %get-tuple-element.51), channel_id=1, source_target_pairs={{0,16},{8,24},{16,0},{24,8},{1,17},{9,25},{17,1},{25,9},{2,18},{10... | collective-permute-start | bytes 49160 | tf_op jit(solution)/shard_map/ppermute | solution.py:439
  46.2 3.7 %copy-start.14 = (bf16[4,128,256]{2,1,0:T(8,128)(2,1)S(1)}, bf16[4,128,256]{2,1,0:T(8,128)(2,1)}, u32[]{:S(2)}) copy-start(bf16[4,128,256]{2,1,0:T(8,128)(2,1)} %constant.17.clone.refs_3_) | copy-start | bytes 786436
  46.2 3.7 %collective-permute-start.5 = (f32[16,256]{1,0:T(8,128)S(1)}, f32[16,256]{1,0:T(8,128)S(1)}, u32[]{:S(2)}, u32[]{:S(2)}) collective-permute-start(f32[16,256]{1,0:T(8,128)S(1)} %get-tuple-element.60.refs_0_), channel_id=1, source_target_pairs={{16,0},{24,8},{0,16},{8,24},{17,1},{25,9},{1,17},{9,25},{18,2},{26... | collective-permute-start | bytes 49160 | tf_op jit(solution)/shard_map/ppermute | solution.py:436
  52.4 3.3 %copy-start.16 = (f32[16,64,256]{2,1,0:T(8,128)S(1)}, f32[16,64,256]{2,1,0:T(8,128)}, u32[]{:S(2)}) copy-start(f32[16,64,256]{2,1,0:T(8,128)} %copy-done.15) | copy-start | bytes 3145732
  52.4 3.3 %copy-start.18 = (bf16[16,64,256]{2,1,0:T(8,128)(2,1)S(1)}, bf16[16,64,256]{2,1,0:T(8,128)(2,1)}, u32[]{:S(2)}) copy-start(bf16[16,64,256]{2,1,0:T(8,128)(2,1)} %copy-done.17) | copy-start | bytes 1572868
  52.4 3.3 %collective-permute-start.7 = (bf16[8,128,256]{2,1,0:T(8,128)(2,1)S(1)}, bf16[8,128,256]{2,1,0:T(8,128)(2,1)S(1)}, u32[]{:S(2)}, u32[]{:S(2)}) collective-permute-start(bf16[8,128,256]{2,1,0:T(8,128)(2,1)S(1)} %backproject.3.refs_4_), channel_id=1, source_target_pairs={{0,8},{8,0},{16,24},{24,16},{1,9},{9,1},{17,25},{25,17},{2,10},{10... | collective-permute-start | bytes 1572872 | tf_op jit(solution)/shard_map/ppermute | solution.py:433
  55.1 3.6 %collective-permute-start.6 = (bf16[8,128,256]{2,1,0:T(8,128)(2,1)S(1)}, bf16[8,128,256]{2,1,0:T(8,128)(2,1)S(1)}, u32[]{:S(2)}, u32[]{:S(2)}) collective-permute-start(bf16[8,128,256]{2,1,0:T(8,128)(2,1)S(1)} %backproject.2.refs_4_), channel_id=1, source_target_pairs={{0,8},{8,0},{16,24},{24,16},{1,9},{9,1},{17,25},{25,17},{2,10},{10... | collective-permute-start | bytes 1572872 | tf_op jit(solution)/shard_map/ppermute | solution.py:433
  58.7 7.0 %copy-start.6 = (f32[16,256]{1,0:T(8,128)S(1)}, f32[16,256]{1,0:T(8,128)}, u32[]{:S(2)}) copy-start(f32[16,256]{1,0:T(8,128)} %get-tuple-element.54.phase_ref) | copy-start | bytes 49156
  61.9 3.7 %collective-permute-start.8 = (f32[16,256]{1,0:T(8,128)S(1)}, f32[16,256]{1,0:T(8,128)S(1)}, u32[]{:S(2)}, u32[]{:S(2)}) collective-permute-start(f32[16,256]{1,0:T(8,128)S(1)} %get-tuple-element.74), channel_id=1, source_target_pairs={{0,16},{8,24},{16,0},{24,8},{1,17},{9,25},{17,1},{25,9},{2,18},{10... | collective-permute-start | bytes 49160 | tf_op jit(solution)/shard_map/ppermute | solution.py:439

commit v5 on v4

--- a/solution.py
+++ b/solution.py
@@ -223,8 +223,8 @@
 
 
 def project_kernel(groups, slices, *refs):
-    angle_refs, sides, (const_ref, down_ref), lines_refs, bases, table_refs = take(
-        refs, groups, 4, 2, groups, 2, 3 * groups
+    angle_refs, sides, (const_ref, down_ref), lines_refs, bases, (slab_ref,), table_refs = take(
+        refs, groups, 4, 2, groups, 2, 1, 3 * groups
     )
     share = sides[0].shape[0] // slices
     tables_kernel(groups, *angle_refs, *table_refs)
@@ -244,10 +244,22 @@
             base = base + (tau_step * smooth_weight) * sum(near[1:], near[0])
             bases[place][z] = base.astype(bases[place].dtype)
         past, now = now, later
+    slab = jnp.concatenate(slab, axis=0)
+    slab_ref[...] = slab.reshape(slab_ref.shape)
     consts = [const_ref.at[0], const_ref.at[1], down_ref, const_ref.at[3]]
-    project_slices(
-        jnp.concatenate(slab, axis=0), slices, share, as_tables(table_refs), consts, lines_refs
-    )
+    project_slices(slab, slices, share, as_tables(table_refs), consts, lines_refs)
+
+
+def own_line_kernel(pieces, made, *refs):
+    slabs, (const_ref, down_ref), given, (line_ref,), table_refs = take(
+        refs, pieces, 2, 3 if made else 1, 1, 0 if made else 3
+    )
+    if not made:
+        tables_kernel(1, *given, *table_refs)
+    slab = jnp.concatenate([ref[...].reshape(-1, ref.shape[2]) for ref in slabs], axis=0)
+    consts = [const_ref.at[0], const_ref.at[1], down_ref, const_ref.at[3]]
+    tables = as_tables(given if made else table_refs)
+    project_slices(slab, line_ref.shape[0], slabs[0].shape[1] // 2, tables, consts, [line_ref])
 
 
 def back_kernel(groups, *refs):
@@ -279,8 +291,8 @@
 
 
 def update_kernel(groups, first, last, aliased, *refs):
-    bases, halos, shares, (const_ref, down_ref), table_refs, unused, (volume_ref,), lines_refs, sides = take(
-        refs, 2, 2, 2, 2, 3 * groups, aliased, 1, groups, 2
+    bases, halos, shares, (const_ref, down_ref), table_refs, unused, (volume_ref, slab_ref), lines_refs, sides = take(
+        refs, 2, 2, 2, 2, 3 * groups, aliased, 2, groups, 2
     )
     consts = [const_ref.at[0], const_ref.at[1], down_ref, const_ref.at[3]]
     own_ref, other_ref = bases
@@ -302,17 +314,19 @@
         for side in range(2):
             sides[side][pl.ds(z, share, stride=slices), :] = own[:, side * half : (side + 1) * half]
         slab += [own.astype(BF16), other.astype(BF16)]
-    project_slices(
-        jnp.concatenate(slab, axis=0), slices, share, as_tables(table_refs), consts, lines_refs
-    )
+    slab = jnp.concatenate(slab, axis=0)
+    slab_ref[...] = slab.reshape(slab_ref.shape)
+    project_slices(slab, slices, share, as_tables(table_refs), consts, lines_refs)
     whole = jnp.concatenate([ref[...] for ref in sides], axis=1)
     volume_ref[...] = whole.reshape(volume_ref.shape)
 
 
 def gradient_kernel(
     offsets_ref, image_ref, measured_ref, probe_r_ref, probe_i_ref,
-    const_ref, out_ref,
+    const_hbm_ref, out_ref, const_ref, sem,
 ):
+    fetch = pltpu.make_async_copy(const_hbm_ref, const_ref, sem)
+    fetch.start()
     right_ref, left_ref = const_ref.at[0], const_ref.at[1]
     left_conj_ref, right_conj_ref = right_ref, left_ref
     positions, height, width = measured_ref.shape
@@ -341,6 +355,7 @@
         )
 
     entry = jnp.concatenate([jnp.concatenate(wave, axis=1) for wave in waves], axis=0)
+    fetch.wait()
     far = dot_split(left_ref[...], to_columns(dot_split(entry, right_ref[...])))
     far_r, far_i = far[:height], far[height:]
     measured = jnp.concatenate([measured_ref[p] for p in range(positions)], axis=1)
@@ -441,9 +456,6 @@
     def lanes(side):
         return pl.BlockSpec((share * slices, half), lambda _: (0, side))
 
-    def gathered(lines):
-        return [lines[0]] + [to_peer(lines[j], j) for j in range(1, groups)]
-
     tables_shape = [
         shape((3, length, half), F32), shape((2, half, length), F32), shape((8, length), F32)
     ] * groups
@@ -452,7 +464,7 @@
     ]
 
     phases = jnp.broadcast_to(phase, (tiles, slices, length))
-    phases, volume = lax.optimization_barrier((phases, volume))
+    phases, volume, angle_sent = lax.optimization_barrier((phases, volume, angle_index))
     image = lax.all_to_all(phases, "tile", split_axis=0, concat_axis=0, tiled=True)
     image = image.reshape(tiles * slices, length)
 
@@ -469,35 +481,48 @@
     )
     before = lax.ppermute(edges[0], "tile", [(i, i + 1) for i in range(tiles - 1)])
     after = lax.ppermute(edges[1], "tile", [(i + 1, i) for i in range(tiles - 1)])
-    angle_index, edges = lax.optimization_barrier((angle_index, edges))
-    angles = [angle_index] + [from_peer(angle_index, j) for j in range(1, groups)]
-    image, before, after, angles = lax.optimization_barrier((image, before, after, angles))
+    angles = [from_peer(angle_sent, j) for j in range(1, groups)]
+    image, before, angles = lax.optimization_barrier((image, before, angles))
 
     (grad,) = call(
         gradient_kernel,
         [shape((tiles, slices, length), BF16)],
         [offsets, image, intensity[0], probe_real, probe_imag, np.stack([right, left])],
-        [SMEM_SPEC] + [VMEM_SPEC] * 5,
+        [SMEM_SPEC] + [VMEM_SPEC] * 4 + [pl.BlockSpec(memory_space=pl.ANY)],
+        scratch=[pltpu.VMEM((2,) + right.shape, BF16), pltpu.SemaphoreType.DMA],
         flops=2 * work,
         vmem=12,
         name="gradient",
     )
-    grad, angles = lax.optimization_barrier((grad, angles))
+    grad, after, angles = lax.optimization_barrier((grad, after, angles))
     grad = lax.all_to_all(grad, "tile", split_axis=0, concat_axis=0, tiled=True)
 
+    far = groups - 1
     outs = call(
-        functools.partial(project_kernel, groups, slices),
-        [line] * groups + [shape((slices, share, length), F32), shape((slices, share, length), BF16)],
+        functools.partial(project_kernel, far, slices),
+        [line] * far
+        + [shape((slices, share, length), F32), shape((slices, share, length), BF16)]
+        + [shape((slices, pair, length), BF16)],
         angles + [flat, flat, other, other, square, down_part],
-        [SMEM_SPEC] * groups + [lanes(0), lanes(1)] * 2 + [VMEM_SPEC] * 2,
-        scratch=[pltpu.VMEM(t.shape, F32) for t in tables_shape],
+        [SMEM_SPEC] * far + [lanes(0), lanes(1)] * 2 + [VMEM_SPEC] * 2,
+        scratch=[pltpu.VMEM(t.shape, F32) for t in tables_shape[3:]],
         grid=(1,),
-        flops=3 * work,
+        flops=3 * work * far // groups,
         vmem=28,
         name="project_old",
     )
-    lines, bases = take(outs, groups, 2)
-    old = gathered(lines)
+    lines, bases, slab = take(outs, far, 2, 1)
+    old = [to_peer(lines[j], j + 1) for j in range(far)]
+    old += call(
+        functools.partial(own_line_kernel, 1, False),
+        [line],
+        slab + [square, down_part, angle_index],
+        [VMEM_SPEC] * 3 + [SMEM_SPEC],
+        scratch=[pltpu.VMEM(t.shape, F32) for t in tables_shape[:3]],
+        flops=3 * work // groups,
+        vmem=24,
+        name="project_old_own",
+    )
 
     phase_part, resid_part = call(
         functools.partial(line_kernel, groups), [line, line], [phase[0], dual[0], inverse_full] + old,
@@ -506,7 +531,7 @@
     phase_new, spectrum = call(
         phase_kernel, [line, line], [grad, phase_part, resid_part, forward_full], name="phase_step"
     )
-    spectrum, angles = lax.optimization_barrier((spectrum, angles))
+    spectrum, angles = lax.optimization_barrier((spectrum, [angle_index] + angles))
     tables = call(
         functools.partial(tables_kernel, groups), tables_shape, angles, [SMEM_SPEC] * groups,
         flops=work, name="turn_tables",
@@ -528,28 +553,38 @@
         )
         halves.append((mine, swap(mine)))
 
-    results = []
+    results, slabs = [], []
     for h in range(parts):
-        args = bases + [before, after] + list(halves[h]) + [square, down_part] + tables
-        results = call(
-            functools.partial(update_kernel, groups, h == 0, h == parts - 1, len(results)),
-            [shape((share, slices, length), F32)] + [line] * groups,
-            args + list(results),
+        args = bases + [before, after] + list(halves[h]) + [square, down_part] + tables[3:]
+        outs = call(
+            functools.partial(update_kernel, far, h == 0, h == parts - 1, len(results)),
+            [shape((share, slices, length), F32), shape((some, pair, length), BF16)] + [line] * far,
+            args + results,
             [pl.BlockSpec((some, share, length), lambda _, h=h: (h, 0, 0))] * 2
             + [VMEM_SPEC] * (len(args) - 2) + [pl.BlockSpec(memory_space=pl.ANY)] * len(results),
-            [pl.BlockSpec((share, some, length), lambda _, h=h: (0, h, 0))]
-            + [block_lines[h]] * groups,
+            [pl.BlockSpec((share, some, length), lambda _, h=h: (0, h, 0)), VMEM_SPEC]
+            + [block_lines[h]] * far,
             scratch=[pltpu.VMEM((share * some, half), F32)] * 2,
             grid=(1,),
-            flops=3 * work // parts,
+            flops=3 * work * far // groups // parts,
             vmem=24,
-            aliases={len(args) + i: i for i in range(len(results))},
+            aliases={len(args) + i: i + (1 if i else 0) for i in range(len(results))},
             name="project_new",
         )
+        slabs.append(outs[1])
+        results = [outs[0]] + list(outs[2:])
     volume_new, lines = results[0], results[1:]
+    new = [to_peer(lines[j], j + 1) for j in range(far)]
+    new += call(
+        functools.partial(own_line_kernel, parts, True),
+        [line],
+        slabs + [square, down_part] + tables[:3],
+        flops=3 * work // groups,
+        vmem=24,
+        name="project_new_own",
+    )
     (dual_new,) = call(
-        functools.partial(dual_kernel, groups), [line],
-        [phase_new, dual[0], inverse_full] + gathered(lines),
+        functools.partial(dual_kernel, groups), [line], [phase_new, dual[0], inverse_full] + new,
         name="dual_step",
     )
     return phase_new[None], volume_new, dual_new[None]

time: 67 us -> 62.2 us (0.928)
  waiting for transfers between devices: 8.08 us -> 1.27 us
  Pallas kernels: 25.3 us -> 28.2 us
  starting transfers between devices: 25.4 us -> 24.6 us
    ppermute x2, waiting for transfers between devices: 4.48 us -> 0.01 us  [to_peer(): lax.ppermute(value, 'ang', [(i, (i + 2 * j) % ang) for i in range(ang)])]
    pallas_call x11 -> x13, Pallas kernels: 25.3 us -> 28.2 us  [call(): pl.pallas_call(kernel, grid=grid, out_shape=tuple(outs), in_specs=specs o...]
    ppermute x2, waiting for transfers between devices: 3.22 us -> 1.24 us  [from_peer(): lax.ppermute(value, 'ang', [((i + 2 * j) % ang, i) for i in range(ang)])]
    ppermute x2, starting transfers between devices: 3 us -> 2.1 us  [to_peer(): lax.ppermute(value, 'ang', [(i, (i + 2 * j) % ang) for i in range(ang)])]
  transfers between devices with their start and end apart: 11 -> 11, of which waited for: 5 -> 2; matrix products, arithmetic and copies ran while one was open for 0% -> 0% of each run, Pallas kernels for 22% -> 36%
where the time goes in v5:
time: 62.2 us; the launch traced here: 61.6 us
  Pallas kernels  28.2 us (45%)
  starting transfers between devices  24.6 us (40%)
  local copies, waits for them, and re-layouts  5.97 us (10%)
  between operations  1.58 us (3%)
  waiting for transfers between devices  1.27 us (2%)
    pallas_call x13, Pallas kernels, call(): pl.pallas_call(kernel, grid=grid, out_shape=tuple(outs), in_specs=specs o...  28.2 us
    all_to_all x1, starting transfers between devices, shards(): lax.all_to_all(phases, 'tile', split_axis=0, concat_axis=0, tiled=True)  6.83 us
    all_to_all x1, starting transfers between devices, shards(): grad = lax.all_to_all(grad, 'tile', split_axis=0, concat_axis=0, tiled=True)  6.35 us
    unnamed x38, local copies, waits for them, and re-layouts  4.59 us
    ppermute x1, starting transfers between devices, shards(): lax.ppermute(edges[0], 'tile', [(i, i + 1) for i in range(tiles - 1)])  3.92 us
    ppermute x2, starting transfers between devices, from_peer(): lax.ppermute(value, 'ang', [((i + 2 * j) % ang, i) for i in range(ang)])  3.05 us
    ppermute x2, starting transfers between devices, to_peer(): lax.ppermute(value, 'ang', [(i, (i + 2 * j) % ang) for i in range(ang)])  2.1 us
    broadcast_in_dim x1, local copies, waits for them, and re-layouts, shards(): phases = jnp.broadcast_to(phase, (tiles, slices, length))  1.38 us
  transfers between devices with their start and end apart: 11, of which 2 were waited for; matrix products, arithmetic and copies ran while one was open for 0% of the time, Pallas kernels for 36%

profile of v5, /device:TPU:0, one launch (start us, length us, event | category | flops | bytes accessed | tf_op | source)
XLA Modules:
  0.0 61.6 jit_solution(7585354099625000742)
XLA Ops:
  0.6 1.4 %broadcast_in_dim.14 = f32[8,16,256]{2,1,0:T(8,128)} broadcast(f32[16,256]{1,0:T(8,128)} %bitcast.13), dimensions={1,2} | broadcast | bytes 147456 | tf_op jit(solution)/shard_map/broadcast_in_dim | solution.py:466
  2.0 0.5 collective-permute-start
  2.5 6.8 %all-to-all-start = ((f32[8,16,256]{2,1,0:T(8,128)}), f32[8,16,256]{2,1,0:T(8,128)S(1)}, u32[]{:S(2)}, u32[]{:S(2)}) async-start(f32[8,16,256]{2,1,0:T(8,128)} %broadcast_in_dim.14), calls=%async_computation | async-start | bytes 262144 | tf_op jit(solution)/shard_map/all_to_all | solution.py:468
  9.3 0.0 collective-permute-done.refs_2_.refs_3_.refs_4_
  9.3 0.0 copy-start
  9.3 1.2 %copy-done = f32[64,16,256]{2,1,0:T(8,128)S(1)} copy-done((f32[64,16,256]{2,1,0:T(8,128)S(1)}, f32[64,16,256]{2,1,0:T(8,128)}, u32[]{:S(2)}) %copy-start) | copy-done | bytes 1048600
  10.5 0.3 edges.1
  10.8 3.9 %collective-permute-start.1 = (bf16[128,256]{1,0:T(8,128)(2,1)S(1)}, bf16[128,256]{1,0:T(8,128)(2,1)S(1)}, u32[]{:S(2)}, u32[]{:S(2)}) collective-permute-start(bf16[128,256]{1,0:T(8,128)(2,1)S(1)} %get-tuple-element.39), channel_id=1, source_target_pairs={{0,1},{1,2},{2,3},{3,4},{4,5},{5,6},{6,7},{8,9},{9,10},{10,11},{11... | collective-permute-start | bytes 196616 | tf_op jit(solution)/shard_map/ppermute | solution.py:482
  14.7 1.6 %collective-permute-start.2 = (s32[1]{0:T(128)}, s32[1]{0:T(128)}, u32[]{:S(2)}, u32[]{:S(2)}) collective-permute-start(s32[1]{0:T(128)} %param.21), channel_id=1, source_target_pairs={{16,0},{24,8},{0,16},{8,24},{17,1},{25,9},{1,17},{9,25},{18,2},{26... | collective-permute-start | bytes 20 | tf_op jit(solution)/shard_map/ppermute | solution.py:451
  17.0 1.3 %collective-permute-start.3 = (bf16[128,256]{1,0:T(8,128)(2,1)S(1)}, bf16[128,256]{1,0:T(8,128)(2,1)S(1)}, u32[]{:S(2)}, u32[]{:S(2)}) collective-permute-start(bf16[128,256]{1,0:T(8,128)(2,1)S(1)} %get-tuple-element.42), channel_id=1, source_target_pairs={{1,0},{2,1},{3,2},{4,3},{5,4},{6,5},{7,6},{9,8},{10,9},{11,10},{12... | collective-permute-start | bytes 196616 | tf_op jit(solution)/shard_map/ppermute | solution.py:483
  18.3 0.3 collective-permute-done.2.refs_0_.refs_1_
  18.6 0.0 all-to-all-done
  18.6 0.0 collective-permute-done.1.refs_2_
  18.6 0.0 copy-done.7
  18.6 0.0 copy-done.8
  18.6 0.6 %copy-done.10 = s32[1,4]{1,0:T(1,128)S(1)} copy-done((s32[1,4]{1,0:T(1,128)S(1)}, s32[1,4]{1,0:T(1,128)}, u32[]{:S(2)}) %copy-start.10) | copy-done | bytes 40
  19.2 1.0 %copy-done.12 = bf16[2,2,256,256]{3,2,1,0:T(8,128)(2,1)S(1)} copy-done((bf16[2,2,256,256]{3,2,1,0:T(8,128)(2,1)S(1)}, bf16[2,2,256,256]{3,2,1,0:T(8,128)(2,1)}, u32[]{:S(2)}) %copy-start.12) | copy-done | bytes 524312
  20.3 3.7 %gradient.1 = bf16[8,16,256]{2,1,0:T(8,128)(2,1)} custom-call(s32[1,4]{1,0:T(1,128)S(1)} %copy-done.10, f32[128,256]{1,0:T(8,128)S(1)} %bitcast.12, f32[4,128,128]{2,1,0:T(8,128)S(1)} %bitcast.18, f32[128,128]{1,0:T(8,128)S(1)} %copy-done.8, f32[128,128]{1,0:T(8,128)S(1)} %copy-done.9, bf16[2,2,256,256]{3,2,1,0:T(8,128)(2,1)S(1)} %copy-done.12), custom_call_target="tpu_custom_call" | custom-call | flops 4294967296 | bytes 1048576 | tf_op jit(solution)/shard_map/gradient/pallas_call | solution.py:408
  24.0 0.0 collective-permute-done.3.refs_3_
  24.0 6.4 %all-to-all-start.1 = ((bf16[8,16,256]{2,1,0:T(8,128)(2,1)}), bf16[8,16,256]{2,1,0:T(8,128)(2,1)S(1)}, u32[]{:S(2)}, u32[]{:S(2)}) async-start(bf16[8,16,256]{2,1,0:T(8,128)(2,1)} %gradient.1), calls=%async_computation.1 | async-start | bytes 131072 | tf_op jit(solution)/shard_map/all_to_all | solution.py:498
  30.3 0.0 copy-start.13
  30.4 0.9 %copy-done.13 = bf16[4,256,128]{2,1,0:T(8,128)(2,1)S(1)} copy-done((bf16[4,256,128]{2,1,0:T(8,128)(2,1)S(1)}, bf16[4,256,128]{2,1,0:T(8,128)(2,1)}, u32[]{:S(2)}) %copy-start.13) | copy-done | bytes 262168
  31.3 5.0 %project_old.1 = (f32[16,256]{1,0:T(8,128)S(1)}, f32[16,64,256]{2,1,0:T(8,128)S(1)}, bf16[16,64,256]{2,1,0:T(8,128)(2,1)S(1)}, bf16[16,128,256]{2,1,0:T(8,128)(2,1)S(1)}) custom-call(s32[1]{0:T(128)} %collective-permute-done.2.refs_0_.refs_1_, f32[1024,256]{1,0:T(8,128)S(1)} %bitcast.10, f32[1024,256]{1,0:T(8,128)S(1)} %bitcast.11, ...), custom_call_target="tpu_custom_call" | custom-call | flops 3221225472 | bytes 1048576 | tf_op jit(solution)/shard_map/project_old/pallas_call | solution.py:408
  36.3 0.0 copy-start.15
  36.3 0.6 collective-permute-start.4
  36.9 3.2 %project_old_own.1.refs_1_ = f32[16,256]{1,0:T(8,128)S(1)} custom-call(bf16[16,128,256]{2,1,0:T(8,128)(2,1)S(1)} %get-tuple-element.47.refs_0_, bf16[4,256,256]{2,1,0:T(8,128)(2,1)S(1)} %copy-done.11, bf16[4,256,128]{2,1,0:T(8,128)(2,1)S(1)} %copy-done.13, s32[1]{0:T(128)S(6)} %copy.21.refs_3_.refs_0_), custom_call_target="tpu_custom_call" | custom-call | flops 3221225472 | bytes 1048576 | tf_op jit(solution)/shard_map/project_old_own/pallas_call | solution.py:408
  40.1 0.0 copy-start.3
  40.1 0.0 collective-permute-done.4.refs_0_
  40.1 0.2 line_step.1
  40.3 0.0 all-to-all-done.1.grad_ref
  40.3 0.7 %copy-done.3 = bf16[2,256,256]{2,1,0:T(8,128)(2,1)S(1)} copy-done((bf16[2,256,256]{2,1,0:T(8,128)(2,1)S(1)}, bf16[2,256,256]{2,1,0:T(8,128)(2,1)}, u32[]{:S(2)}) %copy-start.3) | copy-done | bytes 262168
  41.0 0.6 %phase_step.1 = (f32[16,256]{1,0:T(8,128)}, f32[16,256]{1,0:T(8,128)S(1)}) custom-call(bf16[8,16,256]{2,1,0:T(8,128)(2,1)S(1)} %all-to-all-done.1.grad_ref, f32[16,256]{1,0:T(8,128)S(1)} %get-tuple-element.48.phase_part_ref, f32[16,256]{1,0:T(8,128)S(1)} %get-tuple-element.49.resid_part_ref, bf16[2,256,256]{2,1,0:T(8,128)(2,1)S(1)} %copy-done.3), custom_call_target="tpu_custom_call" | custom-call | bytes 1048576 | tf_op jit(solution)/shard_map/phase_step/pallas_call | solution.py:408
  41.7 1.5 %collective-permute-start.5 = (f32[16,256]{1,0:T(8,128)S(1)}, f32[16,256]{1,0:T(8,128)S(1)}, u32[]{:S(2)}, u32[]{:S(2)}) collective-permute-start(f32[16,256]{1,0:T(8,128)S(1)} %get-tuple-element.56.refs_0_), channel_id=1, source_target_pairs={{16,0},{24,8},{0,16},{8,24},{17,1},{25,9},{1,17},{9,25},{18,2},{26... | collective-permute-start | bytes 49160 | tf_op jit(solution)/shard_map/ppermute | solution.py:451
  43.2 1.3 %turn_tables.1 = (f32[3,256,128]{2,1,0:T(8,128)S(1)}, f32[2,128,256]{2,1,0:T(8,128)S(1)}, f32[8,256]{1,0:T(8,128)S(1)}, f32[3,256,128]{2,1,0:T(8,128)S(1)}, f32[...) custom-call(s32[1]{0:T(128)S(6)} %copy.21.refs_3_.refs_0_, s32[1]{0:T(128)} %collective-permute-done.2.refs_0_.refs_1_), custom_call_target="tpu_custom_call" | custom-call | flops 2147483648 | bytes 1048576 | tf_op jit(solution)/shard_map/turn_tables/pallas_call | solution.py:408
  44.5 0.9 %collective-permute-done.5.refs_1_ = f32[16,256]{1,0:T(8,128)S(1)} collective-permute-done((f32[16,256]{1,0:T(8,128)S(1)}, f32[16,256]{1,0:T(8,128)S(1)}, u32[]{:S(2)}, u32[]{:S(2)}) %collective-permute-start.5) | collective-permute-done | bytes 16416 | tf_op jit(solution)/shard_map/ppermute | solution.py:451
  45.4 2.5 %backproject.3.refs_4_ = bf16[8,128,256]{2,1,0:T(8,128)(2,1)S(1)} custom-call(f32[16,256]{1,0:T(8,128)S(1)} %get-tuple-element.56.refs_0_, f32[16,256]{1,0:T(8,128)S(1)} %collective-permute-done.5.refs_1_, bf16[4,256,256]{2,1,0:T(8,128)(2,1)S(1)} %copy-done.11, bf16[4,128,256]{2,1,0:T(8,128)(2,1)S(1)} %copy-done.14, ...), custom_call_target="tpu_custom_call" | custom-call | flops 3221225472 | bytes 1048576 | tf_op jit(solution)/shard_map/backproject/pallas_call | solution.py:408
  47.9 0.0 copy-start.16
  48.0 0.1 collective-permute-start.7
  48.0 2.8 %backproject.2.refs_4_ = bf16[8,128,256]{2,1,0:T(8,128)(2,1)S(1)} custom-call(f32[16,256]{1,0:T(8,128)S(1)} %get-tuple-element.56.refs_0_, f32[16,256]{1,0:T(8,128)S(1)} %collective-permute-done.5.refs_1_, bf16[4,256,256]{2,1,0:T(8,128)(2,1)S(1)} %copy-done.11, bf16[4,128,256]{2,1,0:T(8,128)(2,1)S(1)} %copy-done.14, ...), custom_call_target="tpu_custom_call" | custom-call | flops 3221225472 | bytes 1048576 | tf_op jit(solution)/shard_map/backproject/pallas_call | solution.py:408
  50.8 0.6 collective-permute-start.6
  51.4 0.0 collective-permute-done.7.refs_5_
  51.4 2.7 %project_new.2 = (f32[64,16,256]{2,1,0:T(8,128)}, bf16[8,128,256]{2,1,0:T(8,128)(2,1)S(1)}, f32[16,256]{1,0:T(8,128)S(1)}) custom-call(f32[16,64,256]{2,1,0:T(8,128)S(1)} %copy-done.16, bf16[16,64,256]{2,1,0:T(8,128)(2,1)S(1)} %copy-done.18, bf16[128,256]{1,0:T(8,128)(2,1)S(1)} %collective-permute-done.1.refs_2_, ...), custom_call_target="tpu_custom_call" | custom-call | flops 1610612736 | bytes 1048576 | tf_op jit(solution)/shard_map/project_new/pallas_call | solution.py:408
  54.0 0.0 collective-permute-done.6.refs_5_
  54.0 2.1 %project_new.3 = (f32[64,16,256]{2,1,0:T(8,128)}, bf16[8,128,256]{2,1,0:T(8,128)(2,1)S(1)}, f32[16,256]{1,0:T(8,128)S(1)}) custom-call(f32[16,64,256]{2,1,0:T(8,128)S(1)} %copy-done.16, bf16[16,64,256]{2,1,0:T(8,128)(2,1)S(1)} %copy-done.18, bf16[128,256]{1,0:T(8,128)(2,1)S(1)} %collective-permute-done.1.refs_2_, ...), custom_call_target="tpu_custom_call", output_to_operand_aliasing={{0}: (11, {}), {2}: (12, {})} | custom-call | flops 1610612736 | bytes 1048576 | tf_op jit(solution)/shard_map/project_new/pallas_call | solution.py:408
  56.1 1.5 %collective-permute-start.8 = (f32[16,256]{1,0:T(8,128)S(1)}, f32[16,256]{1,0:T(8,128)S(1)}, u32[]{:S(2)}, u32[]{:S(2)}) collective-permute-start(f32[16,256]{1,0:T(8,128)S(1)} %get-tuple-element.68), channel_id=1, source_target_pairs={{0,16},{8,24},{16,0},{24,8},{1,17},{9,25},{17,1},{25,9},{2,18},{10... | collective-permute-start | bytes 49160 | tf_op jit(solution)/shard_map/ppermute | solution.py:454
  57.6 3.2 %project_new_own.1.refs_1_ = f32[16,256]{1,0:T(8,128)S(1)} custom-call(bf16[8,128,256]{2,1,0:T(8,128)(2,1)S(1)} %get-tuple-element.69.refs_0_, bf16[8,128,256]{2,1,0:T(8,128)(2,1)S(1)} %get-tuple-element.70.refs_1_, bf16[4,256,256]{2,1,0:T(8,128)(2,1)S(1)} %copy-done.11, bf16[4,256,128]{2,1,0:T(8,128)(2,1)S(1)} %copy-done.13, ...), custom_call_target="tpu_custom_call" | custom-call | flops 3221225472 | bytes 1048576 | tf_op jit(solution)/shard_map/project_new_own/pallas_call | solution.py:408
  60.8 0.0 collective-permute-done.8.refs_0_
  60.8 0.8 %dual_step.1 = f32[16,256]{1,0:T(8,128)} custom-call(f32[16,256]{1,0:T(8,128)S(1)} %copy-done.6, f32[16,256]{1,0:T(8,128)S(1)} %bitcast.16, bf16[2,256,256]{2,1,0:T(8,128)(2,1)S(1)} %copy-done.2, f32[16,256]{1,0:T(8,128)S(1)} %collective-permute-done.8.refs_0_, f32[16,256]{1,0:T(8,128)S(1)} %project_new_own.1.refs_1_), custom_call_target="tpu_custom_call" | custom-call | bytes 1048576 | tf_op jit(solution)/shard_map/dual_step/pallas_call | solution.py:408
  (26 shorter events, 0.0 us)
Async XLA Ops:
  2.0 7.3 %collective-permute-start = (f32[1024,256]{1,0:T(8,128)}, f32[1024,256]{1,0:T(8,128)S(1)}, u32[]{:S(2)}, u32[]{:S(2)}) collective-permute-start(f32[1024,256]{1,0:T(8,128)} %bitcast.7), channel_id=1, source_target_pairs={{0,8},{8,0},{16,24},{24,16},{1,9},{9,1},{17,25},{25,17},{2,10},{10... | collective-permute-start | bytes 3145736 | tf_op jit(solution)/shard_map/ppermute | solution.py:448
  2.5 16.1 %all-to-all-start = ((f32[8,16,256]{2,1,0:T(8,128)}), f32[8,16,256]{2,1,0:T(8,128)S(1)}, u32[]{:S(2)}, u32[]{:S(2)}) async-start(f32[8,16,256]{2,1,0:T(8,128)} %broadcast_in_dim.14), calls=%async_computation | async-start | bytes 262144 | tf_op jit(solution)/shard_map/all_to_all | solution.py:468
  9.3 1.2 %copy-start = (f32[64,16,256]{2,1,0:T(8,128)S(1)}, f32[64,16,256]{2,1,0:T(8,128)}, u32[]{:S(2)}) copy-start(f32[64,16,256]{2,1,0:T(8,128)} %param.14) | copy-start | bytes 3145732
  10.5 8.1 %copy-start.7 = (f32[1,4,128,128]{3,2,1,0:T(8,128)S(1)}, f32[1,4,128,128]{3,2,1,0:T(8,128)}, u32[]{:S(2)}) copy-start(f32[1,4,128,128]{3,2,1,0:T(8,128)} %param.19) | copy-start | bytes 786436
  10.5 8.1 %copy-start.8 = (f32[128,128]{1,0:T(8,128)S(1)}, f32[128,128]{1,0:T(8,128)}, u32[]{:S(2)}) copy-start(f32[128,128]{1,0:T(8,128)} %probe_r_ref.1) | copy-start | bytes 196612
  10.5 8.1 %copy-start.9 = (f32[128,128]{1,0:T(8,128)S(1)}, f32[128,128]{1,0:T(8,128)}, u32[]{:S(2)}) copy-start(f32[128,128]{1,0:T(8,128)} %probe_i_ref.1) | copy-start | bytes 196612
  10.8 7.8 %collective-permute-start.1 = (bf16[128,256]{1,0:T(8,128)(2,1)S(1)}, bf16[128,256]{1,0:T(8,128)(2,1)S(1)}, u32[]{:S(2)}, u32[]{:S(2)}) collective-permute-start(bf16[128,256]{1,0:T(8,128)(2,1)S(1)} %get-tuple-element.39), channel_id=1, source_target_pairs={{0,1},{1,2},{2,3},{3,4},{4,5},{5,6},{6,7},{8,9},{9,10},{10,11},{11... | collective-permute-start | bytes 196616 | tf_op jit(solution)/shard_map/ppermute | solution.py:482
  14.7 3.8 %collective-permute-start.2 = (s32[1]{0:T(128)}, s32[1]{0:T(128)}, u32[]{:S(2)}, u32[]{:S(2)}) collective-permute-start(s32[1]{0:T(128)} %param.21), channel_id=1, source_target_pairs={{16,0},{24,8},{0,16},{8,24},{17,1},{25,9},{1,17},{9,25},{18,2},{26... | collective-permute-start | bytes 20 | tf_op jit(solution)/shard_map/ppermute | solution.py:451
  17.0 7.0 %collective-permute-start.3 = (bf16[128,256]{1,0:T(8,128)(2,1)S(1)}, bf16[128,256]{1,0:T(8,128)(2,1)S(1)}, u32[]{:S(2)}, u32[]{:S(2)}) collective-permute-start(bf16[128,256]{1,0:T(8,128)(2,1)S(1)} %get-tuple-element.42), channel_id=1, source_target_pairs={{1,0},{2,1},{3,2},{4,3},{5,4},{6,5},{7,6},{9,8},{10,9},{11,10},{12... | collective-permute-start | bytes 196616 | tf_op jit(solution)/shard_map/ppermute | solution.py:483
  18.6 0.7 %copy-start.10 = (s32[1,4]{1,0:T(1,128)S(1)}, s32[1,4]{1,0:T(1,128)}, u32[]{:S(2)}) copy-start(s32[1,4]{1,0:T(1,128)} %offsets_ref.1) | copy-start | bytes 52
  19.2 1.0 %copy-start.12 = (bf16[2,2,256,256]{3,2,1,0:T(8,128)(2,1)S(1)}, bf16[2,2,256,256]{3,2,1,0:T(8,128)(2,1)}, u32[]{:S(2)}) copy-start(bf16[2,2,256,256]{3,2,1,0:T(8,128)(2,1)} %constant.12.clone.const_hbm_ref) | copy-start | bytes 1572868
  20.3 10.0 %copy-start.1 = (f32[64,16,256]{2,1,0:T(8,128)S(1)}, f32[64,16,256]{2,1,0:T(8,128)}, u32[]{:S(2)}) copy-start(f32[64,16,256]{2,1,0:T(8,128)} %param.14) | copy-start | bytes 3145732
  20.3 10.1 %copy-start.11 = (bf16[4,256,256]{2,1,0:T(8,128)(2,1)S(1)}, bf16[4,256,256]{2,1,0:T(8,128)(2,1)}, u32[]{:S(2)}) copy-start(bf16[4,256,256]{2,1,0:T(8,128)(2,1)} %constant.13.clone.refs_5_.refs_1_.refs_2_.refs_6_) | copy-start | bytes 1572868
  24.0 16.4 %all-to-all-start.1 = ((bf16[8,16,256]{2,1,0:T(8,128)(2,1)}), bf16[8,16,256]{2,1,0:T(8,128)(2,1)S(1)}, u32[]{:S(2)}, u32[]{:S(2)}) async-start(bf16[8,16,256]{2,1,0:T(8,128)(2,1)} %gradient.1), calls=%async_computation.1 | async-start | bytes 131072 | tf_op jit(solution)/shard_map/all_to_all | solution.py:498
  30.3 1.0 %copy-start.13 = (bf16[4,256,128]{2,1,0:T(8,128)(2,1)S(1)}, bf16[4,256,128]{2,1,0:T(8,128)(2,1)}, u32[]{:S(2)}) copy-start(bf16[4,256,128]{2,1,0:T(8,128)(2,1)} %constant.14.clone.refs_6_.refs_2_.refs_7_.refs_3_) | copy-start | bytes 786436
  36.3 3.8 %copy-start.15 = (f32[16,64,256]{2,1,0:T(8,128)}, f32[16,64,256]{2,1,0:T(8,128)S(1)}, u32[]{:S(2)}) copy-start(f32[16,64,256]{2,1,0:T(8,128)S(1)} %get-tuple-element.51.refs_0_) | copy-start | bytes 3145732
  36.3 3.8 %copy-start.17 = (bf16[16,64,256]{2,1,0:T(8,128)(2,1)}, bf16[16,64,256]{2,1,0:T(8,128)(2,1)S(1)}, u32[]{:S(2)}) copy-start(bf16[16,64,256]{2,1,0:T(8,128)(2,1)S(1)} %get-tuple-element.52.refs_1_) | copy-start | bytes 1572868
  36.3 3.8 %collective-permute-start.4 = (f32[16,256]{1,0:T(8,128)S(1)}, f32[16,256]{1,0:T(8,128)S(1)}, u32[]{:S(2)}, u32[]{:S(2)}) collective-permute-start(f32[16,256]{1,0:T(8,128)S(1)} %get-tuple-element.46), channel_id=1, source_target_pairs={{0,16},{8,24},{16,0},{24,8},{1,17},{9,25},{17,1},{25,9},{2,18},{10... | collective-permute-start | bytes 49160 | tf_op jit(solution)/shard_map/ppermute | solution.py:454
  36.9 3.2 %copy-start.2 = (bf16[2,256,256]{2,1,0:T(8,128)(2,1)S(1)}, bf16[2,256,256]{2,1,0:T(8,128)(2,1)}, u32[]{:S(2)}) copy-start(bf16[2,256,256]{2,1,0:T(8,128)(2,1)} %constant.15.clone.inverse_ref) | copy-start | bytes 786436
  36.9 3.2 %copy-start.4 = (f32[1,16,256]{2,1,0:T(8,128)S(1)}, f32[1,16,256]{2,1,0:T(8,128)}, u32[]{:S(2)}) copy-start(f32[1,16,256]{2,1,0:T(8,128)} %param.15) | copy-start | bytes 49156
  36.9 3.2 %copy-start.5 = (f32[1,16,256]{2,1,0:T(8,128)S(1)}, f32[1,16,256]{2,1,0:T(8,128)}, u32[]{:S(2)}) copy-start(f32[1,16,256]{2,1,0:T(8,128)} %param.16) | copy-start | bytes 49156
  40.1 1.0 %copy-start.3 = (bf16[2,256,256]{2,1,0:T(8,128)(2,1)S(1)}, bf16[2,256,256]{2,1,0:T(8,128)(2,1)}, u32[]{:S(2)}) copy-start(bf16[2,256,256]{2,1,0:T(8,128)(2,1)} %constant.16.clone.forward_ref) | copy-start | bytes 786436
  41.7 3.7 %copy-start.14 = (bf16[4,128,256]{2,1,0:T(8,128)(2,1)S(1)}, bf16[4,128,256]{2,1,0:T(8,128)(2,1)}, u32[]{:S(2)}) copy-start(bf16[4,128,256]{2,1,0:T(8,128)(2,1)} %constant.17.clone.refs_3_) | copy-start | bytes 786436
  41.7 3.7 %collective-permute-start.5 = (f32[16,256]{1,0:T(8,128)S(1)}, f32[16,256]{1,0:T(8,128)S(1)}, u32[]{:S(2)}, u32[]{:S(2)}) collective-permute-start(f32[16,256]{1,0:T(8,128)S(1)} %get-tuple-element.56.refs_0_), channel_id=1, source_target_pairs={{16,0},{24,8},{0,16},{8,24},{17,1},{25,9},{1,17},{9,25},{18,2},{26... | collective-permute-start | bytes 49160 | tf_op jit(solution)/shard_map/ppermute | solution.py:451
  47.9 3.4 %copy-start.16 = (f32[16,64,256]{2,1,0:T(8,128)S(1)}, f32[16,64,256]{2,1,0:T(8,128)}, u32[]{:S(2)}) copy-start(f32[16,64,256]{2,1,0:T(8,128)} %copy-done.15) | copy-start | bytes 3145732
  47.9 3.4 %copy-start.18 = (bf16[16,64,256]{2,1,0:T(8,128)(2,1)S(1)}, bf16[16,64,256]{2,1,0:T(8,128)(2,1)}, u32[]{:S(2)}) copy-start(bf16[16,64,256]{2,1,0:T(8,128)(2,1)} %copy-done.17) | copy-start | bytes 1572868
  48.0 3.4 %collective-permute-start.7 = (bf16[8,128,256]{2,1,0:T(8,128)(2,1)S(1)}, bf16[8,128,256]{2,1,0:T(8,128)(2,1)S(1)}, u32[]{:S(2)}, u32[]{:S(2)}) collective-permute-start(bf16[8,128,256]{2,1,0:T(8,128)(2,1)S(1)} %backproject.3.refs_4_), channel_id=1, source_target_pairs={{0,8},{8,0},{16,24},{24,16},{1,9},{9,1},{17,25},{25,17},{2,10},{10... | collective-permute-start | bytes 1572872 | tf_op jit(solution)/shard_map/ppermute | solution.py:448
  50.8 3.2 %collective-permute-start.6 = (bf16[8,128,256]{2,1,0:T(8,128)(2,1)S(1)}, bf16[8,128,256]{2,1,0:T(8,128)(2,1)S(1)}, u32[]{:S(2)}, u32[]{:S(2)}) collective-permute-start(bf16[8,128,256]{2,1,0:T(8,128)(2,1)S(1)} %backproject.2.refs_4_), channel_id=1, source_target_pairs={{0,8},{8,0},{16,24},{24,16},{1,9},{9,1},{17,25},{25,17},{2,10},{10... | collective-permute-start | bytes 1572872 | tf_op jit(solution)/shard_map/ppermute | solution.py:448
  56.1 4.7 %collective-permute-start.8 = (f32[16,256]{1,0:T(8,128)S(1)}, f32[16,256]{1,0:T(8,128)S(1)}, u32[]{:S(2)}, u32[]{:S(2)}) collective-permute-start(f32[16,256]{1,0:T(8,128)S(1)} %get-tuple-element.68), channel_id=1, source_target_pairs={{0,16},{8,24},{16,0},{24,8},{1,17},{9,25},{17,1},{25,9},{2,18},{10... | collective-permute-start | bytes 49160 | tf_op jit(solution)/shard_map/ppermute | solution.py:454
  57.6 3.2 %copy-start.6 = (f32[16,256]{1,0:T(8,128)S(1)}, f32[16,256]{1,0:T(8,128)}, u32[]{:S(2)}) copy-start(f32[16,256]{1,0:T(8,128)} %get-tuple-element.50.phase_ref) | copy-start | bytes 49156

commit v6 on v5

--- a/solution.py
+++ b/solution.py
@@ -52,11 +52,8 @@
 
 def patch_tables(width):
     cos_t, sin_t = table_pair(width)
-    c = cos_t / np.float32(math.sqrt(width))
-    s = sin_t / np.float32(math.sqrt(width))
-    right = np.block([[c, -s], [s, c]])
-    left = np.block([[c, s], [-s, c]])
-    return split_pair(right.astype(np.float32)), split_pair(left.astype(np.float32))
+    scale = np.float32(math.sqrt(width))
+    return np.stack([split_pair(cos_t / scale), split_pair(sin_t / scale)], axis=1)
 
 
 def dot(left, right):
@@ -69,7 +66,7 @@
 
 def dot_split(left, right):
     def parts(value):
-        if value.dtype == BF16:
+        if isinstance(value, list) or value.dtype == BF16:
             return value[0], value[1]
         high = value.astype(BF16)
         return high, (value - high.astype(F32)).astype(BF16)
@@ -213,6 +210,10 @@
         fill_turn_tables(angle_refs[g][0], row_ref.shape[1], row_ref, col_ref, nyq_ref)
 
 
+def copies_kernel(phase_ref, out_ref):
+    out_ref[...] = jnp.broadcast_to(phase_ref[...][None], out_ref.shape)
+
+
 def edge_kernel(slices, *refs):
     sides, edges = take(refs, 4, 2)
     share = sides[0].shape[0] // slices
@@ -250,9 +251,9 @@
     project_slices(slab, slices, share, as_tables(table_refs), consts, lines_refs)
 
 
-def own_line_kernel(pieces, made, *refs):
-    slabs, (const_ref, down_ref), given, (line_ref,), table_refs = take(
-        refs, pieces, 2, 3 if made else 1, 1, 0 if made else 3
+def own_line_kernel(pieces, made, aliased, *refs):
+    slabs, (const_ref, down_ref), given, unused, (line_ref,), table_refs = take(
+        refs, pieces, 2, 3 if made else 1, aliased, 1, 0 if made else 3
     )
     if not made:
         tables_kernel(1, *given, *table_refs)
@@ -291,8 +292,8 @@
 
 
 def update_kernel(groups, first, last, aliased, *refs):
-    bases, halos, shares, (const_ref, down_ref), table_refs, unused, (volume_ref, slab_ref), lines_refs, sides = take(
-        refs, 2, 2, 2, 2, 3 * groups, aliased, 2, groups, 2
+    bases, halos, shares, (const_ref, down_ref), table_refs, unused, (volume_ref,), lines_refs, slabs, sides = take(
+        refs, 2, 2, 2, 2, 3 * groups, aliased, 1, groups, 1 if last else 0, 2
     )
     consts = [const_ref.at[0], const_ref.at[1], down_ref, const_ref.at[3]]
     own_ref, other_ref = bases
@@ -315,7 +316,8 @@
             sides[side][pl.ds(z, share, stride=slices), :] = own[:, side * half : (side + 1) * half]
         slab += [own.astype(BF16), other.astype(BF16)]
     slab = jnp.concatenate(slab, axis=0)
-    slab_ref[...] = slab.reshape(slab_ref.shape)
+    for slab_ref in slabs:
+        slab_ref[...] = slab.reshape(slab_ref.shape)
     project_slices(slab, slices, share, as_tables(table_refs), consts, lines_refs)
     whole = jnp.concatenate([ref[...] for ref in sides], axis=1)
     volume_ref[...] = whole.reshape(volume_ref.shape)
@@ -323,12 +325,15 @@
 
 def gradient_kernel(
     offsets_ref, image_ref, measured_ref, probe_r_ref, probe_i_ref,
-    const_hbm_ref, out_ref, const_ref, sem,
+    const_ref, out_ref,
 ):
-    fetch = pltpu.make_async_copy(const_hbm_ref, const_ref, sem)
-    fetch.start()
-    right_ref, left_ref = const_ref.at[0], const_ref.at[1]
-    left_conj_ref, right_conj_ref = right_ref, left_ref
+    right, left = [], []
+    for part in range(2):
+        c, s = const_ref[part, 0], const_ref[part, 1]
+        plus = [jnp.concatenate([c, s], axis=1), jnp.concatenate([-s, c], axis=1)]
+        minus = [jnp.concatenate([c, -s], axis=1), jnp.concatenate([s, c], axis=1)]
+        left.append(jnp.concatenate(plus, axis=0))
+        right.append(jnp.concatenate(minus, axis=0))
     positions, height, width = measured_ref.shape
     length = image_ref.shape[1]
     image = image_ref[...]
@@ -336,7 +341,7 @@
     probe_r, probe_i = probe_r_ref[...], probe_i_ref[...]
     waves = []
     for p in range(positions):
-        back = length - offsets_ref[0, p]
+        back = length - offsets_ref[p]
         cos_p = pltpu.roll(cos_image, back, 1)[:, :width]
         sin_p = pltpu.roll(sin_image, back, 1)[:, :width]
         waves.append((probe_r * cos_p - probe_i * sin_p, probe_r * sin_p + probe_i * cos_p))
@@ -355,20 +360,19 @@
         )
 
     entry = jnp.concatenate([jnp.concatenate(wave, axis=1) for wave in waves], axis=0)
-    fetch.wait()
-    far = dot_split(left_ref[...], to_columns(dot_split(entry, right_ref[...])))
+    far = dot_split(left, to_columns(dot_split(entry, right)))
     far_r, far_i = far[:height], far[height:]
     measured = jnp.concatenate([measured_ref[p] for p in range(positions)], axis=1)
     misfit = far_r * far_r + far_i * far_i - measured
     weighted = jnp.concatenate([misfit * far_r, misfit * far_i], axis=0)
-    chi = dot_split(to_rows(dot_split(left_conj_ref[...], weighted)), right_conj_ref[...])
+    chi = dot_split(to_rows(dot_split(right, weighted)), left)
     total = jnp.zeros((height, length), F32)
     for p in range(positions):
         part = block_of(chi, p, positions, 0)
         wave_r, wave_i = waves[p]
         term = 2.0 * (part[:, width:] * wave_r - part[:, :width] * wave_i)
         padded = jnp.concatenate([term, jnp.zeros((height, length - width), F32)], axis=1)
-        total = total + pltpu.roll(padded, offsets_ref[0, p], 1)
+        total = total + pltpu.roll(padded, offsets_ref[p], 1)
     out_ref[...] = total.astype(out_ref.dtype).reshape(out_ref.shape)
 
 
@@ -440,7 +444,6 @@
     down_part = np.stack([down[:, rows] for rows in owners])
     up_part = np.stack([up[rows] for rows in owners])
     square = np.stack([forward, inverse, down, up])
-    right, left = patch_tables(width)
     line = shape((slices, length), F32)
     work = 2 * 2 * length * length * length * slices * groups
 
@@ -463,7 +466,7 @@
         pl.BlockSpec((some, length), functools.partial(lambda h, _: (h, 0), h)) for h in range(parts)
     ]
 
-    phases = jnp.broadcast_to(phase, (tiles, slices, length))
+    (phases,) = call(copies_kernel, [shape((tiles, slices, length), F32)], [phase[0]], name="phase_copies")
     phases, volume, angle_sent = lax.optimization_barrier((phases, volume, angle_index))
     image = lax.all_to_all(phases, "tile", split_axis=0, concat_axis=0, tiled=True)
     image = image.reshape(tiles * slices, length)
@@ -487,9 +490,8 @@
     (grad,) = call(
         gradient_kernel,
         [shape((tiles, slices, length), BF16)],
-        [offsets, image, intensity[0], probe_real, probe_imag, np.stack([right, left])],
-        [SMEM_SPEC] + [VMEM_SPEC] * 4 + [pl.BlockSpec(memory_space=pl.ANY)],
-        scratch=[pltpu.VMEM((2,) + right.shape, BF16), pltpu.SemaphoreType.DMA],
+        [offsets[0], image, intensity[0], probe_real, probe_imag, patch_tables(width)],
+        [SMEM_SPEC] + [VMEM_SPEC] * 5,
         flops=2 * work,
         vmem=12,
         name="gradient",
@@ -514,7 +516,7 @@
     lines, bases, slab = take(outs, far, 2, 1)
     old = [to_peer(lines[j], j + 1) for j in range(far)]
     old += call(
-        functools.partial(own_line_kernel, 1, False),
+        functools.partial(own_line_kernel, 1, False, 0),
         [line],
         slab + [square, down_part, angle_index],
         [VMEM_SPEC] * 3 + [SMEM_SPEC],
@@ -553,34 +555,46 @@
         )
         halves.append((mine, swap(mine)))
 
-    results, slabs = [], []
+    results = []
     for h in range(parts):
-        args = bases + [before, after] + list(halves[h]) + [square, down_part] + tables[3:]
+        last = h == parts - 1
+        count = far if last else groups
+        args = bases + [before, after] + list(halves[h]) + [square, down_part]
+        args = args + (tables[3:] if last else tables[3:] + tables[:3])
+        carried = results[: 1 + count]
         outs = call(
-            functools.partial(update_kernel, far, h == 0, h == parts - 1, len(results)),
-            [shape((share, slices, length), F32), shape((some, pair, length), BF16)] + [line] * far,
-            args + results,
+            functools.partial(update_kernel, count, h == 0, last, len(carried)),
+            [shape((share, slices, length), F32)]
+            + [line] * count
+            + ([shape((some, pair, length), BF16)] if last else []),
+            args + carried,
             [pl.BlockSpec((some, share, length), lambda _, h=h: (h, 0, 0))] * 2
-            + [VMEM_SPEC] * (len(args) - 2) + [pl.BlockSpec(memory_space=pl.ANY)] * len(results),
-            [pl.BlockSpec((share, some, length), lambda _, h=h: (0, h, 0)), VMEM_SPEC]
-            + [block_lines[h]] * far,
+            + [VMEM_SPEC] * (len(args) - 2) + [pl.BlockSpec(memory_space=pl.ANY)] * len(carried),
+            [pl.BlockSpec((share, some, length), lambda _, h=h: (0, h, 0))]
+            + [block_lines[h]] * count
+            + ([VMEM_SPEC] if last else []),
             scratch=[pltpu.VMEM((share * some, half), F32)] * 2,
             grid=(1,),
-            flops=3 * work * far // groups // parts,
+            flops=3 * work * count // groups // parts,
             vmem=24,
-            aliases={len(args) + i: i + (1 if i else 0) for i in range(len(results))},
+            aliases={len(args) + i: i for i in range(len(carried))},
             name="project_new",
         )
-        slabs.append(outs[1])
-        results = [outs[0]] + list(outs[2:])
-    volume_new, lines = results[0], results[1:]
+        results = list(outs[: 1 + count]) + results[1 + count :]
+    volume_new, lines, slab = results[0], results[1:groups], outs[-1]
     new = [to_peer(lines[j], j + 1) for j in range(far)]
+    own_line = results[groups:]
+    args = [slab, square, down_part] + tables[:3] + own_line
     new += call(
-        functools.partial(own_line_kernel, parts, True),
+        functools.partial(own_line_kernel, 1, True, len(own_line)),
         [line],
-        slabs + [square, down_part] + tables[:3],
-        flops=3 * work // groups,
+        args,
+        [VMEM_SPEC] * 6 + [pl.BlockSpec(memory_space=pl.ANY)] * len(own_line),
+        [block_lines[parts - 1]],
+        grid=(1,),
+        flops=3 * work // groups // parts,
         vmem=24,
+        aliases={6: 0} if own_line else None,
         name="project_new_own",
     )
     (dual_new,) = call(

time: 62.2 us -> 60.3 us (0.969)
  local copies, waits for them, and re-layouts: 5.97 us -> 4.25 us
  waiting for transfers between devices: 1.27 us -> 2.25 us
  Pallas kernels: 28.2 us -> 27.5 us
    broadcast_in_dim x1 -> x0, local copies, waits for them, and re-layouts: 1.38 us -> none  [shards(): phases = jnp.broadcast_to(phase, (tiles, slices, length))]
    pallas_call x13 -> x14, Pallas kernels: 28.2 us -> 27.5 us  [call(): pl.pallas_call(kernel, grid=grid, out_shape=tuple(outs), in_specs=specs o...]
    unnamed x38 -> x40, local copies, waits for them, and re-layouts: 4.59 us -> 4.25 us
  transfers between devices with their start and end apart: 11 -> 11, of which waited for: 2 -> 4; matrix products, arithmetic and copies ran while one was open for 0% -> 0% of each run, Pallas kernels for 36% -> 35%
where the time goes in v6:
time: 60.3 us; the launch traced here: 59.7 us
  Pallas kernels  27.5 us (46%)
  starting transfers between devices  24.2 us (40%)
  local copies, waits for them, and re-layouts  4.25 us (7%)
  waiting for transfers between devices  2.25 us (4%)
  between operations  1.58 us (3%)
    pallas_call x14, Pallas kernels, call(): pl.pallas_call(kernel, grid=grid, out_shape=tuple(outs), in_specs=specs o...  27.5 us
    all_to_all x1, starting transfers between devices, shards(): lax.all_to_all(phases, 'tile', split_axis=0, concat_axis=0, tiled=True)  6.83 us
    all_to_all x1, starting transfers between devices, shards(): grad = lax.all_to_all(grad, 'tile', split_axis=0, concat_axis=0, tiled=True)  5.92 us
    unnamed x40, local copies, waits for them, and re-layouts  4.25 us
    ppermute x1, starting transfers between devices, shards(): lax.ppermute(edges[0], 'tile', [(i, i + 1) for i in range(tiles - 1)])  3.92 us
    ppermute x2, starting transfers between devices, from_peer(): lax.ppermute(value, 'ang', [((i + 2 * j) % ang, i) for i in range(ang)])  3.05 us
    ppermute x2, starting transfers between devices, to_peer(): lax.ppermute(value, 'ang', [(i, (i + 2 * j) % ang) for i in range(ang)])  2.09 us
    ppermute x2, waiting for transfers between devices, from_peer(): lax.ppermute(value, 'ang', [((i + 2 * j) % ang, i) for i in range(ang)])  1.31 us
  transfers between devices with their start and end apart: 11, of which 4 were waited for; matrix products, arithmetic and copies ran while one was open for 0% of the time, Pallas kernels for 35%

profile of v6, /device:TPU:0, one launch (start us, length us, event | category | flops | bytes accessed | tf_op | source)
XLA Modules:
  0.0 59.7 jit_solution(9034481529678438040)
XLA Ops:
  0.6 0.0 copy-start.4
  0.6 0.7 %copy-done.4 = f32[1,16,256]{2,1,0:T(8,128)S(1)} copy-done((f32[1,16,256]{2,1,0:T(8,128)S(1)}, f32[1,16,256]{2,1,0:T(8,128)}, u32[]{:S(2)}) %copy-start.4) | copy-done | bytes 16408
  1.4 0.7 %phase_copies.1 = f32[8,16,256]{2,1,0:T(8,128)} custom-call(f32[16,256]{1,0:T(8,128)S(1)} %bitcast.14), custom_call_target="tpu_custom_call" | custom-call | bytes 1048576 | tf_op jit(solution)/shard_map/phase_copies/pallas_call | solution.py:412
  2.0 0.5 collective-permute-start
  2.5 6.8 %all-to-all-start = ((f32[8,16,256]{2,1,0:T(8,128)}), f32[8,16,256]{2,1,0:T(8,128)S(1)}, u32[]{:S(2)}, u32[]{:S(2)}) async-start(f32[8,16,256]{2,1,0:T(8,128)} %phase_copies.1), calls=%async_computation | async-start | bytes 262144 | tf_op jit(solution)/shard_map/all_to_all | solution.py:471
  9.3 0.0 collective-permute-done.refs_2_.refs_3_.refs_4_
  9.3 0.0 copy-start
  9.3 1.2 %copy-done = f32[64,16,256]{2,1,0:T(8,128)S(1)} copy-done((f32[64,16,256]{2,1,0:T(8,128)S(1)}, f32[64,16,256]{2,1,0:T(8,128)}, u32[]{:S(2)}) %copy-start) | copy-done | bytes 1048600
  10.5 0.3 edges.1
  10.8 3.9 %collective-permute-start.1 = (bf16[128,256]{1,0:T(8,128)(2,1)S(1)}, bf16[128,256]{1,0:T(8,128)(2,1)S(1)}, u32[]{:S(2)}, u32[]{:S(2)}) collective-permute-start(bf16[128,256]{1,0:T(8,128)(2,1)S(1)} %get-tuple-element.39), channel_id=1, source_target_pairs={{0,1},{1,2},{2,3},{3,4},{4,5},{5,6},{6,7},{8,9},{9,10},{10,11},{11... | collective-permute-start | bytes 196616 | tf_op jit(solution)/shard_map/ppermute | solution.py:485
  14.7 1.6 %collective-permute-start.2 = (s32[1]{0:T(128)}, s32[1]{0:T(128)}, u32[]{:S(2)}, u32[]{:S(2)}) collective-permute-start(s32[1]{0:T(128)} %param.21), channel_id=1, source_target_pairs={{16,0},{24,8},{0,16},{8,24},{17,1},{25,9},{1,17},{9,25},{18,2},{26... | collective-permute-start | bytes 20 | tf_op jit(solution)/shard_map/ppermute | solution.py:454
  17.0 1.3 %collective-permute-start.3 = (bf16[128,256]{1,0:T(8,128)(2,1)S(1)}, bf16[128,256]{1,0:T(8,128)(2,1)S(1)}, u32[]{:S(2)}, u32[]{:S(2)}) collective-permute-start(bf16[128,256]{1,0:T(8,128)(2,1)S(1)} %get-tuple-element.42), channel_id=1, source_target_pairs={{1,0},{2,1},{3,2},{4,3},{5,4},{6,5},{7,6},{9,8},{10,9},{11,10},{12... | collective-permute-start | bytes 196616 | tf_op jit(solution)/shard_map/ppermute | solution.py:486
  18.3 0.3 collective-permute-done.2.refs_0_.refs_1_
  18.6 0.0 all-to-all-done
  18.6 0.0 collective-permute-done.1.refs_2_
  18.6 0.6 %copy-done.11 = s32[1,4]{1,0:T(1,128)S(1)} copy-done((s32[1,4]{1,0:T(1,128)S(1)}, s32[1,4]{1,0:T(1,128)}, u32[]{:S(2)}) %copy-start.11) | copy-done | bytes 40
  19.3 3.5 %gradient.1 = bf16[8,16,256]{2,1,0:T(8,128)(2,1)} custom-call(s32[4]{0:T(128)S(1)} %bitcast.20, f32[128,256]{1,0:T(8,128)S(1)} %bitcast.13, f32[4,128,128]{2,1,0:T(8,128)S(1)} %bitcast.19, f32[128,128]{1,0:T(8,128)S(1)} %copy-done.9, f32[128,128]{1,0:T(8,128)S(1)} %copy-done.10, bf16[2,2,128,128]{3,2,1,0:T(8,128)(2,1)S(1)} %copy-done.15), custom_call_target="tpu_custom_call" | custom-call | flops 4294967296 | bytes 1048576 | tf_op jit(solution)/shard_map/gradient/pallas_call | solution.py:412
  22.7 0.4 collective-permute-done.3.refs_3_
  23.1 5.9 %all-to-all-start.1 = ((bf16[8,16,256]{2,1,0:T(8,128)(2,1)}), bf16[8,16,256]{2,1,0:T(8,128)(2,1)S(1)}, u32[]{:S(2)}, u32[]{:S(2)}) async-start(bf16[8,16,256]{2,1,0:T(8,128)(2,1)} %gradient.1), calls=%async_computation.1 | async-start | bytes 131072 | tf_op jit(solution)/shard_map/all_to_all | solution.py:500
  29.1 0.0 copy-done.1
  29.1 0.0 copy-start.13
  29.1 0.9 %copy-done.13 = bf16[4,256,128]{2,1,0:T(8,128)(2,1)S(1)} copy-done((bf16[4,256,128]{2,1,0:T(8,128)(2,1)S(1)}, bf16[4,256,128]{2,1,0:T(8,128)(2,1)}, u32[]{:S(2)}) %copy-start.13) | copy-done | bytes 262168
  30.0 4.9 %project_old.1 = (f32[16,256]{1,0:T(8,128)S(1)}, f32[16,64,256]{2,1,0:T(8,128)S(1)}, bf16[16,64,256]{2,1,0:T(8,128)(2,1)S(1)}, bf16[16,128,256]{2,1,0:T(8,128)(2,1)S(1)}) custom-call(s32[1]{0:T(128)} %collective-permute-done.2.refs_0_.refs_1_, f32[1024,256]{1,0:T(8,128)S(1)} %bitcast.11, f32[1024,256]{1,0:T(8,128)S(1)} %bitcast.12, ...), custom_call_target="tpu_custom_call" | custom-call | flops 3221225472 | bytes 1048576 | tf_op jit(solution)/shard_map/project_old/pallas_call | solution.py:412
  34.9 0.0 copy-start.16
  34.9 0.6 %collective-permute-start.4 = (f32[16,256]{1,0:T(8,128)S(1)}, f32[16,256]{1,0:T(8,128)S(1)}, u32[]{:S(2)}, u32[]{:S(2)}) collective-permute-start(f32[16,256]{1,0:T(8,128)S(1)} %get-tuple-element.46), channel_id=1, source_target_pairs={{0,16},{8,24},{16,0},{24,8},{1,17},{9,25},{17,1},{25,9},{2,18},{10... | collective-permute-start | bytes 49160 | tf_op jit(solution)/shard_map/ppermute | solution.py:457
  35.6 3.2 %project_old_own.1.refs_1_ = f32[16,256]{1,0:T(8,128)S(1)} custom-call(bf16[16,128,256]{2,1,0:T(8,128)(2,1)S(1)} %get-tuple-element.47.refs_0_, bf16[4,256,256]{2,1,0:T(8,128)(2,1)S(1)} %copy-done.12, bf16[4,256,128]{2,1,0:T(8,128)(2,1)S(1)} %copy-done.13, s32[1]{0:T(128)S(6)} %copy.23.refs_3_.refs_0_), custom_call_target="tpu_custom_call" | custom-call | flops 3221225472 | bytes 1048576 | tf_op jit(solution)/shard_map/project_old_own/pallas_call | solution.py:412
  38.7 0.0 copy-start.3
  38.8 0.0 collective-permute-done.4.refs_0_
  38.8 0.2 line_step.1
  39.0 0.0 all-to-all-done.1.grad_ref
  39.0 0.7 %copy-done.3 = bf16[2,256,256]{2,1,0:T(8,128)(2,1)S(1)} copy-done((bf16[2,256,256]{2,1,0:T(8,128)(2,1)S(1)}, bf16[2,256,256]{2,1,0:T(8,128)(2,1)}, u32[]{:S(2)}) %copy-start.3) | copy-done | bytes 262168
  39.7 0.6 %phase_step.1 = (f32[16,256]{1,0:T(8,128)}, f32[16,256]{1,0:T(8,128)S(1)}) custom-call(bf16[8,16,256]{2,1,0:T(8,128)(2,1)S(1)} %all-to-all-done.1.grad_ref, f32[16,256]{1,0:T(8,128)S(1)} %get-tuple-element.48.phase_part_ref, f32[16,256]{1,0:T(8,128)S(1)} %get-tuple-element.49.resid_part_ref, bf16[2,256,256]{2,1,0:T(8,128)(2,1)S(1)} %copy-done.3), custom_call_target="tpu_custom_call" | custom-call | bytes 1048576 | tf_op jit(solution)/shard_map/phase_step/pallas_call | solution.py:412
  40.3 1.5 %collective-permute-start.5 = (f32[16,256]{1,0:T(8,128)S(1)}, f32[16,256]{1,0:T(8,128)S(1)}, u32[]{:S(2)}, u32[]{:S(2)}) collective-permute-start(f32[16,256]{1,0:T(8,128)S(1)} %get-tuple-element.56.refs_0_), channel_id=1, source_target_pairs={{16,0},{24,8},{0,16},{8,24},{17,1},{25,9},{1,17},{9,25},{18,2},{26... | collective-permute-start | bytes 49160 | tf_op jit(solution)/shard_map/ppermute | solution.py:454
  41.8 1.2 %turn_tables.1 = (f32[3,256,128]{2,1,0:T(8,128)S(1)}, f32[2,128,256]{2,1,0:T(8,128)S(1)}, f32[8,256]{1,0:T(8,128)S(1)}, f32[3,256,128]{2,1,0:T(8,128)S(1)}, f32[...) custom-call(s32[1]{0:T(128)S(6)} %copy.23.refs_3_.refs_0_, s32[1]{0:T(128)} %collective-permute-done.2.refs_0_.refs_1_), custom_call_target="tpu_custom_call" | custom-call | flops 2147483648 | bytes 1048576 | tf_op jit(solution)/shard_map/turn_tables/pallas_call | solution.py:412
  43.1 1.0 %collective-permute-done.5.refs_1_ = f32[16,256]{1,0:T(8,128)S(1)} collective-permute-done((f32[16,256]{1,0:T(8,128)S(1)}, f32[16,256]{1,0:T(8,128)S(1)}, u32[]{:S(2)}, u32[]{:S(2)}) %collective-permute-start.5) | collective-permute-done | bytes 16416 | tf_op jit(solution)/shard_map/ppermute | solution.py:454
  44.1 2.5 %backproject.3.refs_4_ = bf16[8,128,256]{2,1,0:T(8,128)(2,1)S(1)} custom-call(f32[16,256]{1,0:T(8,128)S(1)} %get-tuple-element.56.refs_0_, f32[16,256]{1,0:T(8,128)S(1)} %collective-permute-done.5.refs_1_, bf16[4,256,256]{2,1,0:T(8,128)(2,1)S(1)} %copy-done.12, bf16[4,128,256]{2,1,0:T(8,128)(2,1)S(1)} %copy-done.14, ...), custom_call_target="tpu_custom_call" | custom-call | flops 3221225472 | bytes 1048576 | tf_op jit(solution)/shard_map/backproject/pallas_call | solution.py:412
  46.6 0.0 copy-start.17
  46.6 0.1 collective-permute-start.7
  46.7 2.8 %backproject.2.refs_4_ = bf16[8,128,256]{2,1,0:T(8,128)(2,1)S(1)} custom-call(f32[16,256]{1,0:T(8,128)S(1)} %get-tuple-element.56.refs_0_, f32[16,256]{1,0:T(8,128)S(1)} %collective-permute-done.5.refs_1_, bf16[4,256,256]{2,1,0:T(8,128)(2,1)S(1)} %copy-done.12, bf16[4,128,256]{2,1,0:T(8,128)(2,1)S(1)} %copy-done.14, ...), custom_call_target="tpu_custom_call" | custom-call | flops 3221225472 | bytes 1048576 | tf_op jit(solution)/shard_map/backproject/pallas_call | solution.py:412
  49.5 0.6 collective-permute-start.6
  50.0 0.0 collective-permute-done.7.refs_5_
  50.0 3.1 %project_new.2 = (f32[64,16,256]{2,1,0:T(8,128)}, f32[16,256]{1,0:T(8,128)S(1)}, f32[16,256]{1,0:T(8,128)S(1)}) custom-call(f32[16,64,256]{2,1,0:T(8,128)S(1)} %copy-done.17, bf16[16,64,256]{2,1,0:T(8,128)(2,1)S(1)} %copy-done.19, bf16[128,256]{1,0:T(8,128)(2,1)S(1)} %collective-permute-done.1.refs_2_, bf16[128,256]{1,0:T(8,128)(2,1)S(1)} %collective-permute-done.3.refs_3_, ...), custom_call_target="tpu_custom_call" | custom-call | flops 3221225472 | bytes 1048576 | tf_op jit(solution)/shard_map/project_new/pallas_call | solution.py:412
  53.1 0.0 collective-permute-done.6.refs_5_
  53.1 2.0 %project_new.3 = (f32[64,16,256]{2,1,0:T(8,128)}, f32[16,256]{1,0:T(8,128)S(1)}, bf16[8,128,256]{2,1,0:T(8,128)(2,1)S(1)}) custom-call(f32[16,64,256]{2,1,0:T(8,128)S(1)} %copy-done.17, bf16[16,64,256]{2,1,0:T(8,128)(2,1)S(1)} %copy-done.19, bf16[128,256]{1,0:T(8,128)(2,1)S(1)} %collective-permute-done.1.refs_2_, ...), custom_call_target="tpu_custom_call", output_to_operand_aliasing={{0}: (11, {}), {1}: (12, {})} | custom-call | flops 1610612736 | bytes 1048576 | tf_op jit(solution)/shard_map/project_new/pallas_call | solution.py:412
  55.2 1.5 %collective-permute-start.8 = (f32[16,256]{1,0:T(8,128)S(1)}, f32[16,256]{1,0:T(8,128)S(1)}, u32[]{:S(2)}, u32[]{:S(2)}) collective-permute-start(f32[16,256]{1,0:T(8,128)S(1)} %get-tuple-element.68), channel_id=1, source_target_pairs={{0,16},{8,24},{16,0},{24,8},{1,17},{9,25},{17,1},{25,9},{2,18},{10... | collective-permute-start | bytes 49160 | tf_op jit(solution)/shard_map/ppermute | solution.py:457
  56.7 1.8 %project_new_own.1.refs_1_ = f32[16,256]{1,0:T(8,128)S(1)} custom-call(bf16[8,128,256]{2,1,0:T(8,128)(2,1)S(1)} %get-tuple-element.69.refs_0_, bf16[4,256,256]{2,1,0:T(8,128)(2,1)S(1)} %copy-done.12, bf16[4,256,128]{2,1,0:T(8,128)(2,1)S(1)} %copy-done.13, ...), custom_call_target="tpu_custom_call", output_to_operand_aliasing={{}: (6, {})} | custom-call | flops 1610612736 | bytes 1048576 | tf_op jit(solution)/shard_map/project_new_own/pallas_call | solution.py:412
  58.5 0.5 collective-permute-done.8.refs_0_
  58.9 0.8 %dual_step.1 = f32[16,256]{1,0:T(8,128)} custom-call(f32[16,256]{1,0:T(8,128)S(1)} %copy-done.7, f32[16,256]{1,0:T(8,128)S(1)} %bitcast.17, bf16[2,256,256]{2,1,0:T(8,128)(2,1)S(1)} %copy-done.2, f32[16,256]{1,0:T(8,128)S(1)} %collective-permute-done.8.refs_0_, f32[16,256]{1,0:T(8,128)S(1)} %project_new_own.1.refs_1_), custom_call_target="tpu_custom_call" | custom-call | bytes 1048576 | tf_op jit(solution)/shard_map/dual_step/pallas_call | solution.py:412
  (28 shorter events, 0.1 us)
Async XLA Ops:
  0.6 0.7 %copy-start.4 = (f32[1,16,256]{2,1,0:T(8,128)S(1)}, f32[1,16,256]{2,1,0:T(8,128)}, u32[]{:S(2)}) copy-start(f32[1,16,256]{2,1,0:T(8,128)} %param.15) | copy-start | bytes 49156
  2.0 7.3 %collective-permute-start = (f32[1024,256]{1,0:T(8,128)}, f32[1024,256]{1,0:T(8,128)S(1)}, u32[]{:S(2)}, u32[]{:S(2)}) collective-permute-start(f32[1024,256]{1,0:T(8,128)} %bitcast.8), channel_id=1, source_target_pairs={{0,8},{8,0},{16,24},{24,16},{1,9},{9,1},{17,25},{25,17},{2,10},{10... | collective-permute-start | bytes 3145736 | tf_op jit(solution)/shard_map/ppermute | solution.py:451
  2.5 16.1 %all-to-all-start = ((f32[8,16,256]{2,1,0:T(8,128)}), f32[8,16,256]{2,1,0:T(8,128)S(1)}, u32[]{:S(2)}, u32[]{:S(2)}) async-start(f32[8,16,256]{2,1,0:T(8,128)} %phase_copies.1), calls=%async_computation | async-start | bytes 262144 | tf_op jit(solution)/shard_map/all_to_all | solution.py:471
  9.3 1.2 %copy-start = (f32[64,16,256]{2,1,0:T(8,128)S(1)}, f32[64,16,256]{2,1,0:T(8,128)}, u32[]{:S(2)}) copy-start(f32[64,16,256]{2,1,0:T(8,128)} %param.14) | copy-start | bytes 3145732
  10.5 8.1 %copy-start.8 = (f32[1,4,128,128]{3,2,1,0:T(8,128)S(1)}, f32[1,4,128,128]{3,2,1,0:T(8,128)}, u32[]{:S(2)}) copy-start(f32[1,4,128,128]{3,2,1,0:T(8,128)} %param.19) | copy-start | bytes 786436
  10.5 8.1 %copy-start.9 = (f32[128,128]{1,0:T(8,128)S(1)}, f32[128,128]{1,0:T(8,128)}, u32[]{:S(2)}) copy-start(f32[128,128]{1,0:T(8,128)} %probe_r_ref.1) | copy-start | bytes 196612
  10.5 8.1 %copy-start.10 = (f32[128,128]{1,0:T(8,128)S(1)}, f32[128,128]{1,0:T(8,128)}, u32[]{:S(2)}) copy-start(f32[128,128]{1,0:T(8,128)} %probe_i_ref.1) | copy-start | bytes 196612
  10.5 8.1 %copy-start.15 = (bf16[2,2,128,128]{3,2,1,0:T(8,128)(2,1)S(1)}, bf16[2,2,128,128]{3,2,1,0:T(8,128)(2,1)}, u32[]{:S(2)}) copy-start(bf16[2,2,128,128]{3,2,1,0:T(8,128)(2,1)} %constant.12.clone.const_ref) | copy-start | bytes 393220
  10.8 7.8 %collective-permute-start.1 = (bf16[128,256]{1,0:T(8,128)(2,1)S(1)}, bf16[128,256]{1,0:T(8,128)(2,1)S(1)}, u32[]{:S(2)}, u32[]{:S(2)}) collective-permute-start(bf16[128,256]{1,0:T(8,128)(2,1)S(1)} %get-tuple-element.39), channel_id=1, source_target_pairs={{0,1},{1,2},{2,3},{3,4},{4,5},{5,6},{6,7},{8,9},{9,10},{10,11},{11... | collective-permute-start | bytes 196616 | tf_op jit(solution)/shard_map/ppermute | solution.py:485
  14.7 3.8 %collective-permute-start.2 = (s32[1]{0:T(128)}, s32[1]{0:T(128)}, u32[]{:S(2)}, u32[]{:S(2)}) collective-permute-start(s32[1]{0:T(128)} %param.21), channel_id=1, source_target_pairs={{16,0},{24,8},{0,16},{8,24},{17,1},{25,9},{1,17},{9,25},{18,2},{26... | collective-permute-start | bytes 20 | tf_op jit(solution)/shard_map/ppermute | solution.py:454
  17.0 6.2 %collective-permute-start.3 = (bf16[128,256]{1,0:T(8,128)(2,1)S(1)}, bf16[128,256]{1,0:T(8,128)(2,1)S(1)}, u32[]{:S(2)}, u32[]{:S(2)}) collective-permute-start(bf16[128,256]{1,0:T(8,128)(2,1)S(1)} %get-tuple-element.42), channel_id=1, source_target_pairs={{1,0},{2,1},{3,2},{4,3},{5,4},{6,5},{7,6},{9,8},{10,9},{11,10},{12... | collective-permute-start | bytes 196616 | tf_op jit(solution)/shard_map/ppermute | solution.py:486
  18.6 0.7 %copy-start.11 = (s32[1,4]{1,0:T(1,128)S(1)}, s32[1,4]{1,0:T(1,128)}, u32[]{:S(2)}) copy-start(s32[1,4]{1,0:T(1,128)} %param.20) | copy-start | bytes 52
  19.3 9.8 %copy-start.1 = (f32[64,16,256]{2,1,0:T(8,128)S(1)}, f32[64,16,256]{2,1,0:T(8,128)}, u32[]{:S(2)}) copy-start(f32[64,16,256]{2,1,0:T(8,128)} %param.14) | copy-start | bytes 3145732
  19.3 9.8 %copy-start.12 = (bf16[4,256,256]{2,1,0:T(8,128)(2,1)S(1)}, bf16[4,256,256]{2,1,0:T(8,128)(2,1)}, u32[]{:S(2)}) copy-start(bf16[4,256,256]{2,1,0:T(8,128)(2,1)} %constant.13.clone.refs_5_.refs_1_.refs_2_.refs_6_) | copy-start | bytes 1572868
  23.1 15.8 %all-to-all-start.1 = ((bf16[8,16,256]{2,1,0:T(8,128)(2,1)}), bf16[8,16,256]{2,1,0:T(8,128)(2,1)S(1)}, u32[]{:S(2)}, u32[]{:S(2)}) async-start(bf16[8,16,256]{2,1,0:T(8,128)(2,1)} %gradient.1), calls=%async_computation.1 | async-start | bytes 131072 | tf_op jit(solution)/shard_map/all_to_all | solution.py:500
  29.1 1.0 %copy-start.13 = (bf16[4,256,128]{2,1,0:T(8,128)(2,1)S(1)}, bf16[4,256,128]{2,1,0:T(8,128)(2,1)}, u32[]{:S(2)}) copy-start(bf16[4,256,128]{2,1,0:T(8,128)(2,1)} %constant.14.clone.refs_6_.refs_2_.refs_7_) | copy-start | bytes 786436
  34.9 3.8 %copy-start.16 = (f32[16,64,256]{2,1,0:T(8,128)}, f32[16,64,256]{2,1,0:T(8,128)S(1)}, u32[]{:S(2)}) copy-start(f32[16,64,256]{2,1,0:T(8,128)S(1)} %get-tuple-element.51.refs_0_) | copy-start | bytes 3145732
  34.9 3.8 %copy-start.18 = (bf16[16,64,256]{2,1,0:T(8,128)(2,1)}, bf16[16,64,256]{2,1,0:T(8,128)(2,1)S(1)}, u32[]{:S(2)}) copy-start(bf16[16,64,256]{2,1,0:T(8,128)(2,1)S(1)} %get-tuple-element.52.refs_1_) | copy-start | bytes 1572868
  34.9 3.8 %collective-permute-start.4 = (f32[16,256]{1,0:T(8,128)S(1)}, f32[16,256]{1,0:T(8,128)S(1)}, u32[]{:S(2)}, u32[]{:S(2)}) collective-permute-start(f32[16,256]{1,0:T(8,128)S(1)} %get-tuple-element.46), channel_id=1, source_target_pairs={{0,16},{8,24},{16,0},{24,8},{1,17},{9,25},{17,1},{25,9},{2,18},{10... | collective-permute-start | bytes 49160 | tf_op jit(solution)/shard_map/ppermute | solution.py:457
  35.5 3.2 %copy-start.2 = (bf16[2,256,256]{2,1,0:T(8,128)(2,1)S(1)}, bf16[2,256,256]{2,1,0:T(8,128)(2,1)}, u32[]{:S(2)}) copy-start(bf16[2,256,256]{2,1,0:T(8,128)(2,1)} %constant.15.clone.inverse_ref) | copy-start | bytes 786436
  35.5 3.2 %copy-start.5 = (f32[1,16,256]{2,1,0:T(8,128)S(1)}, f32[1,16,256]{2,1,0:T(8,128)}, u32[]{:S(2)}) copy-start(f32[1,16,256]{2,1,0:T(8,128)} %param.15) | copy-start | bytes 49156
  35.6 3.2 %copy-start.6 = (f32[1,16,256]{2,1,0:T(8,128)S(1)}, f32[1,16,256]{2,1,0:T(8,128)}, u32[]{:S(2)}) copy-start(f32[1,16,256]{2,1,0:T(8,128)} %param.16) | copy-start | bytes 49156
  38.7 1.0 %copy-start.3 = (bf16[2,256,256]{2,1,0:T(8,128)(2,1)S(1)}, bf16[2,256,256]{2,1,0:T(8,128)(2,1)}, u32[]{:S(2)}) copy-start(bf16[2,256,256]{2,1,0:T(8,128)(2,1)} %constant.16.clone.forward_ref) | copy-start | bytes 786436
  40.3 3.7 %copy-start.14 = (bf16[4,128,256]{2,1,0:T(8,128)(2,1)S(1)}, bf16[4,128,256]{2,1,0:T(8,128)(2,1)}, u32[]{:S(2)}) copy-start(bf16[4,128,256]{2,1,0:T(8,128)(2,1)} %constant.17.clone.refs_3_) | copy-start | bytes 786436
  40.3 3.7 %collective-permute-start.5 = (f32[16,256]{1,0:T(8,128)S(1)}, f32[16,256]{1,0:T(8,128)S(1)}, u32[]{:S(2)}, u32[]{:S(2)}) collective-permute-start(f32[16,256]{1,0:T(8,128)S(1)} %get-tuple-element.56.refs_0_), channel_id=1, source_target_pairs={{16,0},{24,8},{0,16},{8,24},{17,1},{25,9},{1,17},{9,25},{18,2},{26... | collective-permute-start | bytes 49160 | tf_op jit(solution)/shard_map/ppermute | solution.py:454
  46.6 3.4 %copy-start.17 = (f32[16,64,256]{2,1,0:T(8,128)S(1)}, f32[16,64,256]{2,1,0:T(8,128)}, u32[]{:S(2)}) copy-start(f32[16,64,256]{2,1,0:T(8,128)} %copy-done.16) | copy-start | bytes 3145732
  46.6 3.4 %copy-start.19 = (bf16[16,64,256]{2,1,0:T(8,128)(2,1)S(1)}, bf16[16,64,256]{2,1,0:T(8,128)(2,1)}, u32[]{:S(2)}) copy-start(bf16[16,64,256]{2,1,0:T(8,128)(2,1)} %copy-done.18) | copy-start | bytes 1572868
  46.6 3.4 %collective-permute-start.7 = (bf16[8,128,256]{2,1,0:T(8,128)(2,1)S(1)}, bf16[8,128,256]{2,1,0:T(8,128)(2,1)S(1)}, u32[]{:S(2)}, u32[]{:S(2)}) collective-permute-start(bf16[8,128,256]{2,1,0:T(8,128)(2,1)S(1)} %backproject.3.refs_4_), channel_id=1, source_target_pairs={{0,8},{8,0},{16,24},{24,16},{1,9},{9,1},{17,25},{25,17},{2,10},{10... | collective-permute-start | bytes 1572872 | tf_op jit(solution)/shard_map/ppermute | solution.py:451
  49.5 3.7 %collective-permute-start.6 = (bf16[8,128,256]{2,1,0:T(8,128)(2,1)S(1)}, bf16[8,128,256]{2,1,0:T(8,128)(2,1)S(1)}, u32[]{:S(2)}, u32[]{:S(2)}) collective-permute-start(bf16[8,128,256]{2,1,0:T(8,128)(2,1)S(1)} %backproject.2.refs_4_), channel_id=1, source_target_pairs={{0,8},{8,0},{16,24},{24,16},{1,9},{9,1},{17,25},{25,17},{2,10},{10... | collective-permute-start | bytes 1572872 | tf_op jit(solution)/shard_map/ppermute | solution.py:451
  55.2 3.7 %collective-permute-start.8 = (f32[16,256]{1,0:T(8,128)S(1)}, f32[16,256]{1,0:T(8,128)S(1)}, u32[]{:S(2)}, u32[]{:S(2)}) collective-permute-start(f32[16,256]{1,0:T(8,128)S(1)} %get-tuple-element.68), channel_id=1, source_target_pairs={{0,16},{8,24},{16,0},{24,8},{1,17},{9,25},{17,1},{25,9},{2,18},{10... | collective-permute-start | bytes 49160 | tf_op jit(solution)/shard_map/ppermute | solution.py:457
  56.7 2.3 %copy-start.7 = (f32[16,256]{1,0:T(8,128)S(1)}, f32[16,256]{1,0:T(8,128)}, u32[]{:S(2)}) copy-start(f32[16,256]{1,0:T(8,128)} %get-tuple-element.50.phase_ref) | copy-start | bytes 49156

commit v7 on v6

--- a/solution.py
+++ b/solution.py
@@ -73,7 +73,10 @@
 
     left_high, left_low = parts(left)
     right_high, right_low = parts(right)
-    return dot(left_high, right_high) + dot(left_low, right_high) + dot(left_high, right_low)
+    return dot(
+        jnp.concatenate([left_high, left_low, left_high], axis=1),
+        jnp.concatenate([right_high, right_high, right_low], axis=0),
+    )
 
 
 def turn(re, im, c1, s, c2, sign):
@@ -126,6 +129,16 @@
         nyq_ref[:, lanes] = top
 
 
+def chip_places(share):
+    here = lax.axis_index("ang")
+    other = here + 1 - 2 * lax.rem(here, 2)
+    return [pl.ds(pl.multiple_of(which * share, share), share) for which in (here, other)]
+
+
+def chip_table(table_ref, share):
+    return jnp.concatenate([table_ref[rows, :] for rows in chip_places(share)], axis=0)
+
+
 class Tables:
     def __init__(self, row, col, nyq):
         self.row, self.col, self.nyq = row, col, nyq
@@ -134,10 +147,7 @@
         return self.row[0], self.row[1], self.row[2]
 
     def chip_rows(self, share):
-        here = lax.axis_index("ang")
-        other = here + 1 - 2 * lax.rem(here, 2)
-        places = [pl.ds(pl.multiple_of(which * share, 8), share) for which in (here, other)]
-        return tuple(jnp.concatenate([self.row[part, rows, :] for rows in places], axis=0) for part in range(3))
+        return tuple(chip_table(self.row.at[part], share) for part in range(3))
 
     def columns(self):
         c1 = self.col[0]
@@ -171,8 +181,8 @@
 
 
 def project_slices(slab, count, share, tables, consts, lines_refs):
-    forward_ref, inverse_ref, down_ref, up_ref = consts
-    here = lax.axis_index("ang")
+    forward_ref, inverse_ref, up_ref = consts
+    down = jnp.transpose(chip_table(forward_ref, share).astype(F32)).astype(BF16)
     spectrum = dot(slab, forward_ref[...])
     for table, lines_ref in zip(tables, lines_refs):
         chip_rows = table.chip_rows(share)
@@ -181,7 +191,7 @@
             for i in range(count)
         ]
         first = dot(jnp.concatenate(turned, axis=0), inverse_ref[...]).astype(BF16)
-        columns = dot(down_ref[here], side_by_side(first, count))
+        columns = dot(down, side_by_side(first, count))
         turned = [turn_columns(block_of(columns, i, count, 1), table.columns(), 1) for i in range(count)]
         second = dot(up_ref[...], jnp.concatenate(turned, axis=1)).astype(BF16)
         last = dot(stacked(second, count), forward_ref[...])
@@ -224,8 +234,8 @@
 
 
 def project_kernel(groups, slices, *refs):
-    angle_refs, sides, (const_ref, down_ref), lines_refs, bases, (slab_ref,), table_refs = take(
-        refs, groups, 4, 2, groups, 2, 1, 3 * groups
+    angle_refs, sides, (const_ref,), lines_refs, bases, (slab_ref,), table_refs = take(
+        refs, groups, 4, 1, groups, 2, 1, 3 * groups
     )
     share = sides[0].shape[0] // slices
     tables_kernel(groups, *angle_refs, *table_refs)
@@ -247,28 +257,28 @@
         past, now = now, later
     slab = jnp.concatenate(slab, axis=0)
     slab_ref[...] = slab.reshape(slab_ref.shape)
-    consts = [const_ref.at[0], const_ref.at[1], down_ref, const_ref.at[3]]
+    consts = [const_ref.at[0], const_ref.at[1], const_ref.at[3]]
     project_slices(slab, slices, share, as_tables(table_refs), consts, lines_refs)
 
 
 def own_line_kernel(pieces, made, aliased, *refs):
-    slabs, (const_ref, down_ref), given, unused, (line_ref,), table_refs = take(
-        refs, pieces, 2, 3 if made else 1, aliased, 1, 0 if made else 3
+    slabs, (const_ref,), given, unused, (line_ref,), table_refs = take(
+        refs, pieces, 1, 3 if made else 1, aliased, 1, 0 if made else 3
     )
     if not made:
         tables_kernel(1, *given, *table_refs)
     slab = jnp.concatenate([ref[...].reshape(-1, ref.shape[2]) for ref in slabs], axis=0)
-    consts = [const_ref.at[0], const_ref.at[1], down_ref, const_ref.at[3]]
+    consts = [const_ref.at[0], const_ref.at[1], const_ref.at[3]]
     tables = as_tables(given if made else table_refs)
     project_slices(slab, line_ref.shape[0], slabs[0].shape[1] // 2, tables, consts, [line_ref])
 
 
 def back_kernel(groups, *refs):
-    spectra_refs, (const_ref, up_ref), table_refs, (out_ref,) = take(refs, groups, 2, 3 * groups, 1)
+    spectra_refs, (const_ref,), table_refs, (out_ref,) = take(refs, groups, 1, 3 * groups, 1)
     forward_ref, inverse_ref, down_ref = const_ref.at[0], const_ref.at[1], const_ref.at[2]
     slices, pair, length = out_ref.shape
     half = length // 2
-    here = lax.axis_index("ang")
+    up = chip_table(const_ref.at[3], pair // 2)
     totals = None
     for table, spectra_ref in zip(as_tables(table_refs), spectra_refs):
         turned = []
@@ -279,7 +289,7 @@
         spread = dot(jnp.concatenate(turned, axis=0), inverse_ref[...]).astype(BF16)
         columns = dot(down_ref[...], side_by_side(spread, slices))
         turned = [turn_columns(block_of(columns, i, slices, 1), table.columns(), -1) for i in range(slices)]
-        second = dot(up_ref[here], jnp.concatenate(turned, axis=1)).astype(BF16)
+        second = dot(up, jnp.concatenate(turned, axis=1)).astype(BF16)
         last = dot(stacked(second, slices), forward_ref[...])
         chip_rows = table.chip_rows(pair // 2)
         turned = [
@@ -292,10 +302,10 @@
 
 
 def update_kernel(groups, first, last, aliased, *refs):
-    bases, halos, shares, (const_ref, down_ref), table_refs, unused, (volume_ref,), lines_refs, slabs, sides = take(
-        refs, 2, 2, 2, 2, 3 * groups, aliased, 1, groups, 1 if last else 0, 2
-    )
-    consts = [const_ref.at[0], const_ref.at[1], down_ref, const_ref.at[3]]
+    bases, halos, shares, (const_ref,), table_refs, unused, (volume_ref,), lines_refs, slabs, sides = take(
+        refs, 2, 2, 2, 1, 3 * groups, aliased, 1, groups, 1 if last else 0, 2
+    )
+    consts = [const_ref.at[0], const_ref.at[1], const_ref.at[3]]
     own_ref, other_ref = bases
     mine_ref, theirs_ref = shares
     slices, share, length = own_ref.shape
@@ -383,28 +393,28 @@
     return dot_split(line, inverse_ref[...]) * (1.0 / math.sqrt(line.shape[1]))
 
 
-def line_kernel(peers, phase_ref, dual_ref, inverse_ref, *refs):
+def line_kernel(peers, phase_ref, dual_ref, full_ref, *refs):
     line_refs, (phase_part_ref, resid_part_ref) = take(refs, peers, 2)
-    proj_old = projected(line_refs, inverse_ref)
+    proj_old = projected(line_refs, full_ref.at[1])
     phase, dual = phase_ref[...], dual_ref[...]
     phase_part = phase - eta_step * (dual + rho_weight * (phase - proj_old))
     phase_part_ref[...] = phase_part
     resid_part_ref[...] = rho_weight * (proj_old - phase_part) - dual
 
 
-def phase_kernel(grad_ref, phase_part_ref, resid_part_ref, forward_ref, phase_new_ref, spectrum_ref):
+def phase_kernel(grad_ref, phase_part_ref, resid_part_ref, full_ref, phase_new_ref, spectrum_ref):
     grad = grad_ref[0].astype(F32)
     for t in range(1, grad_ref.shape[0]):
         grad = grad + grad_ref[t].astype(F32)
     grad = eta_step * grad
     phase_new_ref[...] = phase_part_ref[...] - grad
     resid = resid_part_ref[...] + rho_weight * grad
-    spectrum_ref[...] = dot_split(resid, forward_ref[...]) * (1.0 / math.sqrt(resid.shape[1]))
-
-
-def dual_kernel(peers, phase_ref, dual_ref, inverse_ref, *refs):
+    spectrum_ref[...] = dot_split(resid, full_ref[0]) * (1.0 / math.sqrt(resid.shape[1]))
+
+
+def dual_kernel(peers, phase_ref, dual_ref, full_ref, *refs):
     line_refs, (dual_new_ref,) = take(refs, peers, 1)
-    proj_new = projected(line_refs, inverse_ref)
+    proj_new = projected(line_refs, full_ref.at[1])
     dual_new_ref[...] = dual_ref[...] + rho_weight * (phase_ref[...] - proj_new)
 
 
@@ -436,13 +446,8 @@
     shape = jax.ShapeDtypeStruct
 
     (forward_full, inverse_full), (forward, inverse) = packed_tables(length)
-    forward_full, inverse_full = split_pair(forward_full), split_pair(inverse_full)
+    full = np.stack([split_pair(forward_full), split_pair(inverse_full)])
     down, up = forward.T, inverse.T
-    owners = [
-        np.r_[i * share : (i + 1) * share, (i ^ 1) * share : ((i ^ 1) + 1) * share] for i in range(ang)
-    ]
-    down_part = np.stack([down[:, rows] for rows in owners])
-    up_part = np.stack([up[rows] for rows in owners])
     square = np.stack([forward, inverse, down, up])
     line = shape((slices, length), F32)
     work = 2 * 2 * length * length * length * slices * groups
@@ -505,8 +510,8 @@
         [line] * far
         + [shape((slices, share, length), F32), shape((slices, share, length), BF16)]
         + [shape((slices, pair, length), BF16)],
-        angles + [flat, flat, other, other, square, down_part],
-        [SMEM_SPEC] * far + [lanes(0), lanes(1)] * 2 + [VMEM_SPEC] * 2,
+        angles + [flat, flat, other, other, square],
+        [SMEM_SPEC] * far + [lanes(0), lanes(1)] * 2 + [VMEM_SPEC],
         scratch=[pltpu.VMEM(t.shape, F32) for t in tables_shape[3:]],
         grid=(1,),
         flops=3 * work * far // groups,
@@ -518,8 +523,8 @@
     old += call(
         functools.partial(own_line_kernel, 1, False, 0),
         [line],
-        slab + [square, down_part, angle_index],
-        [VMEM_SPEC] * 3 + [SMEM_SPEC],
+        slab + [square, angle_index],
+        [VMEM_SPEC] * 2 + [SMEM_SPEC],
         scratch=[pltpu.VMEM(t.shape, F32) for t in tables_shape[:3]],
         flops=3 * work // groups,
         vmem=24,
@@ -527,11 +532,11 @@
     )
 
     phase_part, resid_part = call(
-        functools.partial(line_kernel, groups), [line, line], [phase[0], dual[0], inverse_full] + old,
+        functools.partial(line_kernel, groups), [line, line], [phase[0], dual[0], full] + old,
         name="line_step",
     )
     phase_new, spectrum = call(
-        phase_kernel, [line, line], [grad, phase_part, resid_part, forward_full], name="phase_step"
+        phase_kernel, [line, line], [grad, phase_part, resid_part, full], name="phase_step"
     )
     spectrum, angles = lax.optimization_barrier((spectrum, [angle_index] + angles))
     tables = call(
@@ -546,8 +551,8 @@
         (mine,) = call(
             functools.partial(back_kernel, groups),
             [shape((some, pair, length), BF16)],
-            spectra + [square, up_part] + tables,
-            [block_lines[h]] * groups + [VMEM_SPEC] * (2 + 3 * groups),
+            spectra + [square] + tables,
+            [block_lines[h]] * groups + [VMEM_SPEC] * (1 + 3 * groups),
             grid=(1,),
             flops=3 * work // parts,
             vmem=24,
@@ -559,7 +564,7 @@
     for h in range(parts):
         last = h == parts - 1
         count = far if last else groups
-        args = bases + [before, after] + list(halves[h]) + [square, down_part]
+        args = bases + [before, after] + list(halves[h]) + [square]
         args = args + (tables[3:] if last else tables[3:] + tables[:3])
         carried = results[: 1 + count]
         outs = call(
@@ -584,21 +589,21 @@
     volume_new, lines, slab = results[0], results[1:groups], outs[-1]
     new = [to_peer(lines[j], j + 1) for j in range(far)]
     own_line = results[groups:]
-    args = [slab, square, down_part] + tables[:3] + own_line
+    args = [slab, square] + tables[:3] + own_line
     new += call(
         functools.partial(own_line_kernel, 1, True, len(own_line)),
         [line],
         args,
-        [VMEM_SPEC] * 6 + [pl.BlockSpec(memory_space=pl.ANY)] * len(own_line),
+        [VMEM_SPEC] * 5 + [pl.BlockSpec(memory_space=pl.ANY)] * len(own_line),
         [block_lines[parts - 1]],
         grid=(1,),
         flops=3 * work // groups // parts,
         vmem=24,
-        aliases={6: 0} if own_line else None,
+        aliases={5: 0} if own_line else None,
         name="project_new_own",
     )
     (dual_new,) = call(
-        functools.partial(dual_kernel, groups), [line], [phase_new, dual[0], inverse_full] + new,
+        functools.partial(dual_kernel, groups), [line], [phase_new, dual[0], full] + new,
         name="dual_step",
     )
     return phase_new[None], volume_new, dual_new[None]

time: 60.3 us -> 58.7 us (0.973)
  local copies, waits for them, and re-layouts: 4.25 us -> 2.61 us
    unnamed x40 -> x34, local copies, waits for them, and re-layouts: 4.25 us -> 2.61 us
  transfers between devices with their start and end apart: 11 -> 11, of which waited for: 4 -> 4; matrix products, arithmetic and copies ran while one was open for 0% -> 0% of each run, Pallas kernels for 35% -> 36%
where the time goes in v7:
time: 58.7 us; the launch traced here: 58.1 us
  Pallas kernels  27.5 us (47%)
  starting transfers between devices  24.2 us (41%)
  local copies, waits for them, and re-layouts  2.61 us (4%)
  waiting for transfers between devices  2.25 us (4%)
  between operations  1.56 us (3%)
    pallas_call x14, Pallas kernels, call(): pl.pallas_call(kernel, grid=grid, out_shape=tuple(outs), in_specs=specs o...  27.5 us
    all_to_all x1, starting transfers between devices, shards(): lax.all_to_all(phases, 'tile', split_axis=0, concat_axis=0, tiled=True)  6.83 us
    all_to_all x1, starting transfers between devices, shards(): grad = lax.all_to_all(grad, 'tile', split_axis=0, concat_axis=0, tiled=True)  5.85 us
    ppermute x1, starting transfers between devices, shards(): lax.ppermute(edges[0], 'tile', [(i, i + 1) for i in range(tiles - 1)])  3.92 us
    ppermute x2, starting transfers between devices, from_peer(): lax.ppermute(value, 'ang', [((i + 2 * j) % ang, i) for i in range(ang)])  3.05 us
    unnamed x34, local copies, waits for them, and re-layouts  2.61 us
    ppermute x2, starting transfers between devices, to_peer(): lax.ppermute(value, 'ang', [(i, (i + 2 * j) % ang) for i in range(ang)])  2.15 us
    ppermute x1, starting transfers between devices, shards(): lax.ppermute(edges[1], 'tile', [(i + 1, i) for i in range(tiles - 1)])  1.29 us
  transfers between devices with their start and end apart: 11, of which 4 were waited for; matrix products, arithmetic and copies ran while one was open for 0% of the time, Pallas kernels for 36%

profile of v7, /device:TPU:0, one launch (start us, length us, event | category | flops | bytes accessed | tf_op | source)
XLA Modules:
  0.0 58.1 jit_solution(7349690953920784130)
XLA Ops:
  0.6 0.0 copy-start.3
  0.6 0.7 %copy-done.3 = f32[1,16,256]{2,1,0:T(8,128)S(1)} copy-done((f32[1,16,256]{2,1,0:T(8,128)S(1)}, f32[1,16,256]{2,1,0:T(8,128)}, u32[]{:S(2)}) %copy-start.3) | copy-done | bytes 16408
  1.4 0.7 %phase_copies.1 = f32[8,16,256]{2,1,0:T(8,128)} custom-call(f32[16,256]{1,0:T(8,128)S(1)} %bitcast.14), custom_call_target="tpu_custom_call" | custom-call | bytes 1048576 | tf_op jit(solution)/shard_map/phase_copies/pallas_call | solution.py:422
  2.0 0.5 collective-permute-start
  2.5 6.8 %all-to-all-start = ((f32[8,16,256]{2,1,0:T(8,128)}), f32[8,16,256]{2,1,0:T(8,128)S(1)}, u32[]{:S(2)}, u32[]{:S(2)}) async-start(f32[8,16,256]{2,1,0:T(8,128)} %phase_copies.1), calls=%async_computation | async-start | bytes 262144 | tf_op jit(solution)/shard_map/all_to_all | solution.py:476
  9.3 0.0 collective-permute-done.refs_2_.refs_3_.refs_4_
  9.3 0.0 copy-start.1
  9.3 1.2 %copy-done.1 = f32[64,16,256]{2,1,0:T(8,128)S(1)} copy-done((f32[64,16,256]{2,1,0:T(8,128)S(1)}, f32[64,16,256]{2,1,0:T(8,128)}, u32[]{:S(2)}) %copy-start.1) | copy-done | bytes 1048600
  10.5 0.3 edges.1
  10.8 3.9 %collective-permute-start.1 = (bf16[128,256]{1,0:T(8,128)(2,1)S(1)}, bf16[128,256]{1,0:T(8,128)(2,1)S(1)}, u32[]{:S(2)}, u32[]{:S(2)}) collective-permute-start(bf16[128,256]{1,0:T(8,128)(2,1)S(1)} %get-tuple-element.39), channel_id=1, source_target_pairs={{0,1},{1,2},{2,3},{3,4},{4,5},{5,6},{6,7},{8,9},{9,10},{10,11},{11... | collective-permute-start | bytes 196616 | tf_op jit(solution)/shard_map/ppermute | solution.py:490
  14.7 1.6 %collective-permute-start.2 = (s32[1]{0:T(128)}, s32[1]{0:T(128)}, u32[]{:S(2)}, u32[]{:S(2)}) collective-permute-start(s32[1]{0:T(128)} %param.18), channel_id=1, source_target_pairs={{16,0},{24,8},{0,16},{8,24},{17,1},{25,9},{1,17},{9,25},{18,2},{26... | collective-permute-start | bytes 20 | tf_op jit(solution)/shard_map/ppermute | solution.py:459
  17.0 1.3 %collective-permute-start.3 = (bf16[128,256]{1,0:T(8,128)(2,1)S(1)}, bf16[128,256]{1,0:T(8,128)(2,1)S(1)}, u32[]{:S(2)}, u32[]{:S(2)}) collective-permute-start(bf16[128,256]{1,0:T(8,128)(2,1)S(1)} %get-tuple-element.42), channel_id=1, source_target_pairs={{1,0},{2,1},{3,2},{4,3},{5,4},{6,5},{7,6},{9,8},{10,9},{11,10},{12... | collective-permute-start | bytes 196616 | tf_op jit(solution)/shard_map/ppermute | solution.py:491
  18.3 0.3 collective-permute-done.2.refs_0_.refs_1_
  18.6 0.0 all-to-all-done
  18.6 0.0 collective-permute-done.1.refs_2_
  18.6 0.6 %copy-done.10 = s32[1,4]{1,0:T(1,128)S(1)} copy-done((s32[1,4]{1,0:T(1,128)S(1)}, s32[1,4]{1,0:T(1,128)}, u32[]{:S(2)}) %copy-start.10) | copy-done | bytes 40
  19.3 3.4 %gradient.1 = bf16[8,16,256]{2,1,0:T(8,128)(2,1)} custom-call(s32[4]{0:T(128)S(1)} %bitcast.20, f32[128,256]{1,0:T(8,128)S(1)} %bitcast.13, f32[4,128,128]{2,1,0:T(8,128)S(1)} %bitcast.19, f32[128,128]{1,0:T(8,128)S(1)} %copy-done.8, f32[128,128]{1,0:T(8,128)S(1)} %copy-done.9, bf16[2,2,128,128]{3,2,1,0:T(8,128)(2,1)S(1)} %copy-done.12), custom_call_target="tpu_custom_call" | custom-call | flops 4294967296 | bytes 1048576 | tf_op jit(solution)/shard_map/gradient/pallas_call | solution.py:422
  22.7 0.5 collective-permute-done.3.refs_3_
  23.1 5.9 %all-to-all-start.1 = ((bf16[8,16,256]{2,1,0:T(8,128)(2,1)}), bf16[8,16,256]{2,1,0:T(8,128)(2,1)S(1)}, u32[]{:S(2)}, u32[]{:S(2)}) async-start(bf16[8,16,256]{2,1,0:T(8,128)(2,1)} %gradient.1), calls=%async_computation.1 | async-start | bytes 131072 | tf_op jit(solution)/shard_map/all_to_all | solution.py:505
  29.0 0.0 copy-done.11
  29.0 5.0 %project_old.1 = (f32[16,256]{1,0:T(8,128)S(1)}, f32[16,64,256]{2,1,0:T(8,128)S(1)}, bf16[16,64,256]{2,1,0:T(8,128)(2,1)S(1)}, bf16[16,128,256]{2,1,0:T(8,128)(2,1)S(1)}) custom-call(s32[1]{0:T(128)} %collective-permute-done.2.refs_0_.refs_1_, f32[1024,256]{1,0:T(8,128)S(1)} %bitcast.11, f32[1024,256]{1,0:T(8,128)S(1)} %bitcast.12, ...), custom_call_target="tpu_custom_call" | custom-call | flops 3221225472 | bytes 1048576 | tf_op jit(solution)/shard_map/project_old/pallas_call | solution.py:422
  34.0 0.0 copy-start.13
  34.0 0.6 %collective-permute-start.4 = (f32[16,256]{1,0:T(8,128)S(1)}, f32[16,256]{1,0:T(8,128)S(1)}, u32[]{:S(2)}, u32[]{:S(2)}) collective-permute-start(f32[16,256]{1,0:T(8,128)S(1)} %get-tuple-element.46), channel_id=1, source_target_pairs={{0,16},{8,24},{16,0},{24,8},{1,17},{9,25},{17,1},{25,9},{2,18},{10... | collective-permute-start | bytes 49160 | tf_op jit(solution)/shard_map/ppermute | solution.py:462
  34.6 3.2 %project_old_own.1.refs_1_ = f32[16,256]{1,0:T(8,128)S(1)} custom-call(bf16[16,128,256]{2,1,0:T(8,128)(2,1)S(1)} %get-tuple-element.47.refs_0_, bf16[4,256,256]{2,1,0:T(8,128)(2,1)S(1)} %copy-done.11, s32[1]{0:T(128)S(6)} %copy.20.refs_2_.refs_0_), custom_call_target="tpu_custom_call" | custom-call | flops 3221225472 | bytes 1048576 | tf_op jit(solution)/shard_map/project_old_own/pallas_call | solution.py:422
  37.8 0.0 collective-permute-done.4.refs_0_
  37.8 0.0 copy-done
  37.9 0.0 copy-done.4
  37.9 0.0 copy-done.5
  37.9 0.2 line_step.1
  38.1 0.0 all-to-all-done.1.grad_ref
  38.1 0.6 %phase_step.1 = (f32[16,256]{1,0:T(8,128)}, f32[16,256]{1,0:T(8,128)S(1)}) custom-call(bf16[8,16,256]{2,1,0:T(8,128)(2,1)S(1)} %all-to-all-done.1.grad_ref, f32[16,256]{1,0:T(8,128)S(1)} %get-tuple-element.48.phase_part_ref, f32[16,256]{1,0:T(8,128)S(1)} %get-tuple-element.49.resid_part_ref, bf16[2,2,256,256]{3,2,1,0:T(8,128)(2,1)S(1)} %copy-done), custom_call_target="tpu_custom_call" | custom-call | bytes 1048576 | tf_op jit(solution)/shard_map/phase_step/pallas_call | solution.py:422
  38.7 1.5 %collective-permute-start.5 = (f32[16,256]{1,0:T(8,128)S(1)}, f32[16,256]{1,0:T(8,128)S(1)}, u32[]{:S(2)}, u32[]{:S(2)}) collective-permute-start(f32[16,256]{1,0:T(8,128)S(1)} %get-tuple-element.56.refs_0_), channel_id=1, source_target_pairs={{16,0},{24,8},{0,16},{8,24},{17,1},{25,9},{1,17},{9,25},{18,2},{26... | collective-permute-start | bytes 49160 | tf_op jit(solution)/shard_map/ppermute | solution.py:459
  40.2 1.3 %turn_tables.1 = (f32[3,256,128]{2,1,0:T(8,128)S(1)}, f32[2,128,256]{2,1,0:T(8,128)S(1)}, f32[8,256]{1,0:T(8,128)S(1)}, f32[3,256,128]{2,1,0:T(8,128)S(1)}, f32[...) custom-call(s32[1]{0:T(128)S(6)} %copy.20.refs_2_.refs_0_, s32[1]{0:T(128)} %collective-permute-done.2.refs_0_.refs_1_), custom_call_target="tpu_custom_call" | custom-call | flops 2147483648 | bytes 1048576 | tf_op jit(solution)/shard_map/turn_tables/pallas_call | solution.py:422
  41.5 1.0 %collective-permute-done.5.refs_1_ = f32[16,256]{1,0:T(8,128)S(1)} collective-permute-done((f32[16,256]{1,0:T(8,128)S(1)}, f32[16,256]{1,0:T(8,128)S(1)}, u32[]{:S(2)}, u32[]{:S(2)}) %collective-permute-start.5) | collective-permute-done | bytes 16416 | tf_op jit(solution)/shard_map/ppermute | solution.py:459
  42.5 2.5 %backproject.3.refs_4_ = bf16[8,128,256]{2,1,0:T(8,128)(2,1)S(1)} custom-call(f32[16,256]{1,0:T(8,128)S(1)} %get-tuple-element.56.refs_0_, f32[16,256]{1,0:T(8,128)S(1)} %collective-permute-done.5.refs_1_, bf16[4,256,256]{2,1,0:T(8,128)(2,1)S(1)} %copy-done.11, f32[3,256,128]{2,1,0:T(8,128)S(1)} %get-tuple-element.59.refs_3_.refs_10_.refs_2_, ...), custom_call_target="tpu_custom_call" | custom-call | flops 3221225472 | bytes 1048576 | tf_op jit(solution)/shard_map/backproject/pallas_call | solution.py:422
  45.0 0.0 copy-start.14
  45.0 0.0 copy-start.16
  45.0 0.1 collective-permute-start.7
  45.1 2.8 %backproject.2.refs_4_ = bf16[8,128,256]{2,1,0:T(8,128)(2,1)S(1)} custom-call(f32[16,256]{1,0:T(8,128)S(1)} %get-tuple-element.56.refs_0_, f32[16,256]{1,0:T(8,128)S(1)} %collective-permute-done.5.refs_1_, bf16[4,256,256]{2,1,0:T(8,128)(2,1)S(1)} %copy-done.11, f32[3,256,128]{2,1,0:T(8,128)S(1)} %get-tuple-element.59.refs_3_.refs_10_.refs_2_, ...), custom_call_target="tpu_custom_call" | custom-call | flops 3221225472 | bytes 1048576 | tf_op jit(solution)/shard_map/backproject/pallas_call | solution.py:422
  47.8 0.6 collective-permute-start.6
  48.4 0.0 collective-permute-done.7.refs_5_
  48.4 3.1 %project_new.2 = (f32[64,16,256]{2,1,0:T(8,128)}, f32[16,256]{1,0:T(8,128)S(1)}, f32[16,256]{1,0:T(8,128)S(1)}) custom-call(f32[16,64,256]{2,1,0:T(8,128)S(1)} %copy-done.14, bf16[16,64,256]{2,1,0:T(8,128)(2,1)S(1)} %copy-done.16, bf16[128,256]{1,0:T(8,128)(2,1)S(1)} %collective-permute-done.1.refs_2_, bf16[128,256]{1,0:T(8,128)(2,1)S(1)} %collective-permute-done.3.refs_3_, ...), custom_call_target="tpu_custom_call" | custom-call | flops 3221225472 | bytes 1048576 | tf_op jit(solution)/shard_map/project_new/pallas_call | solution.py:422
  51.6 0.0 collective-permute-done.6.refs_5_
  51.6 1.9 %project_new.3 = (f32[64,16,256]{2,1,0:T(8,128)}, f32[16,256]{1,0:T(8,128)S(1)}, bf16[8,128,256]{2,1,0:T(8,128)(2,1)S(1)}) custom-call(f32[16,64,256]{2,1,0:T(8,128)S(1)} %copy-done.14, bf16[16,64,256]{2,1,0:T(8,128)(2,1)S(1)} %copy-done.16, bf16[128,256]{1,0:T(8,128)(2,1)S(1)} %collective-permute-done.1.refs_2_, ...), custom_call_target="tpu_custom_call", output_to_operand_aliasing={{0}: (10, {}), {1}: (11, {})} | custom-call | flops 1610612736 | bytes 1048576 | tf_op jit(solution)/shard_map/project_new/pallas_call | solution.py:422
  53.5 1.6 %collective-permute-start.8 = (f32[16,256]{1,0:T(8,128)S(1)}, f32[16,256]{1,0:T(8,128)S(1)}, u32[]{:S(2)}, u32[]{:S(2)}) collective-permute-start(f32[16,256]{1,0:T(8,128)S(1)} %get-tuple-element.68), channel_id=1, source_target_pairs={{0,16},{8,24},{16,0},{24,8},{1,17},{9,25},{17,1},{25,9},{2,18},{10... | collective-permute-start | bytes 49160 | tf_op jit(solution)/shard_map/ppermute | solution.py:462
  55.1 1.8 %project_new_own.1.refs_1_ = f32[16,256]{1,0:T(8,128)S(1)} custom-call(bf16[8,128,256]{2,1,0:T(8,128)(2,1)S(1)} %get-tuple-element.69.refs_0_, bf16[4,256,256]{2,1,0:T(8,128)(2,1)S(1)} %copy-done.11, f32[3,256,128]{2,1,0:T(8,128)S(1)} %get-tuple-element.59.refs_3_.refs_10_.refs_2_, ...), custom_call_target="tpu_custom_call", output_to_operand_aliasing={{}: (5, {})} | custom-call | flops 1610612736 | bytes 1048576 | tf_op jit(solution)/shard_map/project_new_own/pallas_call | solution.py:422
  56.8 0.5 collective-permute-done.8.refs_0_
  57.3 0.8 %dual_step.1 = f32[16,256]{1,0:T(8,128)} custom-call(f32[16,256]{1,0:T(8,128)S(1)} %copy-done.6, f32[16,256]{1,0:T(8,128)S(1)} %bitcast.17, bf16[2,2,256,256]{3,2,1,0:T(8,128)(2,1)S(1)} %copy-done, f32[16,256]{1,0:T(8,128)S(1)} %collective-permute-done.8.refs_0_, f32[16,256]{1,0:T(8,128)S(1)} %project_new_own.1.refs_1_), custom_call_target="tpu_custom_call" | custom-call | bytes 1048576 | tf_op jit(solution)/shard_map/dual_step/pallas_call | solution.py:422
  (22 shorter events, 0.0 us)
Async XLA Ops:
  0.6 0.7 %copy-start.3 = (f32[1,16,256]{2,1,0:T(8,128)S(1)}, f32[1,16,256]{2,1,0:T(8,128)}, u32[]{:S(2)}) copy-start(f32[1,16,256]{2,1,0:T(8,128)} %param.12) | copy-start | bytes 49156
  2.0 7.3 %collective-permute-start = (f32[1024,256]{1,0:T(8,128)}, f32[1024,256]{1,0:T(8,128)S(1)}, u32[]{:S(2)}, u32[]{:S(2)}) collective-permute-start(f32[1024,256]{1,0:T(8,128)} %bitcast.8), channel_id=1, source_target_pairs={{0,8},{8,0},{16,24},{24,16},{1,9},{9,1},{17,25},{25,17},{2,10},{10... | collective-permute-start | bytes 3145736 | tf_op jit(solution)/shard_map/ppermute | solution.py:456
  2.5 16.1 %all-to-all-start = ((f32[8,16,256]{2,1,0:T(8,128)}), f32[8,16,256]{2,1,0:T(8,128)S(1)}, u32[]{:S(2)}, u32[]{:S(2)}) async-start(f32[8,16,256]{2,1,0:T(8,128)} %phase_copies.1), calls=%async_computation | async-start | bytes 262144 | tf_op jit(solution)/shard_map/all_to_all | solution.py:476
  9.3 1.2 %copy-start.1 = (f32[64,16,256]{2,1,0:T(8,128)S(1)}, f32[64,16,256]{2,1,0:T(8,128)}, u32[]{:S(2)}) copy-start(f32[64,16,256]{2,1,0:T(8,128)} %param.11) | copy-start | bytes 3145732
  10.5 8.1 %copy-start.7 = (f32[1,4,128,128]{3,2,1,0:T(8,128)S(1)}, f32[1,4,128,128]{3,2,1,0:T(8,128)}, u32[]{:S(2)}) copy-start(f32[1,4,128,128]{3,2,1,0:T(8,128)} %param.16) | copy-start | bytes 786436
  10.5 8.1 %copy-start.8 = (f32[128,128]{1,0:T(8,128)S(1)}, f32[128,128]{1,0:T(8,128)}, u32[]{:S(2)}) copy-start(f32[128,128]{1,0:T(8,128)} %probe_r_ref.1) | copy-start | bytes 196612
  10.5 8.1 %copy-start.9 = (f32[128,128]{1,0:T(8,128)S(1)}, f32[128,128]{1,0:T(8,128)}, u32[]{:S(2)}) copy-start(f32[128,128]{1,0:T(8,128)} %probe_i_ref.1) | copy-start | bytes 196612
  10.5 8.1 %copy-start.12 = (bf16[2,2,128,128]{3,2,1,0:T(8,128)(2,1)S(1)}, bf16[2,2,128,128]{3,2,1,0:T(8,128)(2,1)}, u32[]{:S(2)}) copy-start(bf16[2,2,128,128]{3,2,1,0:T(8,128)(2,1)} %constant.6.clone.const_ref) | copy-start | bytes 393220
  10.8 7.8 %collective-permute-start.1 = (bf16[128,256]{1,0:T(8,128)(2,1)S(1)}, bf16[128,256]{1,0:T(8,128)(2,1)S(1)}, u32[]{:S(2)}, u32[]{:S(2)}) collective-permute-start(bf16[128,256]{1,0:T(8,128)(2,1)S(1)} %get-tuple-element.39), channel_id=1, source_target_pairs={{0,1},{1,2},{2,3},{3,4},{4,5},{5,6},{6,7},{8,9},{9,10},{10,11},{11... | collective-permute-start | bytes 196616 | tf_op jit(solution)/shard_map/ppermute | solution.py:490
  14.7 3.8 %collective-permute-start.2 = (s32[1]{0:T(128)}, s32[1]{0:T(128)}, u32[]{:S(2)}, u32[]{:S(2)}) collective-permute-start(s32[1]{0:T(128)} %param.18), channel_id=1, source_target_pairs={{16,0},{24,8},{0,16},{8,24},{17,1},{25,9},{1,17},{9,25},{18,2},{26... | collective-permute-start | bytes 20 | tf_op jit(solution)/shard_map/ppermute | solution.py:459
  17.0 6.2 %collective-permute-start.3 = (bf16[128,256]{1,0:T(8,128)(2,1)S(1)}, bf16[128,256]{1,0:T(8,128)(2,1)S(1)}, u32[]{:S(2)}, u32[]{:S(2)}) collective-permute-start(bf16[128,256]{1,0:T(8,128)(2,1)S(1)} %get-tuple-element.42), channel_id=1, source_target_pairs={{1,0},{2,1},{3,2},{4,3},{5,4},{6,5},{7,6},{9,8},{10,9},{11,10},{12... | collective-permute-start | bytes 196616 | tf_op jit(solution)/shard_map/ppermute | solution.py:491
  18.6 0.7 %copy-start.10 = (s32[1,4]{1,0:T(1,128)S(1)}, s32[1,4]{1,0:T(1,128)}, u32[]{:S(2)}) copy-start(s32[1,4]{1,0:T(1,128)} %param.17) | copy-start | bytes 52
  19.3 9.7 %copy-start.2 = (f32[64,16,256]{2,1,0:T(8,128)S(1)}, f32[64,16,256]{2,1,0:T(8,128)}, u32[]{:S(2)}) copy-start(f32[64,16,256]{2,1,0:T(8,128)} %param.11) | copy-start | bytes 3145732
  19.3 9.8 %copy-start.11 = (bf16[4,256,256]{2,1,0:T(8,128)(2,1)S(1)}, bf16[4,256,256]{2,1,0:T(8,128)(2,1)}, u32[]{:S(2)}) copy-start(bf16[4,256,256]{2,1,0:T(8,128)(2,1)} %constant.7.clone.refs_5_.refs_1_.refs_2_.refs_6_) | copy-start | bytes 1572868
  23.1 14.9 %all-to-all-start.1 = ((bf16[8,16,256]{2,1,0:T(8,128)(2,1)}), bf16[8,16,256]{2,1,0:T(8,128)(2,1)S(1)}, u32[]{:S(2)}, u32[]{:S(2)}) async-start(bf16[8,16,256]{2,1,0:T(8,128)(2,1)} %gradient.1), calls=%async_computation.1 | async-start | bytes 131072 | tf_op jit(solution)/shard_map/all_to_all | solution.py:505
  34.0 3.8 %copy-start.13 = (f32[16,64,256]{2,1,0:T(8,128)}, f32[16,64,256]{2,1,0:T(8,128)S(1)}, u32[]{:S(2)}) copy-start(f32[16,64,256]{2,1,0:T(8,128)S(1)} %get-tuple-element.51.refs_0_) | copy-start | bytes 3145732
  34.0 3.8 %copy-start.15 = (bf16[16,64,256]{2,1,0:T(8,128)(2,1)}, bf16[16,64,256]{2,1,0:T(8,128)(2,1)S(1)}, u32[]{:S(2)}) copy-start(bf16[16,64,256]{2,1,0:T(8,128)(2,1)S(1)} %get-tuple-element.52.refs_1_) | copy-start | bytes 1572868
  34.0 3.8 %collective-permute-start.4 = (f32[16,256]{1,0:T(8,128)S(1)}, f32[16,256]{1,0:T(8,128)S(1)}, u32[]{:S(2)}, u32[]{:S(2)}) collective-permute-start(f32[16,256]{1,0:T(8,128)S(1)} %get-tuple-element.46), channel_id=1, source_target_pairs={{0,16},{8,24},{16,0},{24,8},{1,17},{9,25},{17,1},{25,9},{2,18},{10... | collective-permute-start | bytes 49160 | tf_op jit(solution)/shard_map/ppermute | solution.py:462
  34.6 3.2 %copy-start = (bf16[2,2,256,256]{3,2,1,0:T(8,128)(2,1)S(1)}, bf16[2,2,256,256]{3,2,1,0:T(8,128)(2,1)}, u32[]{:S(2)}) copy-start(bf16[2,2,256,256]{3,2,1,0:T(8,128)(2,1)} %constant.8.clone.full_ref) | copy-start | bytes 1572868
  34.6 3.2 %copy-start.4 = (f32[1,16,256]{2,1,0:T(8,128)S(1)}, f32[1,16,256]{2,1,0:T(8,128)}, u32[]{:S(2)}) copy-start(f32[1,16,256]{2,1,0:T(8,128)} %param.12) | copy-start | bytes 49156
  34.6 3.2 %copy-start.5 = (f32[1,16,256]{2,1,0:T(8,128)S(1)}, f32[1,16,256]{2,1,0:T(8,128)}, u32[]{:S(2)}) copy-start(f32[1,16,256]{2,1,0:T(8,128)} %param.13) | copy-start | bytes 49156
  38.7 3.7 %collective-permute-start.5 = (f32[16,256]{1,0:T(8,128)S(1)}, f32[16,256]{1,0:T(8,128)S(1)}, u32[]{:S(2)}, u32[]{:S(2)}) collective-permute-start(f32[16,256]{1,0:T(8,128)S(1)} %get-tuple-element.56.refs_0_), channel_id=1, source_target_pairs={{16,0},{24,8},{0,16},{8,24},{17,1},{25,9},{1,17},{9,25},{18,2},{26... | collective-permute-start | bytes 49160 | tf_op jit(solution)/shard_map/ppermute | solution.py:459
  45.0 3.4 %copy-start.14 = (f32[16,64,256]{2,1,0:T(8,128)S(1)}, f32[16,64,256]{2,1,0:T(8,128)}, u32[]{:S(2)}) copy-start(f32[16,64,256]{2,1,0:T(8,128)} %copy-done.13) | copy-start | bytes 3145732
  45.0 3.4 %copy-start.16 = (bf16[16,64,256]{2,1,0:T(8,128)(2,1)S(1)}, bf16[16,64,256]{2,1,0:T(8,128)(2,1)}, u32[]{:S(2)}) copy-start(bf16[16,64,256]{2,1,0:T(8,128)(2,1)} %copy-done.15) | copy-start | bytes 1572868
  45.0 3.4 %collective-permute-start.7 = (bf16[8,128,256]{2,1,0:T(8,128)(2,1)S(1)}, bf16[8,128,256]{2,1,0:T(8,128)(2,1)S(1)}, u32[]{:S(2)}, u32[]{:S(2)}) collective-permute-start(bf16[8,128,256]{2,1,0:T(8,128)(2,1)S(1)} %backproject.3.refs_4_), channel_id=1, source_target_pairs={{0,8},{8,0},{16,24},{24,16},{1,9},{9,1},{17,25},{25,17},{2,10},{10... | collective-permute-start | bytes 1572872 | tf_op jit(solution)/shard_map/ppermute | solution.py:456
  47.8 3.7 %collective-permute-start.6 = (bf16[8,128,256]{2,1,0:T(8,128)(2,1)S(1)}, bf16[8,128,256]{2,1,0:T(8,128)(2,1)S(1)}, u32[]{:S(2)}, u32[]{:S(2)}) collective-permute-start(bf16[8,128,256]{2,1,0:T(8,128)(2,1)S(1)} %backproject.2.refs_4_), channel_id=1, source_target_pairs={{0,8},{8,0},{16,24},{24,16},{1,9},{9,1},{17,25},{25,17},{2,10},{10... | collective-permute-start | bytes 1572872 | tf_op jit(solution)/shard_map/ppermute | solution.py:456
  53.5 3.8 %collective-permute-start.8 = (f32[16,256]{1,0:T(8,128)S(1)}, f32[16,256]{1,0:T(8,128)S(1)}, u32[]{:S(2)}, u32[]{:S(2)}) collective-permute-start(f32[16,256]{1,0:T(8,128)S(1)} %get-tuple-element.68), channel_id=1, source_target_pairs={{0,16},{8,24},{16,0},{24,8},{1,17},{9,25},{17,1},{25,9},{2,18},{10... | collective-permute-start | bytes 49160 | tf_op jit(solution)/shard_map/ppermute | solution.py:462
  55.1 2.3 %copy-start.6 = (f32[16,256]{1,0:T(8,128)S(1)}, f32[16,256]{1,0:T(8,128)}, u32[]{:S(2)}) copy-start(f32[16,256]{1,0:T(8,128)} %get-tuple-element.50.phase_ref) | copy-start | bytes 49156

commit v8 on v7

--- a/solution.py
+++ b/solution.py
@@ -79,6 +79,24 @@
     )
 
 
+def cos_sin(x):
+    turns = jnp.floor(x * (2.0 / math.pi) + 0.5)
+    r = x - turns * 1.5703125 - turns * 4.837512969970703125e-4 - turns * 7.54978995489188216e-8
+    z = r * r
+    sine = r + r * z * (-1.6666654611e-1 + z * (8.3321608736e-3 - z * 1.9515295891e-4))
+    cosine = 1.0 - 0.5 * z + z * z * (
+        4.166664568298827e-2 + z * (-1.388731625493765e-3 + z * 2.443315711809948e-5)
+    )
+    quarter = turns.astype(jnp.int32)
+    odd = (quarter & 1) == 1
+    first = jnp.where(odd, sine, cosine)
+    second = jnp.where(odd, cosine, sine)
+    return (
+        jnp.where(((quarter + 1) & 2) == 2, -first, first),
+        jnp.where((quarter & 2) == 2, -second, second),
+    )
+
+
 def turn(re, im, c1, s, c2, sign):
     if sign > 0:
         return re * c1 + im * s, im * c2 - re * s
@@ -97,11 +115,11 @@
     freq = jnp.where(lane == 0, half, lane).astype(F32)
     phase = unit * coef_a * freq
     base = phase * sub.astype(F32)
-    base_c, base_s = jnp.cos(base), jnp.sin(base)
+    base_c, base_s = cos_sin(base)
     for block in range(length // 64):
         first = 8 * block * 8 - half
         step = phase * (first + 8 * sub).astype(F32)
-        step_c, step_s = jnp.cos(step), jnp.sin(step)
+        step_c, step_s = cos_sin(step)
         for q in range(8):
             sc, ss = step_c[q : q + 1], step_s[q : q + 1]
             c2 = base_c * sc - base_s * ss
@@ -116,10 +134,10 @@
         phase = unit * coef_b * place
         lanes = slice(side * half, side * half + half)
         base = phase * sub.astype(F32)
-        base_c, base_s = jnp.cos(base), jnp.sin(base)
+        base_c, base_s = cos_sin(base)
         for block in range(half // 64):
             step = phase * (block * 64 + 8 * sub).astype(F32)
-            step_c, step_s = jnp.cos(step), jnp.sin(step)
+            step_c, step_s = cos_sin(step)
             for q in range(8):
                 sc, ss = step_c[q : q + 1], step_s[q : q + 1]
                 rows = pl.ds((block * 8 + q) * 8, 8)
@@ -347,7 +365,7 @@
     positions, height, width = measured_ref.shape
     length = image_ref.shape[1]
     image = image_ref[...]
-    cos_image, sin_image = jnp.cos(image), jnp.sin(image)
+    cos_image, sin_image = cos_sin(image)
     probe_r, probe_i = probe_r_ref[...], probe_i_ref[...]
     waves = []
     for p in range(positions):

time: 58.7 us -> 58.2 us (level)
  Pallas kernels: 27.5 us -> 26.9 us
    pallas_call x14, Pallas kernels: 27.5 us -> 26.9 us  [call(): pl.pallas_call(kernel, grid=grid, out_shape=tuple(outs), in_specs=specs o...]
  transfers between devices with their start and end apart: 11 -> 11, of which waited for: 4 -> 4; matrix products, arithmetic and copies ran while one was open for 0% -> 0% of each run, Pallas kernels for 36% -> 35%
where the time goes in v8:
time: 58.2 us; the launch traced here: 57.7 us
  Pallas kernels  26.9 us (46%)
  starting transfers between devices  23.9 us (41%)
  waiting for transfers between devices  2.8 us (5%)
  local copies, waits for them, and re-layouts  2.61 us (4%)
  between operations  1.53 us (3%)
    pallas_call x14, Pallas kernels, call(): pl.pallas_call(kernel, grid=grid, out_shape=tuple(outs), in_specs=specs o...  26.9 us
    all_to_all x1, starting transfers between devices, shards(): lax.all_to_all(phases, 'tile', split_axis=0, concat_axis=0, tiled=True)  6.83 us
    all_to_all x1, starting transfers between devices, shards(): grad = lax.all_to_all(grad, 'tile', split_axis=0, concat_axis=0, tiled=True)  5.56 us
    ppermute x1, starting transfers between devices, shards(): lax.ppermute(edges[0], 'tile', [(i, i + 1) for i in range(tiles - 1)])  3.92 us
    ppermute x2, starting transfers between devices, from_peer(): lax.ppermute(value, 'ang', [((i + 2 * j) % ang, i) for i in range(ang)])  3.04 us
    unnamed x34, local copies, waits for them, and re-layouts  2.61 us
    ppermute x2, starting transfers between devices, to_peer(): lax.ppermute(value, 'ang', [(i, (i + 2 * j) % ang) for i in range(ang)])  2.15 us
    ppermute x2, waiting for transfers between devices, from_peer(): lax.ppermute(value, 'ang', [((i + 2 * j) % ang, i) for i in range(ang)])  1.48 us
  transfers between devices with their start and end apart: 11, of which 4 were waited for; matrix products, arithmetic and copies ran while one was open for 0% of the time, Pallas kernels for 35%

profile of v8, /device:TPU:0, one launch (start us, length us, event | category | flops | bytes accessed | tf_op | source)
XLA Modules:
  0.0 57.7 jit_solution(14733335830651694624)
XLA Ops:
  0.6 0.0 copy-start.3
  0.6 0.7 %copy-done.3 = f32[1,16,256]{2,1,0:T(8,128)S(1)} copy-done((f32[1,16,256]{2,1,0:T(8,128)S(1)}, f32[1,16,256]{2,1,0:T(8,128)}, u32[]{:S(2)}) %copy-start.3) | copy-done | bytes 16408
  1.4 0.7 %phase_copies.1 = f32[8,16,256]{2,1,0:T(8,128)} custom-call(f32[16,256]{1,0:T(8,128)S(1)} %bitcast.14), custom_call_target="tpu_custom_call" | custom-call | bytes 1048576 | tf_op jit(solution)/shard_map/phase_copies/pallas_call | solution.py:440
  2.0 0.5 collective-permute-start
  2.5 6.8 %all-to-all-start = ((f32[8,16,256]{2,1,0:T(8,128)}), f32[8,16,256]{2,1,0:T(8,128)S(1)}, u32[]{:S(2)}, u32[]{:S(2)}) async-start(f32[8,16,256]{2,1,0:T(8,128)} %phase_copies.1), calls=%async_computation | async-start | bytes 262144 | tf_op jit(solution)/shard_map/all_to_all | solution.py:494
  9.3 0.0 collective-permute-done.refs_2_.refs_3_.refs_4_
  9.3 0.0 copy-start.1
  9.3 1.2 %copy-done.1 = f32[64,16,256]{2,1,0:T(8,128)S(1)} copy-done((f32[64,16,256]{2,1,0:T(8,128)S(1)}, f32[64,16,256]{2,1,0:T(8,128)}, u32[]{:S(2)}) %copy-start.1) | copy-done | bytes 1048600
  10.5 0.3 edges.1
  10.8 3.9 %collective-permute-start.1 = (bf16[128,256]{1,0:T(8,128)(2,1)S(1)}, bf16[128,256]{1,0:T(8,128)(2,1)S(1)}, u32[]{:S(2)}, u32[]{:S(2)}) collective-permute-start(bf16[128,256]{1,0:T(8,128)(2,1)S(1)} %get-tuple-element.39), channel_id=1, source_target_pairs={{0,1},{1,2},{2,3},{3,4},{4,5},{5,6},{6,7},{8,9},{9,10},{10,11},{11... | collective-permute-start | bytes 196616 | tf_op jit(solution)/shard_map/ppermute | solution.py:508
  14.7 1.6 %collective-permute-start.2 = (s32[1]{0:T(128)}, s32[1]{0:T(128)}, u32[]{:S(2)}, u32[]{:S(2)}) collective-permute-start(s32[1]{0:T(128)} %param.18), channel_id=1, source_target_pairs={{16,0},{24,8},{0,16},{8,24},{17,1},{25,9},{1,17},{9,25},{18,2},{26... | collective-permute-start | bytes 20 | tf_op jit(solution)/shard_map/ppermute | solution.py:477
  17.0 1.3 %collective-permute-start.3 = (bf16[128,256]{1,0:T(8,128)(2,1)S(1)}, bf16[128,256]{1,0:T(8,128)(2,1)S(1)}, u32[]{:S(2)}, u32[]{:S(2)}) collective-permute-start(bf16[128,256]{1,0:T(8,128)(2,1)S(1)} %get-tuple-element.42), channel_id=1, source_target_pairs={{1,0},{2,1},{3,2},{4,3},{5,4},{6,5},{7,6},{9,8},{10,9},{11,10},{12... | collective-permute-start | bytes 196616 | tf_op jit(solution)/shard_map/ppermute | solution.py:509
  18.3 0.3 collective-permute-done.2.refs_0_.refs_1_
  18.6 0.0 all-to-all-done
  18.6 0.0 collective-permute-done.1.refs_2_
  18.6 0.0 copy-done.7
  18.6 0.0 copy-done.8
  18.6 0.0 copy-done.9
  18.6 0.6 %copy-done.10 = s32[1,4]{1,0:T(1,128)S(1)} copy-done((s32[1,4]{1,0:T(1,128)S(1)}, s32[1,4]{1,0:T(1,128)}, u32[]{:S(2)}) %copy-start.10) | copy-done | bytes 40
  19.3 3.1 %gradient.1 = bf16[8,16,256]{2,1,0:T(8,128)(2,1)} custom-call(s32[4]{0:T(128)S(1)} %bitcast.20, f32[128,256]{1,0:T(8,128)S(1)} %bitcast.13, f32[4,128,128]{2,1,0:T(8,128)S(1)} %bitcast.19, f32[128,128]{1,0:T(8,128)S(1)} %copy-done.8, f32[128,128]{1,0:T(8,128)S(1)} %copy-done.9, bf16[2,2,128,128]{3,2,1,0:T(8,128)(2,1)S(1)} %copy-done.12), custom_call_target="tpu_custom_call" | custom-call | flops 4294967296 | bytes 1048576 | tf_op jit(solution)/shard_map/gradient/pallas_call | solution.py:440
  22.4 0.8 %collective-permute-done.3.refs_3_ = bf16[128,256]{1,0:T(8,128)(2,1)S(1)} collective-permute-done((bf16[128,256]{1,0:T(8,128)(2,1)S(1)}, bf16[128,256]{1,0:T(8,128)(2,1)S(1)}, u32[]{:S(2)}, u32[]{:S(2)}) %collective-permute-start.3) | collective-permute-done | bytes 65568 | tf_op jit(solution)/shard_map/ppermute | solution.py:509
  23.1 5.6 %all-to-all-start.1 = ((bf16[8,16,256]{2,1,0:T(8,128)(2,1)}), bf16[8,16,256]{2,1,0:T(8,128)(2,1)S(1)}, u32[]{:S(2)}, u32[]{:S(2)}) async-start(bf16[8,16,256]{2,1,0:T(8,128)(2,1)} %gradient.1), calls=%async_computation.1 | async-start | bytes 131072 | tf_op jit(solution)/shard_map/all_to_all | solution.py:523
  28.7 0.0 copy-done.2
  28.7 4.9 %project_old.1 = (f32[16,256]{1,0:T(8,128)S(1)}, f32[16,64,256]{2,1,0:T(8,128)S(1)}, bf16[16,64,256]{2,1,0:T(8,128)(2,1)S(1)}, bf16[16,128,256]{2,1,0:T(8,128)(2,1)S(1)}) custom-call(s32[1]{0:T(128)} %collective-permute-done.2.refs_0_.refs_1_, f32[1024,256]{1,0:T(8,128)S(1)} %bitcast.11, f32[1024,256]{1,0:T(8,128)S(1)} %bitcast.12, ...), custom_call_target="tpu_custom_call" | custom-call | flops 3221225472 | bytes 1048576 | tf_op jit(solution)/shard_map/project_old/pallas_call | solution.py:440
  33.6 0.0 copy-start.13
  33.6 0.6 %collective-permute-start.4 = (f32[16,256]{1,0:T(8,128)S(1)}, f32[16,256]{1,0:T(8,128)S(1)}, u32[]{:S(2)}, u32[]{:S(2)}) collective-permute-start(f32[16,256]{1,0:T(8,128)S(1)} %get-tuple-element.46), channel_id=1, source_target_pairs={{0,16},{8,24},{16,0},{24,8},{1,17},{9,25},{17,1},{25,9},{2,18},{10... | collective-permute-start | bytes 49160 | tf_op jit(solution)/shard_map/ppermute | solution.py:480
  34.3 3.1 %project_old_own.1.refs_1_ = f32[16,256]{1,0:T(8,128)S(1)} custom-call(bf16[16,128,256]{2,1,0:T(8,128)(2,1)S(1)} %get-tuple-element.47.refs_0_, bf16[4,256,256]{2,1,0:T(8,128)(2,1)S(1)} %copy-done.11, s32[1]{0:T(128)S(6)} %copy.20.refs_2_.refs_0_), custom_call_target="tpu_custom_call" | custom-call | flops 3221225472 | bytes 1048576 | tf_op jit(solution)/shard_map/project_old_own/pallas_call | solution.py:440
  37.4 0.0 collective-permute-done.4.refs_0_
  37.5 0.2 line_step.1
  37.7 0.0 all-to-all-done.1.grad_ref
  37.7 0.6 %phase_step.1 = (f32[16,256]{1,0:T(8,128)}, f32[16,256]{1,0:T(8,128)S(1)}) custom-call(bf16[8,16,256]{2,1,0:T(8,128)(2,1)S(1)} %all-to-all-done.1.grad_ref, f32[16,256]{1,0:T(8,128)S(1)} %get-tuple-element.48.phase_part_ref, f32[16,256]{1,0:T(8,128)S(1)} %get-tuple-element.49.resid_part_ref, bf16[2,2,256,256]{3,2,1,0:T(8,128)(2,1)S(1)} %copy-done), custom_call_target="tpu_custom_call" | custom-call | bytes 1048576 | tf_op jit(solution)/shard_map/phase_step/pallas_call | solution.py:440
  38.3 1.5 %collective-permute-start.5 = (f32[16,256]{1,0:T(8,128)S(1)}, f32[16,256]{1,0:T(8,128)S(1)}, u32[]{:S(2)}, u32[]{:S(2)}) collective-permute-start(f32[16,256]{1,0:T(8,128)S(1)} %get-tuple-element.56.refs_0_), channel_id=1, source_target_pairs={{16,0},{24,8},{0,16},{8,24},{17,1},{25,9},{1,17},{9,25},{18,2},{26... | collective-permute-start | bytes 49160 | tf_op jit(solution)/shard_map/ppermute | solution.py:477
  39.8 1.1 %turn_tables.1 = (f32[3,256,128]{2,1,0:T(8,128)S(1)}, f32[2,128,256]{2,1,0:T(8,128)S(1)}, f32[8,256]{1,0:T(8,128)S(1)}, f32[3,256,128]{2,1,0:T(8,128)S(1)}, f32[...) custom-call(s32[1]{0:T(128)S(6)} %copy.20.refs_2_.refs_0_, s32[1]{0:T(128)} %collective-permute-done.2.refs_0_.refs_1_), custom_call_target="tpu_custom_call" | custom-call | flops 2147483648 | bytes 1048576 | tf_op jit(solution)/shard_map/turn_tables/pallas_call | solution.py:440
  40.9 1.2 %collective-permute-done.5.refs_1_ = f32[16,256]{1,0:T(8,128)S(1)} collective-permute-done((f32[16,256]{1,0:T(8,128)S(1)}, f32[16,256]{1,0:T(8,128)S(1)}, u32[]{:S(2)}, u32[]{:S(2)}) %collective-permute-start.5) | collective-permute-done | bytes 16416 | tf_op jit(solution)/shard_map/ppermute | solution.py:477
  42.1 2.5 %backproject.3.refs_4_ = bf16[8,128,256]{2,1,0:T(8,128)(2,1)S(1)} custom-call(f32[16,256]{1,0:T(8,128)S(1)} %get-tuple-element.56.refs_0_, f32[16,256]{1,0:T(8,128)S(1)} %collective-permute-done.5.refs_1_, bf16[4,256,256]{2,1,0:T(8,128)(2,1)S(1)} %copy-done.11, f32[3,256,128]{2,1,0:T(8,128)S(1)} %get-tuple-element.59.refs_3_.refs_10_.refs_2_, ...), custom_call_target="tpu_custom_call" | custom-call | flops 3221225472 | bytes 1048576 | tf_op jit(solution)/shard_map/backproject/pallas_call | solution.py:440
  44.6 0.0 copy-start.14
  44.6 0.1 collective-permute-start.7
  44.7 2.8 %backproject.2.refs_4_ = bf16[8,128,256]{2,1,0:T(8,128)(2,1)S(1)} custom-call(f32[16,256]{1,0:T(8,128)S(1)} %get-tuple-element.56.refs_0_, f32[16,256]{1,0:T(8,128)S(1)} %collective-permute-done.5.refs_1_, bf16[4,256,256]{2,1,0:T(8,128)(2,1)S(1)} %copy-done.11, f32[3,256,128]{2,1,0:T(8,128)S(1)} %get-tuple-element.59.refs_3_.refs_10_.refs_2_, ...), custom_call_target="tpu_custom_call" | custom-call | flops 3221225472 | bytes 1048576 | tf_op jit(solution)/shard_map/backproject/pallas_call | solution.py:440
  47.4 0.6 collective-permute-start.6
  48.0 0.0 collective-permute-done.7.refs_5_
  48.0 0.0 copy-done.16
  48.0 3.1 %project_new.2 = (f32[64,16,256]{2,1,0:T(8,128)}, f32[16,256]{1,0:T(8,128)S(1)}, f32[16,256]{1,0:T(8,128)S(1)}) custom-call(f32[16,64,256]{2,1,0:T(8,128)S(1)} %copy-done.14, bf16[16,64,256]{2,1,0:T(8,128)(2,1)S(1)} %copy-done.16, bf16[128,256]{1,0:T(8,128)(2,1)S(1)} %collective-permute-done.1.refs_2_, bf16[128,256]{1,0:T(8,128)(2,1)S(1)} %collective-permute-done.3.refs_3_, ...), custom_call_target="tpu_custom_call" | custom-call | flops 3221225472 | bytes 1048576 | tf_op jit(solution)/shard_map/project_new/pallas_call | solution.py:440
  51.1 0.0 collective-permute-done.6.refs_5_
  51.2 1.9 %project_new.3 = (f32[64,16,256]{2,1,0:T(8,128)}, f32[16,256]{1,0:T(8,128)S(1)}, bf16[8,128,256]{2,1,0:T(8,128)(2,1)S(1)}) custom-call(f32[16,64,256]{2,1,0:T(8,128)S(1)} %copy-done.14, bf16[16,64,256]{2,1,0:T(8,128)(2,1)S(1)} %copy-done.16, bf16[128,256]{1,0:T(8,128)(2,1)S(1)} %collective-permute-done.1.refs_2_, ...), custom_call_target="tpu_custom_call", output_to_operand_aliasing={{0}: (10, {}), {1}: (11, {})} | custom-call | flops 1610612736 | bytes 1048576 | tf_op jit(solution)/shard_map/project_new/pallas_call | solution.py:440
  53.1 1.6 %collective-permute-start.8 = (f32[16,256]{1,0:T(8,128)S(1)}, f32[16,256]{1,0:T(8,128)S(1)}, u32[]{:S(2)}, u32[]{:S(2)}) collective-permute-start(f32[16,256]{1,0:T(8,128)S(1)} %get-tuple-element.68), channel_id=1, source_target_pairs={{0,16},{8,24},{16,0},{24,8},{1,17},{9,25},{17,1},{25,9},{2,18},{10... | collective-permute-start | bytes 49160 | tf_op jit(solution)/shard_map/ppermute | solution.py:480
  54.7 1.8 %project_new_own.1.refs_1_ = f32[16,256]{1,0:T(8,128)S(1)} custom-call(bf16[8,128,256]{2,1,0:T(8,128)(2,1)S(1)} %get-tuple-element.69.refs_0_, bf16[4,256,256]{2,1,0:T(8,128)(2,1)S(1)} %copy-done.11, f32[3,256,128]{2,1,0:T(8,128)S(1)} %get-tuple-element.59.refs_3_.refs_10_.refs_2_, ...), custom_call_target="tpu_custom_call", output_to_operand_aliasing={{}: (5, {})} | custom-call | flops 1610612736 | bytes 1048576 | tf_op jit(solution)/shard_map/project_new_own/pallas_call | solution.py:440
  56.4 0.5 collective-permute-done.8.refs_0_
  56.9 0.8 %dual_step.1 = f32[16,256]{1,0:T(8,128)} custom-call(f32[16,256]{1,0:T(8,128)S(1)} %copy-done.6, f32[16,256]{1,0:T(8,128)S(1)} %bitcast.17, bf16[2,2,256,256]{3,2,1,0:T(8,128)(2,1)S(1)} %copy-done, f32[16,256]{1,0:T(8,128)S(1)} %collective-permute-done.8.refs_0_, f32[16,256]{1,0:T(8,128)S(1)} %project_new_own.1.refs_1_), custom_call_target="tpu_custom_call" | custom-call | bytes 1048576 | tf_op jit(solution)/shard_map/dual_step/pallas_call | solution.py:440
  (22 shorter events, 0.0 us)
Async XLA Ops:
  0.6 0.7 %copy-start.3 = (f32[1,16,256]{2,1,0:T(8,128)S(1)}, f32[1,16,256]{2,1,0:T(8,128)}, u32[]{:S(2)}) copy-start(f32[1,16,256]{2,1,0:T(8,128)} %param.12) | copy-start | bytes 49156
  2.0 7.3 %collective-permute-start = (f32[1024,256]{1,0:T(8,128)}, f32[1024,256]{1,0:T(8,128)S(1)}, u32[]{:S(2)}, u32[]{:S(2)}) collective-permute-start(f32[1024,256]{1,0:T(8,128)} %bitcast.8), channel_id=1, source_target_pairs={{0,8},{8,0},{16,24},{24,16},{1,9},{9,1},{17,25},{25,17},{2,10},{10... | collective-permute-start | bytes 3145736 | tf_op jit(solution)/shard_map/ppermute | solution.py:474
  2.5 16.1 %all-to-all-start = ((f32[8,16,256]{2,1,0:T(8,128)}), f32[8,16,256]{2,1,0:T(8,128)S(1)}, u32[]{:S(2)}, u32[]{:S(2)}) async-start(f32[8,16,256]{2,1,0:T(8,128)} %phase_copies.1), calls=%async_computation | async-start | bytes 262144 | tf_op jit(solution)/shard_map/all_to_all | solution.py:494
  9.3 1.2 %copy-start.1 = (f32[64,16,256]{2,1,0:T(8,128)S(1)}, f32[64,16,256]{2,1,0:T(8,128)}, u32[]{:S(2)}) copy-start(f32[64,16,256]{2,1,0:T(8,128)} %param.11) | copy-start | bytes 3145732
  10.5 8.1 %copy-start.7 = (f32[1,4,128,128]{3,2,1,0:T(8,128)S(1)}, f32[1,4,128,128]{3,2,1,0:T(8,128)}, u32[]{:S(2)}) copy-start(f32[1,4,128,128]{3,2,1,0:T(8,128)} %param.16) | copy-start | bytes 786436
  10.5 8.1 %copy-start.8 = (f32[128,128]{1,0:T(8,128)S(1)}, f32[128,128]{1,0:T(8,128)}, u32[]{:S(2)}) copy-start(f32[128,128]{1,0:T(8,128)} %probe_r_ref.1) | copy-start | bytes 196612
  10.5 8.1 %copy-start.9 = (f32[128,128]{1,0:T(8,128)S(1)}, f32[128,128]{1,0:T(8,128)}, u32[]{:S(2)}) copy-start(f32[128,128]{1,0:T(8,128)} %probe_i_ref.1) | copy-start | bytes 196612
  10.5 8.1 %copy-start.12 = (bf16[2,2,128,128]{3,2,1,0:T(8,128)(2,1)S(1)}, bf16[2,2,128,128]{3,2,1,0:T(8,128)(2,1)}, u32[]{:S(2)}) copy-start(bf16[2,2,128,128]{3,2,1,0:T(8,128)(2,1)} %constant.6.clone.const_ref) | copy-start | bytes 393220
  10.8 7.8 %collective-permute-start.1 = (bf16[128,256]{1,0:T(8,128)(2,1)S(1)}, bf16[128,256]{1,0:T(8,128)(2,1)S(1)}, u32[]{:S(2)}, u32[]{:S(2)}) collective-permute-start(bf16[128,256]{1,0:T(8,128)(2,1)S(1)} %get-tuple-element.39), channel_id=1, source_target_pairs={{0,1},{1,2},{2,3},{3,4},{4,5},{5,6},{6,7},{8,9},{9,10},{10,11},{11... | collective-permute-start | bytes 196616 | tf_op jit(solution)/shard_map/ppermute | solution.py:508
  14.7 3.8 %collective-permute-start.2 = (s32[1]{0:T(128)}, s32[1]{0:T(128)}, u32[]{:S(2)}, u32[]{:S(2)}) collective-permute-start(s32[1]{0:T(128)} %param.18), channel_id=1, source_target_pairs={{16,0},{24,8},{0,16},{8,24},{17,1},{25,9},{1,17},{9,25},{18,2},{26... | collective-permute-start | bytes 20 | tf_op jit(solution)/shard_map/ppermute | solution.py:477
  17.0 6.2 %collective-permute-start.3 = (bf16[128,256]{1,0:T(8,128)(2,1)S(1)}, bf16[128,256]{1,0:T(8,128)(2,1)S(1)}, u32[]{:S(2)}, u32[]{:S(2)}) collective-permute-start(bf16[128,256]{1,0:T(8,128)(2,1)S(1)} %get-tuple-element.42), channel_id=1, source_target_pairs={{1,0},{2,1},{3,2},{4,3},{5,4},{6,5},{7,6},{9,8},{10,9},{11,10},{12... | collective-permute-start | bytes 196616 | tf_op jit(solution)/shard_map/ppermute | solution.py:509
  18.6 0.7 %copy-start.10 = (s32[1,4]{1,0:T(1,128)S(1)}, s32[1,4]{1,0:T(1,128)}, u32[]{:S(2)}) copy-start(s32[1,4]{1,0:T(1,128)} %param.17) | copy-start | bytes 52
  19.3 9.5 %copy-start.2 = (f32[64,16,256]{2,1,0:T(8,128)S(1)}, f32[64,16,256]{2,1,0:T(8,128)}, u32[]{:S(2)}) copy-start(f32[64,16,256]{2,1,0:T(8,128)} %param.11) | copy-start | bytes 3145732
  19.3 9.5 %copy-start.11 = (bf16[4,256,256]{2,1,0:T(8,128)(2,1)S(1)}, bf16[4,256,256]{2,1,0:T(8,128)(2,1)}, u32[]{:S(2)}) copy-start(bf16[4,256,256]{2,1,0:T(8,128)(2,1)} %constant.7.clone.refs_5_.refs_1_.refs_2_.refs_6_) | copy-start | bytes 1572868
  23.1 14.5 %all-to-all-start.1 = ((bf16[8,16,256]{2,1,0:T(8,128)(2,1)}), bf16[8,16,256]{2,1,0:T(8,128)(2,1)S(1)}, u32[]{:S(2)}, u32[]{:S(2)}) async-start(bf16[8,16,256]{2,1,0:T(8,128)(2,1)} %gradient.1), calls=%async_computation.1 | async-start | bytes 131072 | tf_op jit(solution)/shard_map/all_to_all | solution.py:523
  33.6 3.8 %copy-start.13 = (f32[16,64,256]{2,1,0:T(8,128)}, f32[16,64,256]{2,1,0:T(8,128)S(1)}, u32[]{:S(2)}) copy-start(f32[16,64,256]{2,1,0:T(8,128)S(1)} %get-tuple-element.51.refs_0_) | copy-start | bytes 3145732
  33.6 3.8 %copy-start.15 = (bf16[16,64,256]{2,1,0:T(8,128)(2,1)}, bf16[16,64,256]{2,1,0:T(8,128)(2,1)S(1)}, u32[]{:S(2)}) copy-start(bf16[16,64,256]{2,1,0:T(8,128)(2,1)S(1)} %get-tuple-element.52.refs_1_) | copy-start | bytes 1572868
  33.6 3.8 %collective-permute-start.4 = (f32[16,256]{1,0:T(8,128)S(1)}, f32[16,256]{1,0:T(8,128)S(1)}, u32[]{:S(2)}, u32[]{:S(2)}) collective-permute-start(f32[16,256]{1,0:T(8,128)S(1)} %get-tuple-element.46), channel_id=1, source_target_pairs={{0,16},{8,24},{16,0},{24,8},{1,17},{9,25},{17,1},{25,9},{2,18},{10... | collective-permute-start | bytes 49160 | tf_op jit(solution)/shard_map/ppermute | solution.py:480
  34.2 3.2 %copy-start = (bf16[2,2,256,256]{3,2,1,0:T(8,128)(2,1)S(1)}, bf16[2,2,256,256]{3,2,1,0:T(8,128)(2,1)}, u32[]{:S(2)}) copy-start(bf16[2,2,256,256]{3,2,1,0:T(8,128)(2,1)} %constant.8.clone.full_ref) | copy-start | bytes 1572868
  34.2 3.2 %copy-start.4 = (f32[1,16,256]{2,1,0:T(8,128)S(1)}, f32[1,16,256]{2,1,0:T(8,128)}, u32[]{:S(2)}) copy-start(f32[1,16,256]{2,1,0:T(8,128)} %param.12) | copy-start | bytes 49156
  34.3 3.2 %copy-start.5 = (f32[1,16,256]{2,1,0:T(8,128)S(1)}, f32[1,16,256]{2,1,0:T(8,128)}, u32[]{:S(2)}) copy-start(f32[1,16,256]{2,1,0:T(8,128)} %param.13) | copy-start | bytes 49156
  38.3 3.7 %collective-permute-start.5 = (f32[16,256]{1,0:T(8,128)S(1)}, f32[16,256]{1,0:T(8,128)S(1)}, u32[]{:S(2)}, u32[]{:S(2)}) collective-permute-start(f32[16,256]{1,0:T(8,128)S(1)} %get-tuple-element.56.refs_0_), channel_id=1, source_target_pairs={{16,0},{24,8},{0,16},{8,24},{17,1},{25,9},{1,17},{9,25},{18,2},{26... | collective-permute-start | bytes 49160 | tf_op jit(solution)/shard_map/ppermute | solution.py:477
  44.6 3.4 %copy-start.14 = (f32[16,64,256]{2,1,0:T(8,128)S(1)}, f32[16,64,256]{2,1,0:T(8,128)}, u32[]{:S(2)}) copy-start(f32[16,64,256]{2,1,0:T(8,128)} %copy-done.13) | copy-start | bytes 3145732
  44.6 3.4 %copy-start.16 = (bf16[16,64,256]{2,1,0:T(8,128)(2,1)S(1)}, bf16[16,64,256]{2,1,0:T(8,128)(2,1)}, u32[]{:S(2)}) copy-start(bf16[16,64,256]{2,1,0:T(8,128)(2,1)} %copy-done.15) | copy-start | bytes 1572868
  44.6 3.4 %collective-permute-start.7 = (bf16[8,128,256]{2,1,0:T(8,128)(2,1)S(1)}, bf16[8,128,256]{2,1,0:T(8,128)(2,1)S(1)}, u32[]{:S(2)}, u32[]{:S(2)}) collective-permute-start(bf16[8,128,256]{2,1,0:T(8,128)(2,1)S(1)} %backproject.3.refs_4_), channel_id=1, source_target_pairs={{0,8},{8,0},{16,24},{24,16},{1,9},{9,1},{17,25},{25,17},{2,10},{10... | collective-permute-start | bytes 1572872 | tf_op jit(solution)/shard_map/ppermute | solution.py:474
  47.4 3.7 %collective-permute-start.6 = (bf16[8,128,256]{2,1,0:T(8,128)(2,1)S(1)}, bf16[8,128,256]{2,1,0:T(8,128)(2,1)S(1)}, u32[]{:S(2)}, u32[]{:S(2)}) collective-permute-start(bf16[8,128,256]{2,1,0:T(8,128)(2,1)S(1)} %backproject.2.refs_4_), channel_id=1, source_target_pairs={{0,8},{8,0},{16,24},{24,16},{1,9},{9,1},{17,25},{25,17},{2,10},{10... | collective-permute-start | bytes 1572872 | tf_op jit(solution)/shard_map/ppermute | solution.py:474
  53.1 3.8 %collective-permute-start.8 = (f32[16,256]{1,0:T(8,128)S(1)}, f32[16,256]{1,0:T(8,128)S(1)}, u32[]{:S(2)}, u32[]{:S(2)}) collective-permute-start(f32[16,256]{1,0:T(8,128)S(1)} %get-tuple-element.68), channel_id=1, source_target_pairs={{0,16},{8,24},{16,0},{24,8},{1,17},{9,25},{17,1},{25,9},{2,18},{10... | collective-permute-start | bytes 49160 | tf_op jit(solution)/shard_map/ppermute | solution.py:480
  54.7 2.3 %copy-start.6 = (f32[16,256]{1,0:T(8,128)S(1)}, f32[16,256]{1,0:T(8,128)}, u32[]{:S(2)}) copy-start(f32[16,256]{1,0:T(8,128)} %get-tuple-element.50.phase_ref) | copy-start | bytes 49156
